TPU v7x, 256 devices: a whole 4x4x8 slice. The times are simulated.
256 devices in a mesh: pair: 4 (over x), vir: 64 (over y, z, core).
Axes of the slice: x: 4, y: 4, z: 8, core: 2. Of those that a mesh axis runs over, the one named last changes fastest.
Arguments:
- amplitudes: bfloat16 [768, 768, 768], P(('pair', 'vir')), may hold values from -6 to 6
- integral_tiles: bfloat16 [12288, 128, 128], P(('pair', 'vir')), may hold values from -0.21875 to 0.21875
- need_owner: int32 [27648, 1], P(('pair', 'vir')), may hold values from 0 to 255, as said below
- need_slot: int32 [27648, 1], P(('pair', 'vir')), may hold values from 0 to 47
- pair_occ: int32 [768, 2], P(('pair', 'vir')), may hold values from 0 to 399
- domain: int32 [768, 6], P(('pair', 'vir')), may hold values from 0 to 24, as said below
- eps_occ: float32 [400], replicated, may hold values from -2 to -0.3
- eps_vir: float32 [3200], replicated, may hold values from 0.2 to 6
Outputs:
- residual: float32 [768, 768, 768], P(('pair', 'vir'))
Inputs may be any that keep to these rules, and one draw needn't show every extreme that they name: `need_owner`: write a holder as h = q * 64 + v with v its vir index; among the requests of one device's pairs no v is named more than 3 times, and on every device some v is named exactly 3 times. `domain`: each row names 6 different tiles.
All inputs are finite; a program needn't handle non-finite values.
Results may differ from a plain program's by a relative error of at most 0.0031.
Values may be sent and summed in bfloat16 or wider, within the bound.
No kernel may reach another device: no remote copies, remote signals or barrier semaphores. Data moves between devices by JAX's collectives and lax.ppermute only.
A program may use at most 192 MiB of HBM per device.

v0:
```python
import jax
import jax.numpy as jnp
from jax import lax
from jax.sharding import PartitionSpec as P


def bucket_place(targets, count):
    matches = (targets[:, None] == jnp.arange(count, dtype=jnp.int32)[None, :]).astype(jnp.int32)
    return jnp.sum(jnp.cumsum(matches, axis=0) * matches, axis=1) - 1


def body(amplitudes, integral_tiles, need_owner, need_slot, pair_occ, domain, eps_occ, eps_vir):
    pairs_here = amplitudes.shape[0]
    width = amplitudes.shape[1]
    tile_size = integral_tiles.shape[1]
    held_count = integral_tiles.shape[0]
    dom_count = domain.shape[1]
    vir_count = lax.axis_size("vir")
    tile_owner = need_owner[:, 0]
    tile_slot = need_slot[:, 0]
    ask_count = tile_owner.shape[0]
    capacity = max(2, (3 * ask_count + 2 * vir_count - 1) // (2 * vir_count))
    copies = lax.all_gather(integral_tiles, "pair", axis=0, tiled=True)
    owner_column = tile_owner % vir_count
    owner_row = tile_owner // vir_count
    position = owner_column * capacity + bucket_place(owner_column, vir_count)
    requests = (
        jnp.full((vir_count * capacity,), -1, jnp.int32)
        .at[position]
        .set(owner_row * held_count + tile_slot)
    )
    requests = requests.reshape(vir_count, capacity)
    received = lax.all_to_all(requests, "vir", split_axis=0, concat_axis=0, tiled=True)
    served = copies[jnp.maximum(received, 0)]
    returned = lax.all_to_all(served, "vir", split_axis=0, concat_axis=0, tiled=True)
    fetched = returned.reshape(vir_count * capacity, tile_size, tile_size)[position]
    blocks = fetched.reshape(pairs_here, dom_count, dom_count, tile_size, tile_size)
    blocks = blocks.transpose(0, 1, 3, 2, 4).reshape(pairs_here, width, width)
    swapped = jnp.transpose(amplitudes, (0, 2, 1))
    mixed = (2.0 * amplitudes.astype(jnp.float32) - swapped.astype(jnp.float32)).astype(
        jnp.bfloat16
    )
    cycle_term = jnp.einsum("pac,pcb->pab", mixed, blocks, preferred_element_type=jnp.float32)
    cycle_term = cycle_term + jnp.einsum(
        "pca,pcb->pab", blocks, mixed, preferred_element_type=jnp.float32
    )
    vir_energy = eps_vir.reshape(-1, tile_size)[domain].reshape(pairs_here, width)
    occ_total = eps_occ[pair_occ[:, 0]] + eps_occ[pair_occ[:, 1]]
    denominator = occ_total[:, None, None] - vir_energy[:, :, None] - vir_energy[:, None, :]
    return cycle_term / denominator


def solution(mesh):
    return jax.shard_map(
        body,
        mesh=mesh,
        in_specs=(
            P(("pair", "vir"), None, None),
            P(("pair", "vir"), None, None),
            P(("pair", "vir"), None),
            P(("pair", "vir"), None),
            P(("pair", "vir"), None),
            P(("pair", "vir"), None),
            P(),
            P(),
        ),
        out_specs=P(("pair", "vir"), None, None),
        check_vma=False,
    )
```

profile of v0, /device:TPU:1, one launch (start us, length us, event | category | flops | bytes accessed | tf_op | source)
XLA Modules:
  0.0 291.9 jit_solution(16759725127325079642)
XLA Ops:
  6.5 0.7 all-gather.2.cloned.1.call-update
  7.3 0.7 fusion.13
  8.0 0.2 reduce_window_sum.11
  8.2 0.2 select_reduce_fusion
  8.3 0.7 bitcast_add_fusion
  9.0 0.7 fusion.3
  9.7 0.9 scatter_custom_fusion
  10.8 22.2 %all_to_all.14 = s32[64,1,3]{2,1,0:T(1,128)S(1)} all-to-all(s32[64,1,3]{2,1,0:T(1,128)S(1)} %bitcast.45), channel_id=1, replica_groups=mesh['pair'=4,'vir'=64] {'vir'}, dimensions={0} | all-to-all | bytes 1536 | tf_op jit(solution)/shard_map/all_to_all | solution.py:33
  33.1 0.1 reshape.72
  33.3 47.9 %all-gather.2.cloned.1.call-done = bf16[192,128,128]{2,1,0:T(8,128)(2,1)} async-done(((bf16[48,128,128]{2,1,0:T(8,128)(2,1)}), bf16[192,128,128]{2,1,0:T(8,128)(2,1)}) %all-gather.2.cloned.1.call-update) | async-done | bytes 6291472 | tf_op jit(solution)/shard_map/all_gather | solution.py:23
  81.2 10.8 %gather_fusion = bf16[192,128,128]{2,1,0:T(8,128)(2,1)} fusion(bf16[192,128,128]{2,1,0:T(8,128)(2,1)} %all-gather.2.cloned.1.call-done, s32[1024]{0:T(1024)S(1)} %pad_clamp_fusion.4), kind=kCustom, calls=%fused_computation | custom fusion | bytes 12583680 | tf_op jit(solution)/shard_map/gather | solution.py:34
  92.0 11.0 %all-to-all-start.1 = ((bf16[64,3,128,128]{3,2,1,0:T(8,128)(2,1)}), bf16[64,3,128,128]{3,2,1,0:T(8,128)(2,1)}, u32[]{:S(2)}, u32[]{:S(2)}) async-start(bf16[64,3,128,128]{3,2,1,0:T(8,128)(2,1)} %bitcast.43), calls=%async_computation.1 | async-start | bytes 12582912 | tf_op jit(solution)/shard_map/all_to_all | solution.py:35
  103.2 0.6 gather_fusion.3
  103.8 0.6 gather_fusion.2
  104.5 0.6 gather_fusion.4
  105.1 6.4 %copy.18 = f32[3,768,768]{1,2,0:T(8,128)} copy(bf16[3,768,768]{2,1,0:T(8,128)(2,1)} %param.8) | data formatting | bytes 10616832 | tf_op jit(solution)/shard_map/convert_element_type | solution.py:40
  111.5 0.6 pad_clamp_fusion.3
  112.1 0.7 broadcast_subtract_fusion
  112.8 131.1 %all-to-all-done.1 = bf16[64,3,128,128]{3,2,1,0:T(8,128)(2,1)} async-done(((bf16[64,3,128,128]{3,2,1,0:T(8,128)(2,1)}), bf16[64,3,128,128]{3,2,1,0:T(8,128)(2,1)}, u32[]{:S(2)}, u32[]{:S(2)}) %all-to-all-start.1) | async-done | bytes 6291488 | tf_op jit(solution)/shard_map/all_to_all | solution.py:35
  243.9 4.1 %gather_fusion.1 = bf16[108,128,128]{2,1,0:T(8,128)(2,1)S(1)} fusion(bf16[192,128,128]{2,1,0:T(8,128)(2,1)} %bitcast.8, s32[1024]{0:T(1024)} %pad_clamp_fusion.3), kind=kCustom, calls=%fused_computation.1 | custom fusion | bytes 7078320 | tf_op jit(solution)/shard_map/gather | solution.py:36
  248.0 5.2 %copy.20 = bf16[3,6,128,6,128]{4,3,2,1,0:T(8,128)(2,1)} copy(bf16[3,6,128,6,128]{4,2,3,1,0:T(8,128)(2,1)S(1)} %bitcast.44) | data formatting | bytes 7077888 | tf_op jit(solution)/shard_map/transpose | solution.py:38
  253.2 8.4 %reshape.68 = bf16[3,768,768]{2,1,0:T(8,128)(2,1)} reshape(bf16[3,6,128,6,128]{4,3,2,1,0:T(8,128)(2,1)} %copy.20) | data formatting | bytes 7077888 | tf_op jit(solution)/shard_map/reshape | solution.py:38
  261.7 11.2 %fusion.9 = f32[3,768,768]{2,1,0:T(8,128)} fusion(bf16[3,768,768]{2,1,0:T(8,128)(2,1)} %reshape.68, f32[3,768,768]{1,2,0:T(8,128)} %copy.18, bf16[3,768,768]{2,1,0:T(8,128)(2,1)} %param.8), kind=kOutput, calls=%fused_computation.39 | convolution fusion | flops 2724986880 | bytes 21233664 | tf_op jit(solution)/shard_map/pac,pcb->pab/dot_general | solution.py:43
  272.9 12.1 %subtract_divide_fusion = f32[3,768,768]{2,1,0:T(8,128)} fusion(f32[3,768,768]{2,1,0:T(8,128)} %fusion.9, f32[3,768]{1,0:T(4,128)S(1)} %copy-done.3, f32[3,768]{1,0:T(4,128)S(1)} %copy-done.4, bf16[3,768,768]{2,1,0:T(8,128)(2,1)} %reshape.68, f32[3,768,768]{1,2,0:T(8,128)S(1)} %bitcast.42, bf16[3,768,768]{2,1,0:T(8,128)(2,1)} %param.8), kind=kOutput, calls=%fused_computation.8 | convolution fusion | flops 2730295296 | bytes 28329984 | tf_op jit(solution)/shard_map/pca,pcb->pab/dot_general | solution.py:44
  (31 shorter events, 0.5 us)
Async XLA Ops:
  6.5 97.9 %copy-start = (f32[3200]{0:T(1024)S(1)}, f32[3200]{0:T(1024)}, u32[]{:S(2)}) copy-start(f32[3200]{0:T(1024)} %param.15) | copy-start | bytes 38404
  6.5 74.7 %all-gather.2.cloned.1.call-start = ((), (), s32[]{:S(2)}) async-start(), calls=%async_computation.2 | async-start | bytes 7864320 | tf_op jit(solution)/shard_map/all_gather | solution.py:23
  92.0 11.0 %copy-start.5 = (s32[3,6]{1,0:T(4,128)S(1)}, s32[3,6]{1,0:T(4,128)}, u32[]{:S(2)}) copy-start(s32[3,6]{1,0:T(4,128)} %param.13) | copy-start | bytes 220
  92.0 11.1 %copy-start.6 = (s32[3,2]{0,1:T(2,128)S(1)}, s32[3,2]{0,1:T(2,128)}, u32[]{:S(2)}) copy-start(s32[3,2]{0,1:T(2,128)} %param.12) | copy-start | bytes 76
  92.0 11.2 %copy-start.1 = (f32[400]{0:T(512)S(1)}, f32[400]{0:T(512)}, u32[]{:S(2)}) copy-start(f32[400]{0:T(512)} %param.14) | copy-start | bytes 4804
  92.0 151.9 %all-to-all-start.1 = ((bf16[64,3,128,128]{3,2,1,0:T(8,128)(2,1)}), bf16[64,3,128,128]{3,2,1,0:T(8,128)(2,1)}, u32[]{:S(2)}, u32[]{:S(2)}) async-start(bf16[64,3,128,128]{3,2,1,0:T(8,128)(2,1)} %bitcast.43), calls=%async_computation.1 | async-start | bytes 12582912 | tf_op jit(solution)/shard_map/all_to_all | solution.py:35
  105.0 138.8 %copy-start.2 = (f32[3,768]{1,0:T(4,128)}, f32[3,768]{1,0:T(4,128)S(1)}, u32[]{:S(2)}) copy-start(f32[3,768]{1,0:T(4,128)S(1)} %broadcast_in_dim_reshape.4) | copy-start | bytes 27652
  253.2 19.6 %slice-start = ((s8[7077888]{0:T(1024)(128)(4,1)}), s8[2883584]{0:T(1024)(128)(4,1)S(1)}, s32[]{:S(2)}) async-start(s8[7077888]{0:T(1024)(128)(4,1)} %bitcast.41), calls=%async_computation.3 | async-start | bytes 5767168
  261.7 11.2 %slice-start.1 = ((s8[7077888]{0:T(1024)(128)(4,1)}), s8[4194304]{0:T(1024)(128)(4,1)S(1)}, s32[]{:S(2)}) async-start(s8[7077888]{0:T(1024)(128)(4,1)} %bitcast.41), calls=%async_computation.4 | async-start | bytes 8388608
  261.7 11.2 %copy-start.3 = (f32[3,768]{1,0:T(4,128)S(1)}, f32[3,768]{1,0:T(4,128)}, u32[]{:S(2)}) copy-start(f32[3,768]{1,0:T(4,128)} %copy-done.2) | copy-start | bytes 27652
  261.7 11.2 %copy-start.4 = (f32[3,768]{1,0:T(4,128)S(1)}, f32[3,768]{1,0:T(4,128)}, u32[]{:S(2)}) copy-start(f32[3,768]{1,0:T(4,128)} %broadcast_subtract_fusion) | copy-start | bytes 27652
Sparse Core Ops, SparseCore 0:
  9.2 71.9 all-gather.1
where the time goes:
time: 292 us
  waiting for transfers between devices  180 us (62%)
  local copies, waits for them, and re-layouts  38.2 us (13%)
  matrix products  23.3 us (8%)
  blocking collectives  22.2 us (8%)
  between operations  13.5 us (5%)
  starting transfers between devices  11 us (4%)
  other arithmetic  3.82 us (1%)
    all_to_all x1, waiting for transfers between devices, body(): lax.all_to_all(served, 'vir', split_axis=0, concat_axis=0, tiled=True)  131 us
    all_gather x1, waiting for transfers between devices, body(): copies = lax.all_gather(integral_tiles, 'pair', axis=0, tiled=True)  47.9 us
    all_to_all x1, blocking collectives, body(): lax.all_to_all(requests, 'vir', split_axis=0, concat_axis=0, tiled=True)  22.2 us
    dot_general x1, matrix products, body(): jnp.einsum('pca,pcb->pab', blocks, mixed, preferred_element_type=jnp.floa...  12.1 us
    dot_general x1, matrix products, body(): jnp.einsum('pac,pcb->pab', mixed, blocks, preferred_element_type=jnp.floa...  11.2 us
    all_to_all x1, starting transfers between devices, body(): lax.all_to_all(served, 'vir', split_axis=0, concat_axis=0, tiled=True)  11 us
    gather x1, local copies, waits for them, and re-layouts, body(): served = copies[jnp.maximum(received, 0)]  10.8 us
    reshape x1, local copies, waits for them, and re-layouts, body(): blocks = blocks.transpose(0, 1, 3, 2, 4).reshape(pairs_here, width, width)  8.44 us
  transfers between devices with their start and end apart: 2, of which 2 were waited for; matrix products, arithmetic and copies ran while one was open for 5% of the time, Pallas kernels for 0%

commit v1 on v0

v1 whole, which is shorter than its diff:
```python
import functools

import jax
import jax.numpy as jnp
from jax import lax
from jax.experimental import pallas as pl
from jax.experimental.pallas import tpu as pltpu
from jax.sharding import PartitionSpec as P

ROWS_FIRST = 32
PER_COLUMN = 3
ANY = pl.BlockSpec(memory_space=pl.ANY)
SMEM = pl.BlockSpec(memory_space=pltpu.SMEM)
BIG = 100 * 2**20 // 2


def split_kernel(row_from, tiles_ref, after_ref, low_ref, high_ref, sem):
    half, rows = low_ref.shape[0], low_ref.shape[1]
    first = pltpu.make_async_copy(
        tiles_ref.at[pl.ds(0, half), pl.ds(row_from, rows)], low_ref, sem.at[0]
    )
    second = pltpu.make_async_copy(
        tiles_ref.at[pl.ds(half, half), pl.ds(row_from, rows)], high_ref, sem.at[1]
    )
    first.start()
    second.start()
    first.wait()
    second.wait()


def split(tiles, after, row_from, rows):
    half = tiles.shape[0] // 2
    shape = jax.ShapeDtypeStruct((half, rows, tiles.shape[2]), tiles.dtype)
    return pl.pallas_call(
        functools.partial(split_kernel, row_from),
        out_shape=(shape, shape),
        in_specs=[ANY, ANY],
        out_specs=(ANY, ANY),
        scratch_shapes=[pltpu.SemaphoreType.DMA((2,))],
        cost_estimate=pl.CostEstimate(
            flops=0, bytes_accessed=4 * half * rows * 128 * 2, transcendentals=0
        ),
        name="split_rows",
    )(tiles, after)


def serve_kernel(row_from, code_ref, tiles_ref, *refs):
    sources, out_ref, sem = refs[:6], refs[6], refs[7]
    half = tiles_ref.shape[0] // 2
    rows = out_ref.shape[1]

    def step(slot, carry):
        code = code_ref[slot]
        place = code & 31

        def own():
            pltpu.make_async_copy(
                tiles_ref.at[place + half * ((code >> 5) & 1), pl.ds(row_from, rows)],
                out_ref.at[slot],
                sem,
            ).start()

        def other(source):
            pltpu.make_async_copy(source.at[place], out_ref.at[slot], sem).start()

        lax.switch(
            code >> 5,
            [own, own] + [functools.partial(other, source) for source in sources],
        )
        return carry

    lax.fori_loop(0, out_ref.shape[0], step, 0)
    pltpu.make_async_copy(out_ref, out_ref, sem).wait()


def serve(codes, tiles, sources, row_from, rows):
    slots = codes.shape[0]
    return pl.pallas_call(
        functools.partial(serve_kernel, row_from),
        out_shape=jax.ShapeDtypeStruct((slots, rows, tiles.shape[2]), tiles.dtype),
        in_specs=[SMEM] + [ANY] * 7,
        out_specs=ANY,
        scratch_shapes=[pltpu.SemaphoreType.DMA],
        cost_estimate=pl.CostEstimate(
            flops=0, bytes_accessed=2 * slots * rows * 128 * 2, transcendentals=0
        ),
        name="serve_tiles",
    )(codes, tiles, *sources)


def gather_pairs(low, high):
    n = lax.axis_size("pair")
    up = [(i, (i + 1) % n) for i in range(n)]
    down = [(i, (i + n - 1) % n) for i in range(n)]
    up_low = lax.ppermute(low, "pair", up)
    down_high = lax.ppermute(high, "pair", down)
    up_high = lax.ppermute(high, "pair", up)
    down_low = lax.ppermute(low, "pair", down)
    far_low = lax.ppermute(up_low, "pair", up)
    far_high = lax.ppermute(down_high, "pair", down)
    return down_low, down_high, far_low, far_high, up_low, up_high


def mix_kernel(amp_ref, after_ref, mixed_ref):
    amp = amp_ref[0]
    mixed_ref[0] = (
        2.0 * amp.astype(jnp.float32) - jnp.transpose(amp).astype(jnp.float32)
    ).astype(mixed_ref.dtype)


def mix(amplitudes, after):
    pairs, width, _ = amplitudes.shape
    spec = pl.BlockSpec((1, width, width), lambda p: (p, 0, 0))
    return pl.pallas_call(
        mix_kernel,
        grid=(pairs,),
        out_shape=jax.ShapeDtypeStruct(amplitudes.shape, amplitudes.dtype),
        in_specs=[spec, ANY],
        out_specs=spec,
        cost_estimate=pl.CostEstimate(
            flops=pairs * width * width, bytes_accessed=4 * pairs * width * width, transcendentals=0
        ),
        compiler_params=pltpu.CompilerParams(vmem_limit_bytes=BIG),
        name="mix_amplitudes",
    )(amplitudes, after)


def residual_kernel(
    rows_first, tile, place_ref, occ_ref, domain_ref, eps_occ_ref, eps_vir_ref,
    mixed_ref, first_ref, second_ref, out_ref, block, sem,
):
    pair = pl.program_id(0)
    pairs = pl.num_programs(0)
    width = out_ref.shape[2]
    count = width // tile

    def fetch(which):
        slot = which % 2

        def step(k, carry):
            row = pl.multiple_of((k // count) * tile, tile)
            column = pl.ds(pl.multiple_of((k % count) * tile, tile), tile)
            place = place_ref[which * count * count + k]
            pltpu.make_async_copy(
                first_ref.at[place], block.at[slot, pl.ds(row, rows_first), column], sem.at[slot]
            ).start()
            pltpu.make_async_copy(
                second_ref.at[place],
                block.at[slot, pl.ds(row + rows_first, tile - rows_first), column],
                sem.at[slot],
            ).start()
            return carry

        lax.fori_loop(0, count * count, step, 0)

    @pl.when(pair == 0)
    def _():
        fetch(0)

    @pl.when(pair + 1 < pairs)
    def _():
        fetch(pair + 1)

    now = pair % 2
    pltpu.make_async_copy(block.at[now], block.at[now], sem.at[now]).wait()

    occ = eps_occ_ref[occ_ref[2 * pair]] + eps_occ_ref[occ_ref[2 * pair + 1]]
    energies = [
        eps_vir_ref[pl.ds(domain_ref[count * pair + c], 1), :] for c in range(count)
    ]
    across = jnp.concatenate(energies, axis=1)
    for c in range(0, count, 2):
        part = pl.ds(c * tile, 2 * tile)
        down = jnp.transpose(
            jnp.broadcast_to(jnp.concatenate(energies[c : c + 2], axis=1), (8, 2 * tile))
        )[:, :1]
        total = jnp.dot(
            mixed_ref[0, part, :], block[now], preferred_element_type=jnp.float32
        )
        total = total + lax.dot_general(
            block[now, :, part],
            mixed_ref[0],
            (((0,), (0,)), ((), ())),
            preferred_element_type=jnp.float32,
        )
        out_ref[0, part, :] = total / (occ - down - across)


def residual(places, pair_occ, domain, eps_occ, eps_vir, mixed, first, second):
    pairs, width, _ = mixed.shape
    rows_first, tile = first.shape[1], first.shape[2]
    return pl.pallas_call(
        functools.partial(residual_kernel, rows_first, tile),
        grid=(pairs,),
        out_shape=jax.ShapeDtypeStruct(mixed.shape, jnp.float32),
        in_specs=[
            SMEM,
            SMEM,
            SMEM,
            SMEM,
            pl.BlockSpec(memory_space=pltpu.VMEM),
            pl.BlockSpec((1, width, width), lambda p: (p, 0, 0)),
            ANY,
            ANY,
        ],
        out_specs=pl.BlockSpec((1, width, width), lambda p: (p, 0, 0)),
        scratch_shapes=[
            pltpu.VMEM((2, width, width), mixed.dtype),
            pltpu.SemaphoreType.DMA((2,)),
        ],
        cost_estimate=pl.CostEstimate(
            flops=4 * pairs * width**3, bytes_accessed=8 * pairs * width**2, transcendentals=0
        ),
        compiler_params=pltpu.CompilerParams(vmem_limit_bytes=BIG),
        name="residual",
    )(places, pair_occ, domain, eps_occ, eps_vir, mixed, first, second)


def body(amplitudes, integral_tiles, need_owner, need_slot, pair_occ, domain, eps_occ, eps_vir):
    held, tile, _ = integral_tiles.shape
    half = held // 2
    vir = lax.axis_size("vir")
    n_pair = lax.axis_size("pair")
    owner, slot = need_owner[:, 0], need_slot[:, 0]
    asks = owner.shape[0]
    column = owner % vir
    across = (owner // vir - lax.axis_index("pair") + n_pair) % n_pair
    code = (across * 2 + slot // half) * 32 + slot % half
    order = jnp.arange(asks, dtype=jnp.int32)
    earlier = (column[:, None] == column[None, :]) & (order[None, :] < order[:, None])
    rank = jnp.sum(earlier.astype(jnp.int32), axis=1)
    places = column * PER_COLUMN + rank
    all_slots = jnp.arange(vir * PER_COLUMN, dtype=jnp.int32)
    hits = places[None, :] == all_slots[:, None]
    requests = jnp.sum(jnp.where(hits, code[None, :], 0), axis=1).reshape(vir, PER_COLUMN)
    codes = lax.all_to_all(requests, "vir", split_axis=0, concat_axis=0, tiled=True)
    codes = codes.reshape(vir * PER_COLUMN)

    first = gather_pairs(
        integral_tiles[:half, :ROWS_FIRST], integral_tiles[half:, :ROWS_FIRST]
    )
    low, high = split(integral_tiles, first[0], ROWS_FIRST, tile - ROWS_FIRST)
    second = gather_pairs(low, high)

    served = serve(codes, integral_tiles, first, 0, ROWS_FIRST)
    mixed = mix(amplitudes, served)
    got_first = lax.all_to_all(served, "vir", split_axis=0, concat_axis=0, tiled=True)
    served = serve(codes, integral_tiles, second, ROWS_FIRST, tile - ROWS_FIRST)
    got_second = lax.all_to_all(served, "vir", split_axis=0, concat_axis=0, tiled=True)
    return residual(
        places,
        pair_occ.reshape(-1),
        domain.reshape(-1),
        eps_occ,
        eps_vir.reshape(-1, tile),
        mixed,
        got_first,
        got_second,
    )


def solution(mesh):
    split_both = ("pair", "vir")
    return jax.shard_map(
        body,
        mesh=mesh,
        in_specs=(
            P(split_both, None, None),
            P(split_both, None, None),
            P(split_both, None),
            P(split_both, None),
            P(split_both, None),
            P(split_both, None),
            P(),
            P(),
        ),
        out_specs=P(split_both, None, None),
        check_vma=False,
    )
```

time: 292 us -> 449 us (1.54)
  Pallas kernels: 0 us -> 248 us
  waiting for transfers between devices: 180 us -> 138 us
  local copies, waits for them, and re-layouts: 38.2 us -> 4.99 us
  matrix products: 23.3 us -> 0 us
  starting transfers between devices: 11 us -> 31.9 us
  between operations: 13.5 us -> 0.38 us
    pallas_call x0 -> x5, Pallas kernels: none -> 248 us  [the longest x2 194 us: serve(): pl.pallas_call(functools.partial(serve_kernel, row_from), out_shape=jax.S...]
    all_gather x1 -> x0, waiting for transfers between devices: 47.9 us -> none  [body(): copies = lax.all_gather(integral_tiles, 'pair', axis=0, tiled=True)]
    ppermute x0 -> x12, waiting for transfers between devices: none -> 36.5 us  [the longest x2 13.9 us: gather_pairs(): up_low = lax.ppermute(low, 'pair', up)]
    all_to_all x1 -> x2, waiting for transfers between devices: 131 us -> 102 us  [body(): lax.all_to_all(served, 'vir', split_axis=0, concat_axis=0, tiled=True)]
    dot_general x2 -> x0, matrix products: 23.3 us -> none  [the longest x1 12.1 us: body(): jnp.einsum('pca,pcb->pab', blocks, mixed, preferred_element_type=jnp.floa...]
    gather x5 -> x0, local copies, waits for them, and re-layouts: 16.8 us -> none  [the longest x1 10.8 us: body(): served = copies[jnp.maximum(received, 0)]]
    ppermute x0 -> x12, starting transfers between devices: none -> 15.4 us  [the longest x2 4.16 us: gather_pairs(): far_high = lax.ppermute(down_high, 'pair', down)]
    reshape x1 -> x3, local copies, waits for them, and re-layouts: 8.44 us -> 0.88 us  [the longest x1 0.71 us: body(): codes = codes.reshape(vir * PER_COLUMN)]
  transfers between devices with their start and end apart: 2 -> 14, of which waited for: 2 -> 6; matrix products, arithmetic and copies ran while one was open for 5% -> 1% of each run, Pallas kernels for 0% -> 42%
where the time goes in v1:
time: 449 us
  Pallas kernels  248 us (55%)
  waiting for transfers between devices  138 us (31%)
  starting transfers between devices  31.9 us (7%)
  blocking collectives  22.9 us (5%)
  local copies, waits for them, and re-layouts  4.99 us (1%)
    pallas_call x2, Pallas kernels, serve(): pl.pallas_call(functools.partial(serve_kernel, row_from), out_shape=jax.S...  194 us
    all_to_all x2, waiting for transfers between devices, body(): lax.all_to_all(served, 'vir', split_axis=0, concat_axis=0, tiled=True)  102 us
    pallas_call x1, Pallas kernels, split(): pl.pallas_call(functools.partial(split_kernel, row_from), out_shape=(shap...  36.9 us
    all_to_all x1, blocking collectives, body(): lax.all_to_all(requests, 'vir', split_axis=0, concat_axis=0, tiled=True)  22.9 us
    all_to_all x2, starting transfers between devices, body(): lax.all_to_all(served, 'vir', split_axis=0, concat_axis=0, tiled=True)  16.5 us
    ppermute x2, waiting for transfers between devices, gather_pairs(): up_low = lax.ppermute(low, 'pair', up)  13.9 us
    ppermute x2, waiting for transfers between devices, gather_pairs(): far_low = lax.ppermute(up_low, 'pair', up)  12.6 us
    pallas_call x1, Pallas kernels, residual(): pl.pallas_call(functools.partial(residual_kernel, rows_first, tile), grid...  11.7 us
  transfers between devices with their start and end apart: 14, of which 6 were waited for; matrix products, arithmetic and copies ran while one was open for 1% of the time, Pallas kernels for 42%

profile of v1, /device:TPU:1, one launch (start us, length us, event | category | flops | bytes accessed | tf_op | source)
XLA Modules:
  0.0 448.6 jit_solution(9420990365928918373)
XLA Ops:
  0.0 1.1 fusion.8
  1.1 2.1 collective-permute-start.5
  3.2 1.4 collective-permute-start.1
  4.6 2.6 collective-permute-start
  8.8 1.5 collective-permute-start.4
  10.3 2.1 collective-permute-done.2.refs_4_
  13.1 22.9 %all_to_all.19 = s32[64,1,3]{2,1,0:T(1,128)S(1)} all-to-all(s32[64,1,3]{2,1,0:T(1,128)S(1)} %bitcast.43), channel_id=1, replica_groups=mesh['pair'=4,'vir'=64] {'vir'}, dimensions={0} | all-to-all | bytes 1536 | tf_op jit(solution)/shard_map/all_to_all | solution.py:236
  39.4 49.5 %serve_tiles.2.after_ref = bf16[192,32,128]{2,1,0:T(8,128)(2,1)} custom-call(s32[192]{0:T(256)} %reshape.126.code_ref, bf16[48,128,128]{2,1,0:T(8,128)(2,1)} %tiles_ref.5, bf16[24,32,128]{2,1,0:T(8,128)(2,1)} %copy-done.3, bf16[24,32,128]{2,1,0:T(8,128)(2,1)} %copy-done.10, bf16[24,32,128]{2,1,0:T(8,128)(2,1)} %copy-done.13, ...), custom_call_target="tpu_custom_call" | custom-call | bytes 3145728 | tf_op jit(solution)/shard_map/serve_tiles/pallas_call | solution.py:78
  88.9 4.8 %all-to-all-start.1 = ((bf16[192,32,128]{2,1,0:T(8,128)(2,1)}), bf16[192,32,128]{2,1,0:T(8,128)(2,1)S(1)}, u32[]{:S(2)}, u32[]{:S(2)}) async-start(bf16[192,32,128]{2,1,0:T(8,128)(2,1)} %serve_tiles.2.after_ref), calls=%async_computation.1 | async-start | bytes 3145728 | tf_op jit(solution)/shard_map/all_to_all | solution.py:247
  93.7 36.9 %split_rows.1 = (bf16[24,96,128]{2,1,0:T(8,128)(2,1)}, bf16[24,96,128]{2,1,0:T(8,128)(2,1)}) custom-call(bf16[48,128,128]{2,1,0:T(8,128)(2,1)} %tiles_ref.5, bf16[24,32,128]{2,1,0:T(8,128)(2,1)} %copy-done.3), custom_call_target="tpu_custom_call" | custom-call | bytes 2359296 | tf_op jit(solution)/shard_map/split_rows/pallas_call | solution.py:34
  130.6 1.3 collective-permute-start.8
  131.9 1.8 collective-permute-start.7
  133.6 1.4 collective-permute-start.6
  135.1 11.8 %collective-permute-done.8.refs_4_ = bf16[24,96,128]{2,1,0:T(8,128)(2,1)S(1)} collective-permute-done((bf16[24,96,128]{2,1,0:T(8,128)(2,1)}, bf16[24,96,128]{2,1,0:T(8,128)(2,1)S(1)}, u32[]{:S(2)}, u32[]{:S(2)}) %collective-permute-start.8) | collective-permute-done | bytes 589856 | tf_op jit(solution)/shard_map/ppermute | solution.py:95
  146.9 2.7 collective-permute-start.10
  149.6 9.2 %collective-permute-done.6.refs_0_ = bf16[24,96,128]{2,1,0:T(8,128)(2,1)S(1)} collective-permute-done((bf16[24,96,128]{2,1,0:T(8,128)(2,1)}, bf16[24,96,128]{2,1,0:T(8,128)(2,1)S(1)}, u32[]{:S(2)}, u32[]{:S(2)}) %collective-permute-start.6) | collective-permute-done | bytes 589856 | tf_op jit(solution)/shard_map/ppermute | solution.py:98
  158.7 0.8 collective-permute-done.11.refs_5_
  159.5 12.6 %collective-permute-done.9.refs_2_ = bf16[24,96,128]{2,1,0:T(8,128)(2,1)S(1)} collective-permute-done((bf16[24,96,128]{2,1,0:T(8,128)(2,1)S(1)}, bf16[24,96,128]{2,1,0:T(8,128)(2,1)S(1)}, u32[]{:S(2)}, u32[]{:S(2)}) %collective-permute-start.9) | collective-permute-done | bytes 589856 | tf_op jit(solution)/shard_map/ppermute | solution.py:99
  172.2 0.8 copy-done.8
  173.0 144.8 %serve_tiles.3 = bf16[192,96,128]{2,1,0:T(8,128)(2,1)} custom-call(s32[192]{0:T(256)} %reshape.126.code_ref, bf16[48,128,128]{2,1,0:T(8,128)(2,1)} %tiles_ref.5, bf16[24,96,128]{2,1,0:T(8,128)(2,1)} %copy-done.6, bf16[24,96,128]{2,1,0:T(8,128)(2,1)} %copy-done.5, bf16[24,96,128]{2,1,0:T(8,128)(2,1)} %copy-done.8, ...), custom_call_target="tpu_custom_call" | custom-call | bytes 9437184 | tf_op jit(solution)/shard_map/serve_tiles/pallas_call | solution.py:78
  317.9 11.7 %all-to-all-start.2 = ((bf16[192,96,128]{2,1,0:T(8,128)(2,1)}), bf16[192,96,128]{2,1,0:T(8,128)(2,1)}, u32[]{:S(2)}, u32[]{:S(2)}) async-start(bf16[192,96,128]{2,1,0:T(8,128)(2,1)} %serve_tiles.3), calls=%async_computation.2 | async-start | bytes 9437184 | tf_op jit(solution)/shard_map/all_to_all | solution.py:249
  329.9 5.3 %mix_amplitudes.1.mixed_ref = bf16[3,768,768]{2,1,0:T(8,128)(2,1)} custom-call(bf16[3,768,768]{2,1,0:T(8,128)(2,1)} %amp_ref.1, bf16[192,32,128]{2,1,0:T(8,128)(2,1)S(1)} %copy-done), custom_call_target="tpu_custom_call" | custom-call | flops 1769472 | bytes 7077888 | tf_op jit(solution)/shard_map/mix_amplitudes/pallas_call | solution.py:114
  335.2 101.5 %all-to-all-done.2.second_ref = bf16[192,96,128]{2,1,0:T(8,128)(2,1)} async-done(((bf16[192,96,128]{2,1,0:T(8,128)(2,1)}), bf16[192,96,128]{2,1,0:T(8,128)(2,1)}, u32[]{:S(2)}, u32[]{:S(2)}) %all-to-all-start.2) | async-done | bytes 4718624 | tf_op jit(solution)/shard_map/all_to_all | solution.py:249
  436.8 11.7 %residual.1 = f32[3,768,768]{2,1,0:T(8,128)} custom-call(s32[108]{0:T(128)S(1)} %multiply_add_fusion.place_ref, s32[6]{0:T(128)S(1)} %reshape.123.occ_ref, s32[18]{0:T(128)S(1)} %reshape.124.domain_ref, f32[400]{0:T(512)S(1)} %copy-done.2, f32[25,128]{1,0:T(8,128)S(1)} %bitcast.42, bf16[3,768,768]{2,1,0:T(8,128)(2,1)} %mix_amplitudes.1.mixed_ref, ...), custom_call_target="tpu_custom_call" | custom-call | flops 5435817984 | bytes 14155776 | tf_op jit(solution)/shard_map/residual/pallas_call | solution.py:192
  (55 shorter events, 6.2 us)
Async XLA Ops:
  1.1 36.8 %collective-permute-start.5 = (bf16[24,32,128]{2,1,0:T(8,128)(2,1)S(1)}, bf16[24,32,128]{2,1,0:T(8,128)(2,1)S(1)}, u32[]{:S(2)}, u32[]{:S(2)}) collective-permute-start(bf16[24,32,128]{2,1,0:T(8,128)(2,1)S(1)} %get-tuple-element.9), channel_id=1, source_target_pairs={{0,64},{64,128},{128,192},{192,0},{1,65},{65,129},{129,193},{193,1... | collective-permute-start | bytes 589832 | tf_op jit(solution)/shard_map/ppermute | solution.py:97
  3.2 5.6 %collective-permute-start.1 = (bf16[24,32,128]{2,1,0:T(8,128)(2,1)S(1)}, bf16[24,32,128]{2,1,0:T(8,128)(2,1)S(1)}, u32[]{:S(2)}, u32[]{:S(2)}) collective-permute-start(bf16[24,32,128]{2,1,0:T(8,128)(2,1)S(1)} %get-tuple-element.9), channel_id=1, source_target_pairs={{0,192},{64,0},{128,64},{192,128},{1,193},{65,1},{129,65},{193,129... | collective-permute-start | bytes 589832 | tf_op jit(solution)/shard_map/ppermute | solution.py:96
  4.5 7.8 %collective-permute-start.2 = (bf16[24,32,128]{2,1,0:T(8,128)(2,1)S(1)}, bf16[24,32,128]{2,1,0:T(8,128)(2,1)S(1)}, u32[]{:S(2)}, u32[]{:S(2)}) collective-permute-start(bf16[24,32,128]{2,1,0:T(8,128)(2,1)S(1)} %get-tuple-element.10), channel_id=1, source_target_pairs={{0,64},{64,128},{128,192},{192,0},{1,65},{65,129},{129,193},{193,1... | collective-permute-start | bytes 589832 | tf_op jit(solution)/shard_map/ppermute | solution.py:95
  4.6 33.2 %collective-permute-start = (bf16[24,32,128]{2,1,0:T(8,128)(2,1)S(1)}, bf16[24,32,128]{2,1,0:T(8,128)(2,1)S(1)}, u32[]{:S(2)}, u32[]{:S(2)}) collective-permute-start(bf16[24,32,128]{2,1,0:T(8,128)(2,1)S(1)} %get-tuple-element.10), channel_id=1, source_target_pairs={{0,192},{64,0},{128,64},{192,128},{1,193},{65,1},{129,65},{193,129... | collective-permute-start | bytes 589832 | tf_op jit(solution)/shard_map/ppermute | solution.py:98
  8.8 29.2 %copy-start.10 = (bf16[24,32,128]{2,1,0:T(8,128)(2,1)}, bf16[24,32,128]{2,1,0:T(8,128)(2,1)S(1)}, u32[]{:S(2)}) copy-start(bf16[24,32,128]{2,1,0:T(8,128)(2,1)S(1)} %collective-permute-done.1.refs_1_) | copy-start | bytes 589828
  8.8 29.1 %collective-permute-start.4 = (bf16[24,32,128]{2,1,0:T(8,128)(2,1)S(1)}, bf16[24,32,128]{2,1,0:T(8,128)(2,1)S(1)}, u32[]{:S(2)}, u32[]{:S(2)}) collective-permute-start(bf16[24,32,128]{2,1,0:T(8,128)(2,1)S(1)} %collective-permute-done.1.refs_1_), channel_id=1, source_target_pairs={{0,192},{64,0},{128,64},{192,128},{1,193},{65,1},{129,65},{193,129... | collective-permute-start | bytes 589832 | tf_op jit(solution)/shard_map/ppermute | solution.py:100
  12.4 25.6 %copy-start.11 = (bf16[24,32,128]{2,1,0:T(8,128)(2,1)}, bf16[24,32,128]{2,1,0:T(8,128)(2,1)S(1)}, u32[]{:S(2)}) copy-start(bf16[24,32,128]{2,1,0:T(8,128)(2,1)S(1)} %collective-permute-done.2.refs_4_) | copy-start | bytes 589828
  12.4 25.6 %collective-permute-start.3 = (bf16[24,32,128]{2,1,0:T(8,128)(2,1)S(1)}, bf16[24,32,128]{2,1,0:T(8,128)(2,1)S(1)}, u32[]{:S(2)}, u32[]{:S(2)}) collective-permute-start(bf16[24,32,128]{2,1,0:T(8,128)(2,1)S(1)} %collective-permute-done.2.refs_4_), channel_id=1, source_target_pairs={{0,64},{64,128},{128,192},{192,0},{1,65},{65,129},{129,193},{193,1... | collective-permute-start | bytes 589832 | tf_op jit(solution)/shard_map/ppermute | solution.py:99
  88.9 228.9 %all-to-all-start.1 = ((bf16[192,32,128]{2,1,0:T(8,128)(2,1)}), bf16[192,32,128]{2,1,0:T(8,128)(2,1)S(1)}, u32[]{:S(2)}, u32[]{:S(2)}) async-start(bf16[192,32,128]{2,1,0:T(8,128)(2,1)} %serve_tiles.2.after_ref), calls=%async_computation.1 | async-start | bytes 3145728 | tf_op jit(solution)/shard_map/all_to_all | solution.py:247
  130.6 16.3 %collective-permute-start.8 = (bf16[24,96,128]{2,1,0:T(8,128)(2,1)}, bf16[24,96,128]{2,1,0:T(8,128)(2,1)S(1)}, u32[]{:S(2)}, u32[]{:S(2)}) collective-permute-start(bf16[24,96,128]{2,1,0:T(8,128)(2,1)} %get-tuple-element.7), channel_id=1, source_target_pairs={{0,64},{64,128},{128,192},{192,0},{1,65},{65,129},{129,193},{193,1... | collective-permute-start | bytes 1769480 | tf_op jit(solution)/shard_map/ppermute | solution.py:95
  131.9 15.0 %collective-permute-start.7 = (bf16[24,96,128]{2,1,0:T(8,128)(2,1)}, bf16[24,96,128]{2,1,0:T(8,128)(2,1)S(1)}, u32[]{:S(2)}, u32[]{:S(2)}) collective-permute-start(bf16[24,96,128]{2,1,0:T(8,128)(2,1)} %get-tuple-element.8), channel_id=1, source_target_pairs={{0,192},{64,0},{128,64},{192,128},{1,193},{65,1},{129,65},{193,129... | collective-permute-start | bytes 1769480 | tf_op jit(solution)/shard_map/ppermute | solution.py:96
  133.6 25.1 %collective-permute-start.6 = (bf16[24,96,128]{2,1,0:T(8,128)(2,1)}, bf16[24,96,128]{2,1,0:T(8,128)(2,1)S(1)}, u32[]{:S(2)}, u32[]{:S(2)}) collective-permute-start(bf16[24,96,128]{2,1,0:T(8,128)(2,1)} %get-tuple-element.7), channel_id=1, source_target_pairs={{0,192},{64,0},{128,64},{192,128},{1,193},{65,1},{129,65},{193,129... | collective-permute-start | bytes 1769480 | tf_op jit(solution)/shard_map/ppermute | solution.py:98
  135.0 24.5 %collective-permute-start.11 = (bf16[24,96,128]{2,1,0:T(8,128)(2,1)}, bf16[24,96,128]{2,1,0:T(8,128)(2,1)S(1)}, u32[]{:S(2)}, u32[]{:S(2)}) collective-permute-start(bf16[24,96,128]{2,1,0:T(8,128)(2,1)} %get-tuple-element.8), channel_id=1, source_target_pairs={{0,64},{64,128},{128,192},{192,0},{1,65},{65,129},{129,193},{193,1... | collective-permute-start | bytes 1769480 | tf_op jit(solution)/shard_map/ppermute | solution.py:97
  146.9 26.1 %copy-start.4 = (bf16[24,96,128]{2,1,0:T(8,128)(2,1)}, bf16[24,96,128]{2,1,0:T(8,128)(2,1)S(1)}, u32[]{:S(2)}) copy-start(bf16[24,96,128]{2,1,0:T(8,128)(2,1)S(1)} %collective-permute-done.8.refs_4_) | copy-start | bytes 1769476
  146.9 25.3 %collective-permute-start.9 = (bf16[24,96,128]{2,1,0:T(8,128)(2,1)S(1)}, bf16[24,96,128]{2,1,0:T(8,128)(2,1)S(1)}, u32[]{:S(2)}, u32[]{:S(2)}) collective-permute-start(bf16[24,96,128]{2,1,0:T(8,128)(2,1)S(1)} %collective-permute-done.8.refs_4_), channel_id=1, source_target_pairs={{0,64},{64,128},{128,192},{192,0},{1,65},{65,129},{129,193},{193,1... | collective-permute-start | bytes 1769480 | tf_op jit(solution)/shard_map/ppermute | solution.py:99
  146.9 26.1 %copy-start.5 = (bf16[24,96,128]{2,1,0:T(8,128)(2,1)}, bf16[24,96,128]{2,1,0:T(8,128)(2,1)S(1)}, u32[]{:S(2)}) copy-start(bf16[24,96,128]{2,1,0:T(8,128)(2,1)S(1)} %collective-permute-done.7.refs_1_) | copy-start | bytes 1769476
  146.9 26.1 %collective-permute-start.10 = (bf16[24,96,128]{2,1,0:T(8,128)(2,1)S(1)}, bf16[24,96,128]{2,1,0:T(8,128)(2,1)}, u32[]{:S(2)}, u32[]{:S(2)}) collective-permute-start(bf16[24,96,128]{2,1,0:T(8,128)(2,1)S(1)} %collective-permute-done.7.refs_1_), channel_id=1, source_target_pairs={{0,192},{64,0},{128,64},{192,128},{1,193},{65,1},{129,65},{193,129... | collective-permute-start | bytes 1769480 | tf_op jit(solution)/shard_map/ppermute | solution.py:100
  158.7 14.3 %copy-start.6 = (bf16[24,96,128]{2,1,0:T(8,128)(2,1)}, bf16[24,96,128]{2,1,0:T(8,128)(2,1)S(1)}, u32[]{:S(2)}) copy-start(bf16[24,96,128]{2,1,0:T(8,128)(2,1)S(1)} %collective-permute-done.6.refs_0_) | copy-start | bytes 1769476
  159.5 12.6 %copy-start.7 = (bf16[24,96,128]{2,1,0:T(8,128)(2,1)}, bf16[24,96,128]{2,1,0:T(8,128)(2,1)S(1)}, u32[]{:S(2)}) copy-start(bf16[24,96,128]{2,1,0:T(8,128)(2,1)S(1)} %collective-permute-done.11.refs_5_) | copy-start | bytes 1769476
  317.8 11.9 %copy-start.15 = (s32[3,2]{0,1:T(2,128)S(1)}, s32[3,2]{0,1:T(2,128)}, u32[]{:S(2)}) copy-start(s32[3,2]{0,1:T(2,128)} %param.12) | copy-start | bytes 76
  317.8 12.0 %copy-start = (bf16[192,32,128]{2,1,0:T(8,128)(2,1)S(1)}, bf16[192,32,128]{2,1,0:T(8,128)(2,1)}, u32[]{:S(2)}) copy-start(bf16[192,32,128]{2,1,0:T(8,128)(2,1)} %serve_tiles.2.after_ref) | copy-start | bytes 4718596
  317.9 118.9 %all-to-all-start.2 = ((bf16[192,96,128]{2,1,0:T(8,128)(2,1)}), bf16[192,96,128]{2,1,0:T(8,128)(2,1)}, u32[]{:S(2)}, u32[]{:S(2)}) async-start(bf16[192,96,128]{2,1,0:T(8,128)(2,1)} %serve_tiles.3), calls=%async_computation.2 | async-start | bytes 9437184 | tf_op jit(solution)/shard_map/all_to_all | solution.py:249
  329.9 106.9 %copy-start.1 = (f32[3200]{0:T(1024)S(1)}, f32[3200]{0:T(1024)}, u32[]{:S(2)}) copy-start(f32[3200]{0:T(1024)} %param.15) | copy-start | bytes 38404
  329.9 106.9 %copy-start.2 = (f32[400]{0:T(512)S(1)}, f32[400]{0:T(512)}, u32[]{:S(2)}) copy-start(f32[400]{0:T(512)} %eps_occ_ref.1) | copy-start | bytes 4804
  (6 other events, 15.5 us)

commit v2 on v1

--- a/solution.py
+++ b/solution.py
@@ -9,9 +9,48 @@
 
 ROWS_FIRST = 32
 PER_COLUMN = 3
+DEEP = 8
 ANY = pl.BlockSpec(memory_space=pl.ANY)
+VMEM = pl.BlockSpec(memory_space=pltpu.VMEM)
 SMEM = pl.BlockSpec(memory_space=pltpu.SMEM)
 BIG = 100 * 2**20 // 2
+
+
+def ask_kernel(n_pair, half, here_ref, owner_ref, slot_ref, request_ref, place_ref):
+    vir = request_ref.shape[0]
+    owner, slot = owner_ref[...], slot_ref[...]
+    asks = owner.shape[1]
+    column = owner % vir
+    across = (owner // vir - here_ref[0] + n_pair) % n_pair
+    code = (across * 2 + slot // half) * 32 + slot % half
+    along = jnp.broadcast_to(column, (asks, asks))
+    down = jnp.transpose(along)
+    at_row = lax.broadcasted_iota(jnp.int32, (asks, asks), 0)
+    at_column = lax.broadcasted_iota(jnp.int32, (asks, asks), 1)
+    earlier = jnp.where((along == down) & (at_row < at_column), 1, 0)
+    place = column * PER_COLUMN + jnp.sum(earlier, axis=0, keepdims=True)
+    place_ref[...] = place
+    target = lax.broadcasted_iota(jnp.int32, (vir, asks), 0) * PER_COLUMN
+    lane = lax.broadcasted_iota(jnp.int32, (vir, request_ref.shape[2]), 1)
+    request = jnp.zeros((vir, request_ref.shape[2]), jnp.int32)
+    for k in range(PER_COLUMN):
+        asked = jnp.sum(jnp.where(place == target + k, code, 0), axis=1, keepdims=True)
+        request = jnp.where(lane == k, asked, request)
+    request_ref[...] = jnp.zeros_like(request_ref)
+    request_ref[:, 0, :] = request
+
+
+def ask(here, owner, slot, n_pair, vir, half):
+    return pl.pallas_call(
+        functools.partial(ask_kernel, n_pair, half),
+        out_shape=(
+            jax.ShapeDtypeStruct((vir, DEEP, 128), jnp.int32),
+            jax.ShapeDtypeStruct(owner.shape, jnp.int32),
+        ),
+        in_specs=[SMEM, VMEM, VMEM],
+        out_specs=(VMEM, VMEM),
+        name="make_requests",
+    )(here, owner, slot)
 
 
 def split_kernel(row_from, tiles_ref, after_ref, low_ref, high_ref, sem):
@@ -35,8 +74,9 @@
         functools.partial(split_kernel, row_from),
         out_shape=(shape, shape),
         in_specs=[ANY, ANY],
-        out_specs=(ANY, ANY),
+        out_specs=(VMEM, VMEM),
         scratch_shapes=[pltpu.SemaphoreType.DMA((2,))],
+        compiler_params=pltpu.CompilerParams(vmem_limit_bytes=BIG),
         cost_estimate=pl.CostEstimate(
             flops=0, bytes_accessed=4 * half * rows * 128 * 2, transcendentals=0
         ),
@@ -45,12 +85,15 @@
 
 
 def serve_kernel(row_from, code_ref, tiles_ref, *refs):
-    sources, out_ref, sem = refs[:6], refs[6], refs[7]
+    sources, (out_ref, code_smem, code_sem, sem) = refs[:6], refs[6:]
+    copy = pltpu.make_async_copy(code_ref.at[:, pl.ds(0, 1)], code_smem, code_sem)
+    copy.start()
+    copy.wait()
     half = tiles_ref.shape[0] // 2
     rows = out_ref.shape[1]
 
     def step(slot, carry):
-        code = code_ref[slot]
+        code = code_smem[slot // PER_COLUMN, 0, slot % PER_COLUMN]
         place = code & 31
 
         def own():
@@ -74,13 +117,18 @@
 
 
 def serve(codes, tiles, sources, row_from, rows):
-    slots = codes.shape[0]
+    slots = codes.shape[0] * PER_COLUMN
     return pl.pallas_call(
         functools.partial(serve_kernel, row_from),
         out_shape=jax.ShapeDtypeStruct((slots, rows, tiles.shape[2]), tiles.dtype),
-        in_specs=[SMEM] + [ANY] * 7,
-        out_specs=ANY,
-        scratch_shapes=[pltpu.SemaphoreType.DMA],
+        in_specs=[ANY] * 8,
+        out_specs=VMEM,
+        scratch_shapes=[
+            pltpu.SMEM((codes.shape[0], 1, codes.shape[2]), jnp.int32),
+            pltpu.SemaphoreType.DMA,
+            pltpu.SemaphoreType.DMA,
+        ],
+        compiler_params=pltpu.CompilerParams(vmem_limit_bytes=BIG),
         cost_estimate=pl.CostEstimate(
             flops=0, bytes_accessed=2 * slots * rows * 128 * 2, transcendentals=0
         ),
@@ -220,25 +268,13 @@
     held, tile, _ = integral_tiles.shape
     half = held // 2
     vir = lax.axis_size("vir")
-    n_pair = lax.axis_size("pair")
-    owner, slot = need_owner[:, 0], need_slot[:, 0]
-    asks = owner.shape[0]
-    column = owner % vir
-    across = (owner // vir - lax.axis_index("pair") + n_pair) % n_pair
-    code = (across * 2 + slot // half) * 32 + slot % half
-    order = jnp.arange(asks, dtype=jnp.int32)
-    earlier = (column[:, None] == column[None, :]) & (order[None, :] < order[:, None])
-    rank = jnp.sum(earlier.astype(jnp.int32), axis=1)
-    places = column * PER_COLUMN + rank
-    all_slots = jnp.arange(vir * PER_COLUMN, dtype=jnp.int32)
-    hits = places[None, :] == all_slots[:, None]
-    requests = jnp.sum(jnp.where(hits, code[None, :], 0), axis=1).reshape(vir, PER_COLUMN)
+    here = lax.axis_index("pair").astype(jnp.int32).reshape(1)
+    requests, places = ask(
+        here, need_owner.reshape(1, -1), need_slot.reshape(1, -1), lax.axis_size("pair"), vir, half
+    )
     codes = lax.all_to_all(requests, "vir", split_axis=0, concat_axis=0, tiled=True)
-    codes = codes.reshape(vir * PER_COLUMN)
-
-    first = gather_pairs(
-        integral_tiles[:half, :ROWS_FIRST], integral_tiles[half:, :ROWS_FIRST]
-    )
+
+    first = gather_pairs(*split(integral_tiles, requests, 0, ROWS_FIRST))
     low, high = split(integral_tiles, first[0], ROWS_FIRST, tile - ROWS_FIRST)
     second = gather_pairs(low, high)
 
@@ -248,7 +284,7 @@
     served = serve(codes, integral_tiles, second, ROWS_FIRST, tile - ROWS_FIRST)
     got_second = lax.all_to_all(served, "vir", split_axis=0, concat_axis=0, tiled=True)
     return residual(
-        places,
+        places.reshape(-1),
         pair_occ.reshape(-1),
         domain.reshape(-1),
         eps_occ,

time: 449 us -> 243 us (0.54)
  Pallas kernels: 248 us -> 44.5 us
  blocking collectives: 22.9 us -> 0 us
  starting transfers between devices: 31.9 us -> 49 us
  waiting for transfers between devices: 138 us -> 144 us
    pallas_call x2, Pallas kernels: 194 us -> 25.7 us  [serve(): pl.pallas_call(functools.partial(serve_kernel, row_from), out_shape=jax.S...]
    pallas_call x1 -> x2, Pallas kernels: 36.9 us -> 0.18 us  [split(): pl.pallas_call(functools.partial(split_kernel, row_from), out_shape=(shap...]
    all_to_all x1 -> x0, blocking collectives: 22.9 us -> none  [body(): lax.all_to_all(requests, 'vir', split_axis=0, concat_axis=0, tiled=True)]
    all_to_all x0 -> x1, starting transfers between devices: none -> 13.2 us  [body(): lax.all_to_all(requests, 'vir', split_axis=0, concat_axis=0, tiled=True)]
    all_to_all x2, starting transfers between devices: 16.5 us -> 21.7 us  [body(): lax.all_to_all(served, 'vir', split_axis=0, concat_axis=0, tiled=True)]
  transfers between devices with their start and end apart: 14 -> 15, of which waited for: 6 -> 8; matrix products, arithmetic and copies ran while one was open for 1% -> 0% of each run, Pallas kernels for 42% -> 8%
where the time goes in v2:
time: 243 us; the launch traced here: 242 us
  waiting for transfers between devices  144 us (59%)
  starting transfers between devices  49 us (20%)
  Pallas kernels  44.5 us (18%)
  local copies, waits for them, and re-layouts  3.56 us (1%)
    all_to_all x2, waiting for transfers between devices, body(): lax.all_to_all(served, 'vir', split_axis=0, concat_axis=0, tiled=True)  102 us
    pallas_call x2, Pallas kernels, serve(): pl.pallas_call(functools.partial(serve_kernel, row_from), out_shape=jax.S...  25.7 us
    all_to_all x2, starting transfers between devices, body(): lax.all_to_all(served, 'vir', split_axis=0, concat_axis=0, tiled=True)  21.7 us
    ppermute x2, waiting for transfers between devices, gather_pairs(): far_low = lax.ppermute(up_low, 'pair', up)  16.9 us
    ppermute x2, waiting for transfers between devices, gather_pairs(): up_low = lax.ppermute(low, 'pair', up)  14.8 us
    all_to_all x1, starting transfers between devices, body(): lax.all_to_all(requests, 'vir', split_axis=0, concat_axis=0, tiled=True)  13.2 us
    pallas_call x1, Pallas kernels, residual(): pl.pallas_call(functools.partial(residual_kernel, rows_first, tile), grid...  11.7 us
    ppermute x2, waiting for transfers between devices, gather_pairs(): down_low = lax.ppermute(low, 'pair', down)  10.6 us
  transfers between devices with their start and end apart: 15, of which 8 were waited for; matrix products, arithmetic and copies ran while one was open for 0% of the time, Pallas kernels for 8%

profile of v2, /device:TPU:1, one launch (start us, length us, event | category | flops | bytes accessed | tf_op | source)
XLA Modules:
  0.0 241.9 jit_solution(10813861874259626320)
XLA Ops:
  0.0 1.7 make_requests.1
  1.7 13.2 %all-to-all-start = ((s32[64,8,128]{2,1,0:T(8,128)}), s32[64,8,128]{2,1,0:T(8,128)S(1)}, u32[]{:S(2)}, u32[]{:S(2)}) async-start(s32[64,8,128]{2,1,0:T(8,128)} %get-tuple-element.12.after_ref), calls=%async_computation | async-start | bytes 524288 | tf_op jit(solution)/shard_map/all_to_all | solution.py:275
  14.8 1.4 copy-done
  17.3 1.3 collective-permute-start.2
  18.6 1.5 collective-permute-start.1
  20.0 1.3 collective-permute-start
  21.5 3.1 %collective-permute-done.2.refs_4_ = bf16[24,32,128]{2,1,0:T(8,128)(2,1)S(1)} collective-permute-done((bf16[24,32,128]{2,1,0:T(8,128)(2,1)S(1)}, bf16[24,32,128]{2,1,0:T(8,128)(2,1)S(1)}, u32[]{:S(2)}, u32[]{:S(2)}) %collective-permute-start.2) | collective-permute-done | bytes 196640 | tf_op jit(solution)/shard_map/ppermute | solution.py:143
  24.6 2.7 %collective-permute-start.4 = (bf16[24,32,128]{2,1,0:T(8,128)(2,1)S(1)}, bf16[24,32,128]{2,1,0:T(8,128)(2,1)S(1)}, u32[]{:S(2)}, u32[]{:S(2)}) collective-permute-start(bf16[24,32,128]{2,1,0:T(8,128)(2,1)S(1)} %collective-permute-done.1.refs_1_), channel_id=1, source_target_pairs={{0,192},{64,0},{128,64},{192,128},{1,193},{65,1},{129,65},{193,129... | collective-permute-start | bytes 589832 | tf_op jit(solution)/shard_map/ppermute | solution.py:148
  27.3 1.2 collective-permute-done.refs_0_.after_ref
  28.5 4.3 %collective-permute-done.3.refs_2_ = bf16[24,32,128]{2,1,0:T(8,128)(2,1)S(1)} collective-permute-done((bf16[24,32,128]{2,1,0:T(8,128)(2,1)S(1)}, bf16[24,32,128]{2,1,0:T(8,128)(2,1)S(1)}, u32[]{:S(2)}, u32[]{:S(2)}) %collective-permute-start.3) | collective-permute-done | bytes 196640 | tf_op jit(solution)/shard_map/ppermute | solution.py:147
  32.8 11.4 %serve_tiles.2.after_ref = bf16[192,32,128]{2,1,0:T(8,128)(2,1)} custom-call(s32[64,8,128]{2,1,0:T(8,128)S(1)} %all-to-all-done.code_ref, bf16[48,128,128]{2,1,0:T(8,128)(2,1)} %tiles_ref.7, bf16[24,32,128]{2,1,0:T(8,128)(2,1)S(1)} %collective-permute-done.refs_0_.after_ref, bf16[24,32,128]{2,1,0:T(8,128)(2,1)S(1)} %collective-permute-done.1.refs_1_, ...), custom_call_target="tpu_custom_call" | custom-call | bytes 3145728 | tf_op jit(solution)/shard_map/serve_tiles/pallas_call | solution.py:121
  44.2 11.1 %all-to-all-start.1 = ((bf16[192,32,128]{2,1,0:T(8,128)(2,1)}), bf16[192,32,128]{2,1,0:T(8,128)(2,1)S(1)}, u32[]{:S(2)}, u32[]{:S(2)}) async-start(bf16[192,32,128]{2,1,0:T(8,128)(2,1)} %serve_tiles.2.after_ref), calls=%async_computation.1 | async-start | bytes 3145728 | tf_op jit(solution)/shard_map/all_to_all | solution.py:283
  56.4 1.7 collective-permute-start.8
  58.1 1.5 collective-permute-start.7
  59.6 1.4 collective-permute-start.6
  61.0 11.7 %collective-permute-done.8.refs_4_ = bf16[24,96,128]{2,1,0:T(8,128)(2,1)S(1)} collective-permute-done((bf16[24,96,128]{2,1,0:T(8,128)(2,1)S(1)}, bf16[24,96,128]{2,1,0:T(8,128)(2,1)S(1)}, u32[]{:S(2)}, u32[]{:S(2)}) %collective-permute-start.8) | collective-permute-done | bytes 589856 | tf_op jit(solution)/shard_map/ppermute | solution.py:143
  72.8 2.7 %collective-permute-start.10 = (bf16[24,96,128]{2,1,0:T(8,128)(2,1)S(1)}, bf16[24,96,128]{2,1,0:T(8,128)(2,1)S(1)}, u32[]{:S(2)}, u32[]{:S(2)}) collective-permute-start(bf16[24,96,128]{2,1,0:T(8,128)(2,1)S(1)} %collective-permute-done.7.refs_1_), channel_id=1, source_target_pairs={{0,192},{64,0},{128,64},{192,128},{1,193},{65,1},{129,65},{193,129... | collective-permute-start | bytes 1769480 | tf_op jit(solution)/shard_map/ppermute | solution.py:148
  75.5 9.4 %collective-permute-done.6.refs_0_ = bf16[24,96,128]{2,1,0:T(8,128)(2,1)S(1)} collective-permute-done((bf16[24,96,128]{2,1,0:T(8,128)(2,1)S(1)}, bf16[24,96,128]{2,1,0:T(8,128)(2,1)S(1)}, u32[]{:S(2)}, u32[]{:S(2)}) %collective-permute-start.6) | collective-permute-done | bytes 589856 | tf_op jit(solution)/shard_map/ppermute | solution.py:146
  85.4 12.6 %collective-permute-done.9.refs_2_ = bf16[24,96,128]{2,1,0:T(8,128)(2,1)S(1)} collective-permute-done((bf16[24,96,128]{2,1,0:T(8,128)(2,1)S(1)}, bf16[24,96,128]{2,1,0:T(8,128)(2,1)S(1)}, u32[]{:S(2)}, u32[]{:S(2)}) %collective-permute-start.9) | collective-permute-done | bytes 589856 | tf_op jit(solution)/shard_map/ppermute | solution.py:147
  98.1 14.2 %serve_tiles.3 = bf16[192,96,128]{2,1,0:T(8,128)(2,1)} custom-call(s32[64,8,128]{2,1,0:T(8,128)S(1)} %all-to-all-done.code_ref, bf16[48,128,128]{2,1,0:T(8,128)(2,1)} %tiles_ref.7, bf16[24,96,128]{2,1,0:T(8,128)(2,1)S(1)} %collective-permute-done.6.refs_0_, bf16[24,96,128]{2,1,0:T(8,128)(2,1)S(1)} %collective-permute-done.7.refs_1_, ...), custom_call_target="tpu_custom_call" | custom-call | bytes 9437184 | tf_op jit(solution)/shard_map/serve_tiles/pallas_call | solution.py:121
  112.4 10.5 %all-to-all-start.2 = ((bf16[192,96,128]{2,1,0:T(8,128)(2,1)}), bf16[192,96,128]{2,1,0:T(8,128)(2,1)}, u32[]{:S(2)}, u32[]{:S(2)}) async-start(bf16[192,96,128]{2,1,0:T(8,128)(2,1)} %serve_tiles.3), calls=%async_computation.2 | async-start | bytes 9437184 | tf_op jit(solution)/shard_map/all_to_all | solution.py:285
  123.2 5.4 %mix_amplitudes.1.mixed_ref = bf16[3,768,768]{2,1,0:T(8,128)(2,1)} custom-call(bf16[3,768,768]{2,1,0:T(8,128)(2,1)} %amp_ref.1, bf16[192,32,128]{2,1,0:T(8,128)(2,1)} %serve_tiles.2.after_ref), custom_call_target="tpu_custom_call" | custom-call | flops 1769472 | bytes 7077888 | tf_op jit(solution)/shard_map/mix_amplitudes/pallas_call | solution.py:162
  128.5 101.5 %all-to-all-done.2.second_ref = bf16[192,96,128]{2,1,0:T(8,128)(2,1)} async-done(((bf16[192,96,128]{2,1,0:T(8,128)(2,1)}), bf16[192,96,128]{2,1,0:T(8,128)(2,1)}, u32[]{:S(2)}, u32[]{:S(2)}) %all-to-all-start.2) | async-done | bytes 4718624 | tf_op jit(solution)/shard_map/all_to_all | solution.py:285
  230.1 11.7 %residual.1 = f32[3,768,768]{2,1,0:T(8,128)} custom-call(s32[108]{0:T(128)S(1)} %bitcast.6, s32[6]{0:T(128)S(1)} %reshape.25.occ_ref, s32[18]{0:T(128)S(1)} %reshape.26.domain_ref, f32[400]{0:T(512)S(1)} %copy-done.6, f32[25,128]{1,0:T(8,128)S(1)} %bitcast.5, bf16[3,768,768]{2,1,0:T(8,128)(2,1)} %mix_amplitudes.1.mixed_ref, ...), custom_call_target="tpu_custom_call" | custom-call | flops 5435817984 | bytes 14155776 | tf_op jit(solution)/shard_map/residual/pallas_call | solution.py:240
  (36 shorter events, 3.3 us)
Async XLA Ops:
  1.7 31.1 %all-to-all-start = ((s32[64,8,128]{2,1,0:T(8,128)}), s32[64,8,128]{2,1,0:T(8,128)S(1)}, u32[]{:S(2)}, u32[]{:S(2)}) async-start(s32[64,8,128]{2,1,0:T(8,128)} %get-tuple-element.12.after_ref), calls=%async_computation | async-start | bytes 524288 | tf_op jit(solution)/shard_map/all_to_all | solution.py:275
  14.8 1.4 copy-start
  16.2 0.9 copy-start.2
  17.3 7.3 %collective-permute-start.2 = (bf16[24,32,128]{2,1,0:T(8,128)(2,1)S(1)}, bf16[24,32,128]{2,1,0:T(8,128)(2,1)S(1)}, u32[]{:S(2)}, u32[]{:S(2)}) collective-permute-start(bf16[24,32,128]{2,1,0:T(8,128)(2,1)S(1)} %get-tuple-element.13), channel_id=1, source_target_pairs={{0,64},{64,128},{128,192},{192,0},{1,65},{65,129},{129,193},{193,1... | collective-permute-start | bytes 589832 | tf_op jit(solution)/shard_map/ppermute | solution.py:143
  18.6 36.8 %copy-start.1 = (bf16[48,128,128]{2,1,0:T(8,128)(2,1)S(1)}, bf16[48,128,128]{2,1,0:T(8,128)(2,1)}, u32[]{:S(2)}) copy-start(bf16[48,128,128]{2,1,0:T(8,128)(2,1)} %tiles_ref.7) | copy-start | bytes 4718596
  18.6 6.0 %collective-permute-start.1 = (bf16[24,32,128]{2,1,0:T(8,128)(2,1)S(1)}, bf16[24,32,128]{2,1,0:T(8,128)(2,1)S(1)}, u32[]{:S(2)}, u32[]{:S(2)}) collective-permute-start(bf16[24,32,128]{2,1,0:T(8,128)(2,1)S(1)} %get-tuple-element.14), channel_id=1, source_target_pairs={{0,192},{64,0},{128,64},{192,128},{1,193},{65,1},{129,65},{193,129... | collective-permute-start | bytes 589832 | tf_op jit(solution)/shard_map/ppermute | solution.py:144
  20.0 8.4 %collective-permute-start = (bf16[24,32,128]{2,1,0:T(8,128)(2,1)S(1)}, bf16[24,32,128]{2,1,0:T(8,128)(2,1)S(1)}, u32[]{:S(2)}, u32[]{:S(2)}) collective-permute-start(bf16[24,32,128]{2,1,0:T(8,128)(2,1)S(1)} %get-tuple-element.13), channel_id=1, source_target_pairs={{0,192},{64,0},{128,64},{192,128},{1,193},{65,1},{129,65},{193,129... | collective-permute-start | bytes 589832 | tf_op jit(solution)/shard_map/ppermute | solution.py:146
  21.3 7.2 %collective-permute-start.5 = (bf16[24,32,128]{2,1,0:T(8,128)(2,1)S(1)}, bf16[24,32,128]{2,1,0:T(8,128)(2,1)S(1)}, u32[]{:S(2)}, u32[]{:S(2)}) collective-permute-start(bf16[24,32,128]{2,1,0:T(8,128)(2,1)S(1)} %get-tuple-element.14), channel_id=1, source_target_pairs={{0,64},{64,128},{128,192},{192,0},{1,65},{65,129},{129,193},{193,1... | collective-permute-start | bytes 589832 | tf_op jit(solution)/shard_map/ppermute | solution.py:145
  24.6 8.2 %collective-permute-start.3 = (bf16[24,32,128]{2,1,0:T(8,128)(2,1)S(1)}, bf16[24,32,128]{2,1,0:T(8,128)(2,1)S(1)}, u32[]{:S(2)}, u32[]{:S(2)}) collective-permute-start(bf16[24,32,128]{2,1,0:T(8,128)(2,1)S(1)} %collective-permute-done.2.refs_4_), channel_id=1, source_target_pairs={{0,64},{64,128},{128,192},{192,0},{1,65},{65,129},{129,193},{193,1... | collective-permute-start | bytes 589832 | tf_op jit(solution)/shard_map/ppermute | solution.py:147
  24.6 8.2 %collective-permute-start.4 = (bf16[24,32,128]{2,1,0:T(8,128)(2,1)S(1)}, bf16[24,32,128]{2,1,0:T(8,128)(2,1)S(1)}, u32[]{:S(2)}, u32[]{:S(2)}) collective-permute-start(bf16[24,32,128]{2,1,0:T(8,128)(2,1)S(1)} %collective-permute-done.1.refs_1_), channel_id=1, source_target_pairs={{0,192},{64,0},{128,64},{192,128},{1,193},{65,1},{129,65},{193,129... | collective-permute-start | bytes 589832 | tf_op jit(solution)/shard_map/ppermute | solution.py:148
  28.5 15.7 %copy-start.3 = (bf16[24,32,128]{2,1,0:T(8,128)(2,1)}, bf16[24,32,128]{2,1,0:T(8,128)(2,1)S(1)}, u32[]{:S(2)}) copy-start(bf16[24,32,128]{2,1,0:T(8,128)(2,1)S(1)} %collective-permute-done.refs_0_.after_ref) | copy-start | bytes 589828
  44.2 68.1 %all-to-all-start.1 = ((bf16[192,32,128]{2,1,0:T(8,128)(2,1)}), bf16[192,32,128]{2,1,0:T(8,128)(2,1)S(1)}, u32[]{:S(2)}, u32[]{:S(2)}) async-start(bf16[192,32,128]{2,1,0:T(8,128)(2,1)} %serve_tiles.2.after_ref), calls=%async_computation.1 | async-start | bytes 3145728 | tf_op jit(solution)/shard_map/all_to_all | solution.py:283
  56.4 16.4 %collective-permute-start.8 = (bf16[24,96,128]{2,1,0:T(8,128)(2,1)S(1)}, bf16[24,96,128]{2,1,0:T(8,128)(2,1)S(1)}, u32[]{:S(2)}, u32[]{:S(2)}) collective-permute-start(bf16[24,96,128]{2,1,0:T(8,128)(2,1)S(1)} %get-tuple-element.15), channel_id=1, source_target_pairs={{0,64},{64,128},{128,192},{192,0},{1,65},{65,129},{129,193},{193,1... | collective-permute-start | bytes 1769480 | tf_op jit(solution)/shard_map/ppermute | solution.py:143
  58.1 14.7 %collective-permute-start.7 = (bf16[24,96,128]{2,1,0:T(8,128)(2,1)S(1)}, bf16[24,96,128]{2,1,0:T(8,128)(2,1)S(1)}, u32[]{:S(2)}, u32[]{:S(2)}) collective-permute-start(bf16[24,96,128]{2,1,0:T(8,128)(2,1)S(1)} %get-tuple-element.16), channel_id=1, source_target_pairs={{0,192},{64,0},{128,64},{192,128},{1,193},{65,1},{129,65},{193,129... | collective-permute-start | bytes 1769480 | tf_op jit(solution)/shard_map/ppermute | solution.py:144
  59.6 25.3 %collective-permute-start.6 = (bf16[24,96,128]{2,1,0:T(8,128)(2,1)S(1)}, bf16[24,96,128]{2,1,0:T(8,128)(2,1)S(1)}, u32[]{:S(2)}, u32[]{:S(2)}) collective-permute-start(bf16[24,96,128]{2,1,0:T(8,128)(2,1)S(1)} %get-tuple-element.15), channel_id=1, source_target_pairs={{0,192},{64,0},{128,64},{192,128},{1,193},{65,1},{129,65},{193,129... | collective-permute-start | bytes 1769480 | tf_op jit(solution)/shard_map/ppermute | solution.py:146
  60.9 24.5 %collective-permute-start.11 = (bf16[24,96,128]{2,1,0:T(8,128)(2,1)S(1)}, bf16[24,96,128]{2,1,0:T(8,128)(2,1)S(1)}, u32[]{:S(2)}, u32[]{:S(2)}) collective-permute-start(bf16[24,96,128]{2,1,0:T(8,128)(2,1)S(1)} %get-tuple-element.16), channel_id=1, source_target_pairs={{0,64},{64,128},{128,192},{192,0},{1,65},{65,129},{129,193},{193,1... | collective-permute-start | bytes 1769480 | tf_op jit(solution)/shard_map/ppermute | solution.py:145
  72.8 25.3 %collective-permute-start.9 = (bf16[24,96,128]{2,1,0:T(8,128)(2,1)S(1)}, bf16[24,96,128]{2,1,0:T(8,128)(2,1)S(1)}, u32[]{:S(2)}, u32[]{:S(2)}) collective-permute-start(bf16[24,96,128]{2,1,0:T(8,128)(2,1)S(1)} %collective-permute-done.8.refs_4_), channel_id=1, source_target_pairs={{0,64},{64,128},{128,192},{192,0},{1,65},{65,129},{129,193},{193,1... | collective-permute-start | bytes 1769480 | tf_op jit(solution)/shard_map/ppermute | solution.py:147
  72.8 25.3 %collective-permute-start.10 = (bf16[24,96,128]{2,1,0:T(8,128)(2,1)S(1)}, bf16[24,96,128]{2,1,0:T(8,128)(2,1)S(1)}, u32[]{:S(2)}, u32[]{:S(2)}) collective-permute-start(bf16[24,96,128]{2,1,0:T(8,128)(2,1)S(1)} %collective-permute-done.7.refs_1_), channel_id=1, source_target_pairs={{0,192},{64,0},{128,64},{192,128},{1,193},{65,1},{129,65},{193,129... | collective-permute-start | bytes 1769480 | tf_op jit(solution)/shard_map/ppermute | solution.py:148
  112.3 10.6 %copy-start.8 = (s32[3,6]{1,0:T(4,128)S(1)}, s32[3,6]{1,0:T(4,128)}, u32[]{:S(2)}) copy-start(s32[3,6]{1,0:T(4,128)} %param.13) | copy-start | bytes 220
  112.3 10.7 %copy-start.9 = (s32[3,2]{0,1:T(2,128)S(1)}, s32[3,2]{0,1:T(2,128)}, u32[]{:S(2)}) copy-start(s32[3,2]{0,1:T(2,128)} %param.12) | copy-start | bytes 76
  112.4 117.7 %all-to-all-start.2 = ((bf16[192,96,128]{2,1,0:T(8,128)(2,1)}), bf16[192,96,128]{2,1,0:T(8,128)(2,1)}, u32[]{:S(2)}, u32[]{:S(2)}) async-start(bf16[192,96,128]{2,1,0:T(8,128)(2,1)} %serve_tiles.3), calls=%async_computation.2 | async-start | bytes 9437184 | tf_op jit(solution)/shard_map/all_to_all | solution.py:285
  123.2 106.9 %copy-start.5 = (f32[3200]{0:T(1024)S(1)}, f32[3200]{0:T(1024)}, u32[]{:S(2)}) copy-start(f32[3200]{0:T(1024)} %param.15) | copy-start | bytes 38404
  123.2 106.9 %copy-start.6 = (f32[400]{0:T(512)S(1)}, f32[400]{0:T(512)}, u32[]{:S(2)}) copy-start(f32[400]{0:T(512)} %eps_occ_ref.1) | copy-start | bytes 4804
  123.2 106.9 %copy-start.7 = (s32[1,108]{1,0:T(1,128)S(1)}, s32[1,108]{1,0:T(1,128)}, u32[]{:S(2)}) copy-start(s32[1,108]{1,0:T(1,128)} %get-tuple-element.11) | copy-start | bytes 1300
  (1 other events, 0.9 us)

commit v3 on v2

v3 whole, which is shorter than its diff:
```python
import functools

import jax
import jax.numpy as jnp
from jax import lax
from jax.experimental import pallas as pl
from jax.experimental.pallas import tpu as pltpu
from jax.sharding import PartitionSpec as P

ROWS_FIRST = 32
PER_COLUMN = 3
ANY = pl.BlockSpec(memory_space=pl.ANY)
VMEM = pl.BlockSpec(memory_space=pltpu.VMEM)
SMEM = pl.BlockSpec(memory_space=pltpu.SMEM)
BIG = 100 * 2**20 // 2


def ask_kernel(held, owner_ref, slot_ref, request_ref, place_ref):
    vir = request_ref.shape[0]
    owner, slot = owner_ref[...], slot_ref[...]
    asks = owner.shape[1]
    column = owner % vir
    code = (owner // vir) * held + slot
    along = jnp.broadcast_to(column, (asks, asks))
    down = jnp.transpose(along)
    at_row = lax.broadcasted_iota(jnp.int32, (asks, asks), 0)
    at_column = lax.broadcasted_iota(jnp.int32, (asks, asks), 1)
    earlier = jnp.where((along == down) & (at_row < at_column), 1, 0)
    place = column * PER_COLUMN + jnp.sum(earlier, axis=0, keepdims=True)
    place_ref[...] = place
    target = lax.broadcasted_iota(jnp.int32, (vir, asks), 0) * PER_COLUMN
    request_ref[...] = jnp.concatenate(
        [
            jnp.sum(jnp.where(place == target + k, code, 0), axis=1, keepdims=True)
            for k in range(PER_COLUMN)
        ],
        axis=1,
    )


def ask(owner, slot, vir, held):
    return pl.pallas_call(
        functools.partial(ask_kernel, held),
        out_shape=(
            jax.ShapeDtypeStruct((vir, PER_COLUMN), jnp.int32),
            jax.ShapeDtypeStruct(owner.shape, jnp.int32),
        ),
        in_specs=[VMEM, VMEM],
        out_specs=(VMEM, VMEM),
        name="make_requests",
    )(owner, slot)


def serve_kernel(n_pair, row_from, here_ref, code_ref, own_ref, *refs):
    sources, (out_ref, pool, sem) = refs[: n_pair - 1], refs[n_pair - 1 :]
    held, rows = own_ref.shape[0], out_ref.shape[1]
    copies = []
    for step in range(n_pair):
        owner = (here_ref[0] + step) % n_pair
        source = sources[step - 1] if step else own_ref.at[:, pl.ds(row_from, rows)]
        target = pool.at[pl.ds(owner * held, held)]
        copies.append(pltpu.make_async_copy(source, target, sem.at[step]))
    for copy in copies:
        copy.start()
    for copy in copies:
        copy.wait()
    take(code_ref, pool, out_ref)


def take(code_ref, pool, out_ref):
    def step(column, carry):
        for k in range(PER_COLUMN):
            out_ref[column * PER_COLUMN + k] = pool[code_ref[column, 0, k]]
        return carry

    lax.fori_loop(0, code_ref.shape[0], step, 0, unroll=4)


def serve(here, codes, tiles, sources, row_from, rows):
    slots = codes.shape[0] * PER_COLUMN
    n_pair = len(sources) + 1
    held, tile = tiles.shape[0], tiles.shape[2]
    return pl.pallas_call(
        functools.partial(serve_kernel, n_pair, row_from),
        out_shape=jax.ShapeDtypeStruct((slots, rows, tile), tiles.dtype),
        in_specs=[SMEM, SMEM] + [ANY] * n_pair,
        out_specs=VMEM,
        scratch_shapes=[
            pltpu.VMEM((n_pair * held, rows, tile), tiles.dtype),
            pltpu.SemaphoreType.DMA((n_pair,)),
        ],
        compiler_params=pltpu.CompilerParams(vmem_limit_bytes=BIG),
        cost_estimate=pl.CostEstimate(
            flops=0, bytes_accessed=4 * slots * rows * tile, transcendentals=0
        ),
        name="serve_near",
    )(here, codes, tiles, *sources)


def serve_gathered(codes, gathered):
    slots = codes.shape[0] * PER_COLUMN
    _, rows, tile = gathered.shape
    return pl.pallas_call(
        take,
        out_shape=jax.ShapeDtypeStruct((slots, rows, tile), gathered.dtype),
        in_specs=[SMEM, VMEM],
        out_specs=VMEM,
        compiler_params=pltpu.CompilerParams(vmem_limit_bytes=BIG),
        cost_estimate=pl.CostEstimate(
            flops=0, bytes_accessed=4 * slots * rows * tile, transcendentals=0
        ),
        name="serve_gathered",
    )(codes, gathered)


def from_others(mine):
    n = lax.axis_size("pair")
    return [
        lax.ppermute(mine, "pair", [((i + step) % n, i) for i in range(n)])
        for step in range(1, n)
    ]


def mix_kernel(amp_ref, after_ref, mixed_ref):
    amp = amp_ref[0]
    mixed_ref[0] = (
        2.0 * amp.astype(jnp.float32) - jnp.transpose(amp).astype(jnp.float32)
    ).astype(mixed_ref.dtype)


def mix(amplitudes, after):
    pairs, width, _ = amplitudes.shape
    spec = pl.BlockSpec((1, width, width), lambda p: (p, 0, 0))
    return pl.pallas_call(
        mix_kernel,
        grid=(pairs,),
        out_shape=jax.ShapeDtypeStruct(amplitudes.shape, amplitudes.dtype),
        in_specs=[spec, ANY],
        out_specs=spec,
        cost_estimate=pl.CostEstimate(
            flops=pairs * width * width, bytes_accessed=4 * pairs * width * width, transcendentals=0
        ),
        compiler_params=pltpu.CompilerParams(vmem_limit_bytes=BIG),
        name="mix_amplitudes",
    )(amplitudes, after)


def residual_kernel(
    rows_first, tile, place_ref, occ_ref, domain_ref, eps_occ_ref, eps_vir_ref,
    mixed_ref, first_ref, second_ref, out_ref, block, sem,
):
    pair = pl.program_id(0)
    pairs = pl.num_programs(0)
    width = out_ref.shape[2]
    count = width // tile

    def fetch(which):
        slot = which % 2

        def step(k, carry):
            row = pl.multiple_of((k // count) * tile, tile)
            column = pl.ds(pl.multiple_of((k % count) * tile, tile), tile)
            place = place_ref[which * count * count + k]
            pltpu.make_async_copy(
                first_ref.at[place], block.at[slot, pl.ds(row, rows_first), column], sem.at[slot]
            ).start()
            pltpu.make_async_copy(
                second_ref.at[place],
                block.at[slot, pl.ds(row + rows_first, tile - rows_first), column],
                sem.at[slot],
            ).start()
            return carry

        lax.fori_loop(0, count * count, step, 0)

    @pl.when(pair == 0)
    def _():
        fetch(0)

    @pl.when(pair + 1 < pairs)
    def _():
        fetch(pair + 1)

    now = pair % 2
    pltpu.make_async_copy(block.at[now], block.at[now], sem.at[now]).wait()

    occ = eps_occ_ref[occ_ref[2 * pair]] + eps_occ_ref[occ_ref[2 * pair + 1]]
    energies = [
        eps_vir_ref[pl.ds(domain_ref[count * pair + c], 1), :] for c in range(count)
    ]
    across = jnp.concatenate(energies, axis=1)
    for c in range(0, count, 2):
        part = pl.ds(c * tile, 2 * tile)
        down = jnp.transpose(
            jnp.broadcast_to(jnp.concatenate(energies[c : c + 2], axis=1), (8, 2 * tile))
        )[:, :1]
        total = jnp.dot(
            mixed_ref[0, part, :], block[now], preferred_element_type=jnp.float32
        )
        total = total + lax.dot_general(
            block[now, :, part],
            mixed_ref[0],
            (((0,), (0,)), ((), ())),
            preferred_element_type=jnp.float32,
        )
        out_ref[0, part, :] = total / (occ - down - across)


def residual(places, pair_occ, domain, eps_occ, eps_vir, mixed, first, second):
    pairs, width, _ = mixed.shape
    rows_first, tile = first.shape[1], first.shape[2]
    return pl.pallas_call(
        functools.partial(residual_kernel, rows_first, tile),
        grid=(pairs,),
        out_shape=jax.ShapeDtypeStruct(mixed.shape, jnp.float32),
        in_specs=[
            SMEM,
            SMEM,
            SMEM,
            SMEM,
            pl.BlockSpec(memory_space=pltpu.VMEM),
            pl.BlockSpec((1, width, width), lambda p: (p, 0, 0)),
            ANY,
            ANY,
        ],
        out_specs=pl.BlockSpec((1, width, width), lambda p: (p, 0, 0)),
        scratch_shapes=[
            pltpu.VMEM((2, width, width), mixed.dtype),
            pltpu.SemaphoreType.DMA((2,)),
        ],
        cost_estimate=pl.CostEstimate(
            flops=4 * pairs * width**3, bytes_accessed=8 * pairs * width**2, transcendentals=0
        ),
        compiler_params=pltpu.CompilerParams(vmem_limit_bytes=BIG),
        name="residual",
    )(places, pair_occ, domain, eps_occ, eps_vir, mixed, first, second)


def body(amplitudes, integral_tiles, need_owner, need_slot, pair_occ, domain, eps_occ, eps_vir):
    held, tile, _ = integral_tiles.shape
    vir = lax.axis_size("vir")
    here = lax.axis_index("pair").astype(jnp.int32).reshape(1)
    near = from_others(integral_tiles[:, :ROWS_FIRST])
    gathered = lax.all_gather(integral_tiles[:, ROWS_FIRST:], "pair", axis=0, tiled=True)
    requests, places = ask(need_owner.reshape(1, -1), need_slot.reshape(1, -1), vir, held)
    codes = lax.all_to_all(
        requests.reshape(vir, 1, PER_COLUMN), "vir", split_axis=0, concat_axis=0, tiled=True
    )

    served = serve(here, codes, integral_tiles, near, 0, ROWS_FIRST)
    mixed = mix(amplitudes, served)
    got_first = lax.all_to_all(served, "vir", split_axis=0, concat_axis=0, tiled=True)
    served = serve_gathered(codes, gathered)
    got_second = lax.all_to_all(served, "vir", split_axis=0, concat_axis=0, tiled=True)
    return residual(
        places.reshape(-1),
        pair_occ.reshape(-1),
        domain.reshape(-1),
        eps_occ,
        eps_vir.reshape(-1, tile),
        mixed,
        got_first,
        got_second,
    )


def solution(mesh):
    split_both = ("pair", "vir")
    return jax.shard_map(
        body,
        mesh=mesh,
        in_specs=(
            P(split_both, None, None),
            P(split_both, None, None),
            P(split_both, None),
            P(split_both, None),
            P(split_both, None),
            P(split_both, None),
            P(),
            P(),
        ),
        out_specs=P(split_both, None, None),
        check_vma=False,
    )
```

time: 243 us -> 226 us (0.930)
  Pallas kernels: 44.5 us -> 27.1 us
  starting transfers between devices: 49 us -> 35.4 us
  between operations: 0.31 us -> 13.5 us
    ppermute x12 -> x3, waiting for transfers between devices: 43 us -> 0.01 us  [from_others(): lax.ppermute(mine, 'pair', [((i + step) % n, i) for i in range(n)])]
    all_to_all x2, waiting for transfers between devices: 102 us -> 119 us  [body(): lax.all_to_all(served, 'vir', split_axis=0, concat_axis=0, tiled=True)]
    pallas_call x5 -> x3, Pallas kernels: 27.5 us -> 10.1 us  [the longest x1 4.93 us: serve_gathered(): pl.pallas_call(take, out_shape=jax.ShapeDtypeStruct((slots, rows, tile),...]
    all_gather x0 -> x1, waiting for transfers between devices: none -> 17.3 us  [body(): lax.all_gather(integral_tiles[:, ROWS_FIRST:], 'pair', axis=0, tiled=True)]
    all_to_all x1, waiting for transfers between devices: 0.01 us -> 9.28 us  [body(): lax.all_to_all(requests.reshape(vir, 1, PER_COLUMN), 'vir', split_axis=0,...]
    ppermute x12 -> x3, starting transfers between devices: 14.2 us -> 5.72 us  [from_others(): lax.ppermute(mine, 'pair', [((i + step) % n, i) for i in range(n)])]
    all_to_all x2, starting transfers between devices: 21.7 us -> 16.5 us  [body(): lax.all_to_all(served, 'vir', split_axis=0, concat_axis=0, tiled=True)]
    slice x0 -> x2, local copies, waits for them, and re-layouts: none -> 3.4 us  [the longest x1 2.36 us: body(): integral_tiles[:, ROWS_FIRST:]]
  transfers between devices with their start and end apart: 15 -> 7, of which waited for: 8 -> 4; matrix products, arithmetic and copies ran while one was open for 0% -> 1% of each run, Pallas kernels for 8% -> 7%
where the time goes in v3:
time: 226 us; the launch traced here: 225 us
  waiting for transfers between devices  146 us (65%)
  starting transfers between devices  35.4 us (16%)
  Pallas kernels  27.1 us (12%)
  between operations  13.5 us (6%)
  local copies, waits for them, and re-layouts  3.67 us (2%)
    all_to_all x2, waiting for transfers between devices, body(): lax.all_to_all(served, 'vir', split_axis=0, concat_axis=0, tiled=True)  119 us
    all_gather x1, waiting for transfers between devices, body(): lax.all_gather(integral_tiles[:, ROWS_FIRST:], 'pair', axis=0, tiled=True)  17.3 us
    all_to_all x2, starting transfers between devices, body(): lax.all_to_all(served, 'vir', split_axis=0, concat_axis=0, tiled=True)  16.5 us
    all_to_all x1, starting transfers between devices, body(): lax.all_to_all(requests.reshape(vir, 1, PER_COLUMN), 'vir', split_axis=0,...  13.2 us
    pallas_call x1, Pallas kernels, residual(): pl.pallas_call(functools.partial(residual_kernel, rows_first, tile), grid...  11.7 us
    all_to_all x1, waiting for transfers between devices, body(): lax.all_to_all(requests.reshape(vir, 1, PER_COLUMN), 'vir', split_axis=0,...  9.28 us
    ppermute x3, starting transfers between devices, from_others(): lax.ppermute(mine, 'pair', [((i + step) % n, i) for i in range(n)])  5.72 us
    pallas_call x1, Pallas kernels, mix(): pl.pallas_call(mix_kernel, grid=(pairs,), out_shape=jax.ShapeDtypeStruct(...  5.32 us
  transfers between devices with their start and end apart: 7, of which 4 were waited for; matrix products, arithmetic and copies ran while one was open for 1% of the time, Pallas kernels for 7%

profile of v3, /device:TPU:1, one launch (start us, length us, event | category | flops | bytes accessed | tf_op | source)
XLA Modules:
  0.0 225.3 jit_solution(17691290194827496798)
XLA Ops:
  6.5 2.4 %slice.7 = bf16[48,96,128]{2,1,0:T(8,128)(2,1)} slice(bf16[48,128,128]{2,1,0:T(8,128)(2,1)} %own_ref.1), slice={[0:48], [32:128], [0:128]} | slice | bytes 2359296 | tf_op jit(solution)/shard_map/slice | solution.py:244
  8.9 0.0 all-gather.2.cloned.1.call-update
  8.9 1.0 slice.6
  10.0 2.1 collective-permute-start.2
  12.1 2.5 %collective-permute-start.1 = (bf16[48,32,128]{2,1,0:T(8,128)(2,1)S(1)}, bf16[48,32,128]{2,1,0:T(8,128)(2,1)S(1)}, u32[]{:S(2)}, u32[]{:S(2)}) collective-permute-start(bf16[48,32,128]{2,1,0:T(8,128)(2,1)S(1)} %slice.6), channel_id=1, source_target_pairs={{128,0},{192,64},{0,128},{64,192},{129,1},{193,65},{1,129},{65,193... | collective-permute-start | bytes 1179656 | tf_op jit(solution)/shard_map/ppermute | solution.py:119
  14.5 1.2 collective-permute-start
  15.7 1.5 make_requests.1
  17.2 13.2 %all-to-all-start = ((s32[64,1,3]{2,1,0:T(1,128)}), s32[64,1,3]{2,1,0:T(1,128)S(1)}, u32[]{:S(2)}, u32[]{:S(2)}) async-start(s32[64,1,3]{2,1,0:T(1,128)} %bitcast.8), calls=%async_computation | async-start | bytes 65536 | tf_op jit(solution)/shard_map/all_to_all | solution.py:246
  30.4 9.3 %all-to-all-done.code_ref = s32[64,1,3]{2,1,0:T(1,128)S(1)} async-done(((s32[64,1,3]{2,1,0:T(1,128)}), s32[64,1,3]{2,1,0:T(1,128)S(1)}, u32[]{:S(2)}, u32[]{:S(2)}) %all-to-all-start) | async-done | bytes 800 | tf_op jit(solution)/shard_map/all_to_all | solution.py:246
  39.7 0.0 collective-permute-done.2.refs_2_
  39.7 0.0 collective-permute-done.1.refs_1_
  39.7 0.0 collective-permute-done.refs_0_
  39.7 3.6 %serve_near.1.after_ref = bf16[192,32,128]{2,1,0:T(8,128)(2,1)} custom-call(s32[1]{0:T(128)} %bitcast.4.here_ref, s32[64,1,3]{2,1,0:T(1,128)S(1)} %all-to-all-done.code_ref, bf16[48,128,128]{2,1,0:T(8,128)(2,1)} %own_ref.1, bf16[48,32,128]{2,1,0:T(8,128)(2,1)S(1)} %collective-permute-done.refs_0_, bf16[48,32,128]{2,1,0:T(8,128)(2,1)S(1)} %collective-permute-done.1.refs_1_, ...), custom_call_target="tpu_custom_call" | custom-call | bytes 3145728 | tf_op jit(solution)/shard_map/serve_near/pallas_call | solution.py:83
  43.3 10.3 %all-to-all-start.1 = ((bf16[192,32,128]{2,1,0:T(8,128)(2,1)}), bf16[192,32,128]{2,1,0:T(8,128)(2,1)S(1)}, u32[]{:S(2)}, u32[]{:S(2)}) async-start(bf16[192,32,128]{2,1,0:T(8,128)(2,1)} %serve_near.1.after_ref), calls=%async_computation.1 | async-start | bytes 3145728 | tf_op jit(solution)/shard_map/all_to_all | solution.py:252
  53.6 17.3 %all-gather.2.cloned.1.call-done.pool = bf16[192,96,128]{2,1,0:T(8,128)(2,1)} async-done(((bf16[48,96,128]{2,1,0:T(8,128)(2,1)}), bf16[192,96,128]{2,1,0:T(8,128)(2,1)}) %all-gather.2.cloned.1.call-update) | async-done | bytes 4718608 | tf_op jit(solution)/shard_map/all_gather | solution.py:244
  70.9 4.9 %serve_gathered.1 = bf16[192,96,128]{2,1,0:T(8,128)(2,1)} custom-call(s32[64,1,3]{2,1,0:T(1,128)S(1)} %all-to-all-done.code_ref, bf16[192,96,128]{2,1,0:T(8,128)(2,1)} %all-gather.2.cloned.1.call-done.pool), custom_call_target="tpu_custom_call" | custom-call | bytes 9437184 | tf_op jit(solution)/shard_map/serve_gathered/pallas_call | solution.py:103
  75.8 17.5 %all-to-all-done.1.first_ref = bf16[192,32,128]{2,1,0:T(8,128)(2,1)S(1)} async-done(((bf16[192,32,128]{2,1,0:T(8,128)(2,1)}), bf16[192,32,128]{2,1,0:T(8,128)(2,1)S(1)}, u32[]{:S(2)}, u32[]{:S(2)}) %all-to-all-start.1) | async-done | bytes 1572896 | tf_op jit(solution)/shard_map/all_to_all | solution.py:252
  93.3 6.3 %all-to-all-start.2 = ((bf16[192,96,128]{2,1,0:T(8,128)(2,1)}), bf16[192,96,128]{2,1,0:T(8,128)(2,1)}, u32[]{:S(2)}, u32[]{:S(2)}) async-start(bf16[192,96,128]{2,1,0:T(8,128)(2,1)} %serve_gathered.1), calls=%async_computation.2 | async-start | bytes 9437184 | tf_op jit(solution)/shard_map/all_to_all | solution.py:254
  99.7 0.1 reshape.28.domain_ref
  99.7 0.1 copy.11
  99.8 0.1 reshape.27.occ_ref
  99.9 5.3 %mix_amplitudes.1.mixed_ref = bf16[3,768,768]{2,1,0:T(8,128)(2,1)} custom-call(bf16[3,768,768]{2,1,0:T(8,128)(2,1)} %amp_ref.1, bf16[192,32,128]{2,1,0:T(8,128)(2,1)} %serve_near.1.after_ref), custom_call_target="tpu_custom_call" | custom-call | flops 1769472 | bytes 7077888 | tf_op jit(solution)/shard_map/mix_amplitudes/pallas_call | solution.py:134
  105.2 101.5 %all-to-all-done.2.second_ref = bf16[192,96,128]{2,1,0:T(8,128)(2,1)} async-done(((bf16[192,96,128]{2,1,0:T(8,128)(2,1)}), bf16[192,96,128]{2,1,0:T(8,128)(2,1)}, u32[]{:S(2)}, u32[]{:S(2)}) %all-to-all-start.2) | async-done | bytes 4718624 | tf_op jit(solution)/shard_map/all_to_all | solution.py:254
  206.8 11.7 %residual.1 = f32[3,768,768]{2,1,0:T(8,128)} custom-call(s32[108]{0:T(128)S(1)} %bitcast.7, s32[6]{0:T(128)S(1)} %reshape.27.occ_ref, s32[18]{0:T(128)S(1)} %reshape.28.domain_ref, f32[400]{0:T(512)S(1)} %copy-done.1, f32[25,128]{1,0:T(8,128)S(1)} %bitcast.6, bf16[3,768,768]{2,1,0:T(8,128)(2,1)} %mix_amplitudes.1.mixed_ref, ...), custom_call_target="tpu_custom_call" | custom-call | flops 5435817984 | bytes 14155776 | tf_op jit(solution)/shard_map/residual/pallas_call | solution.py:212
  (11 shorter events, 0.0 us)
Async XLA Ops:
  6.5 64.3 %all-gather.2.cloned.1.call-start = ((), (), s32[]{:S(2)}) async-start(), calls=%async_computation.3 | async-start | bytes 5898240 | tf_op jit(solution)/shard_map/all_gather | solution.py:244
  10.0 29.7 %collective-permute-start.2 = (bf16[48,32,128]{2,1,0:T(8,128)(2,1)S(1)}, bf16[48,32,128]{2,1,0:T(8,128)(2,1)S(1)}, u32[]{:S(2)}, u32[]{:S(2)}) collective-permute-start(bf16[48,32,128]{2,1,0:T(8,128)(2,1)S(1)} %slice.6), channel_id=1, source_target_pairs={{192,0},{0,64},{64,128},{128,192},{193,1},{1,65},{65,129},{129,193... | collective-permute-start | bytes 1179656 | tf_op jit(solution)/shard_map/ppermute | solution.py:119
  12.1 27.6 %collective-permute-start.1 = (bf16[48,32,128]{2,1,0:T(8,128)(2,1)S(1)}, bf16[48,32,128]{2,1,0:T(8,128)(2,1)S(1)}, u32[]{:S(2)}, u32[]{:S(2)}) collective-permute-start(bf16[48,32,128]{2,1,0:T(8,128)(2,1)S(1)} %slice.6), channel_id=1, source_target_pairs={{128,0},{192,64},{0,128},{64,192},{129,1},{193,65},{1,129},{65,193... | collective-permute-start | bytes 1179656 | tf_op jit(solution)/shard_map/ppermute | solution.py:119
  14.5 25.2 %collective-permute-start = (bf16[48,32,128]{2,1,0:T(8,128)(2,1)S(1)}, bf16[48,32,128]{2,1,0:T(8,128)(2,1)S(1)}, u32[]{:S(2)}, u32[]{:S(2)}) collective-permute-start(bf16[48,32,128]{2,1,0:T(8,128)(2,1)S(1)} %slice.6), channel_id=1, source_target_pairs={{64,0},{128,64},{192,128},{0,192},{65,1},{129,65},{193,129},{1,193... | collective-permute-start | bytes 1179656 | tf_op jit(solution)/shard_map/ppermute | solution.py:119
  17.2 22.5 %all-to-all-start = ((s32[64,1,3]{2,1,0:T(1,128)}), s32[64,1,3]{2,1,0:T(1,128)S(1)}, u32[]{:S(2)}, u32[]{:S(2)}) async-start(s32[64,1,3]{2,1,0:T(1,128)} %bitcast.8), calls=%async_computation | async-start | bytes 65536 | tf_op jit(solution)/shard_map/all_to_all | solution.py:246
  43.3 50.1 %all-to-all-start.1 = ((bf16[192,32,128]{2,1,0:T(8,128)(2,1)}), bf16[192,32,128]{2,1,0:T(8,128)(2,1)S(1)}, u32[]{:S(2)}, u32[]{:S(2)}) async-start(bf16[192,32,128]{2,1,0:T(8,128)(2,1)} %serve_near.1.after_ref), calls=%async_computation.1 | async-start | bytes 3145728 | tf_op jit(solution)/shard_map/all_to_all | solution.py:252
  75.8 23.8 %copy-start.3 = (s32[3,6]{1,0:T(4,128)S(1)}, s32[3,6]{1,0:T(4,128)}, u32[]{:S(2)}) copy-start(s32[3,6]{1,0:T(4,128)} %param.13) | copy-start | bytes 220
  75.8 23.9 %copy-start.4 = (s32[3,2]{0,1:T(2,128)S(1)}, s32[3,2]{0,1:T(2,128)}, u32[]{:S(2)}) copy-start(s32[3,2]{0,1:T(2,128)} %param.12) | copy-start | bytes 76
  93.3 113.4 %all-to-all-start.2 = ((bf16[192,96,128]{2,1,0:T(8,128)(2,1)}), bf16[192,96,128]{2,1,0:T(8,128)(2,1)}, u32[]{:S(2)}, u32[]{:S(2)}) async-start(bf16[192,96,128]{2,1,0:T(8,128)(2,1)} %serve_gathered.1), calls=%async_computation.2 | async-start | bytes 9437184 | tf_op jit(solution)/shard_map/all_to_all | solution.py:254
  99.9 106.9 %copy-start = (f32[3200]{0:T(1024)S(1)}, f32[3200]{0:T(1024)}, u32[]{:S(2)}) copy-start(f32[3200]{0:T(1024)} %param.15) | copy-start | bytes 38404
  99.9 106.9 %copy-start.1 = (f32[400]{0:T(512)S(1)}, f32[400]{0:T(512)}, u32[]{:S(2)}) copy-start(f32[400]{0:T(512)} %eps_occ_ref.1) | copy-start | bytes 4804
  99.9 106.9 %copy-start.2 = (s32[1,108]{1,0:T(1,128)S(1)}, s32[1,108]{1,0:T(1,128)}, u32[]{:S(2)}) copy-start(s32[1,108]{1,0:T(1,128)} %get-tuple-element.7) | copy-start | bytes 1300
Sparse Core Ops, SparseCore 0:
  9.2 61.6 all-gather.1

commit v4 on v3

--- a/solution.py
+++ b/solution.py
@@ -7,7 +7,7 @@
 from jax.experimental.pallas import tpu as pltpu
 from jax.sharding import PartitionSpec as P
 
-ROWS_FIRST = 32
+ROWS_FIRST = 48
 PER_COLUMN = 3
 ANY = pl.BlockSpec(memory_space=pl.ANY)
 VMEM = pl.BlockSpec(memory_space=pltpu.VMEM)
@@ -51,15 +51,14 @@
     )(owner, slot)
 
 
-def serve_kernel(n_pair, row_from, here_ref, code_ref, own_ref, *refs):
-    sources, (out_ref, pool, sem) = refs[: n_pair - 1], refs[n_pair - 1 :]
-    held, rows = own_ref.shape[0], out_ref.shape[1]
+def serve_kernel(n_pair, here_ref, code_ref, *refs):
+    sources, (out_ref, pool, sem) = refs[:n_pair], refs[n_pair:]
+    held = sources[0].shape[0]
     copies = []
     for step in range(n_pair):
         owner = (here_ref[0] + step) % n_pair
-        source = sources[step - 1] if step else own_ref.at[:, pl.ds(row_from, rows)]
         target = pool.at[pl.ds(owner * held, held)]
-        copies.append(pltpu.make_async_copy(source, target, sem.at[step]))
+        copies.append(pltpu.make_async_copy(sources[step], target, sem.at[step]))
     for copy in copies:
         copy.start()
     for copy in copies:
@@ -76,46 +75,55 @@
     lax.fori_loop(0, code_ref.shape[0], step, 0, unroll=4)
 
 
-def serve(here, codes, tiles, sources, row_from, rows):
+def serve(here, codes, sources):
     slots = codes.shape[0] * PER_COLUMN
-    n_pair = len(sources) + 1
-    held, tile = tiles.shape[0], tiles.shape[2]
-    return pl.pallas_call(
-        functools.partial(serve_kernel, n_pair, row_from),
-        out_shape=jax.ShapeDtypeStruct((slots, rows, tile), tiles.dtype),
+    n_pair = len(sources)
+    held, rows, tile = sources[0].shape
+    dtype = sources[0].dtype
+    return pl.pallas_call(
+        functools.partial(serve_kernel, n_pair),
+        out_shape=jax.ShapeDtypeStruct((slots, rows, tile), dtype),
         in_specs=[SMEM, SMEM] + [ANY] * n_pair,
         out_specs=VMEM,
         scratch_shapes=[
-            pltpu.VMEM((n_pair * held, rows, tile), tiles.dtype),
+            pltpu.VMEM((n_pair * held, rows, tile), dtype),
             pltpu.SemaphoreType.DMA((n_pair,)),
         ],
         compiler_params=pltpu.CompilerParams(vmem_limit_bytes=BIG),
         cost_estimate=pl.CostEstimate(
             flops=0, bytes_accessed=4 * slots * rows * tile, transcendentals=0
         ),
-        name="serve_near",
-    )(here, codes, tiles, *sources)
-
-
-def serve_gathered(codes, gathered):
-    slots = codes.shape[0] * PER_COLUMN
-    _, rows, tile = gathered.shape
-    return pl.pallas_call(
-        take,
-        out_shape=jax.ShapeDtypeStruct((slots, rows, tile), gathered.dtype),
-        in_specs=[SMEM, VMEM],
+        name="serve_tiles",
+    )(here, codes, *sources)
+
+
+def cut_kernel(row_from, tiles_ref, after_ref, out_ref, sem):
+    copy = pltpu.make_async_copy(
+        tiles_ref.at[:, pl.ds(row_from, out_ref.shape[1])], out_ref, sem
+    )
+    copy.start()
+    copy.wait()
+
+
+def cut(tiles, after, row_from, rows):
+    held, _, tile = tiles.shape
+    return pl.pallas_call(
+        functools.partial(cut_kernel, row_from),
+        out_shape=jax.ShapeDtypeStruct((held, rows, tile), tiles.dtype),
+        in_specs=[ANY, ANY],
         out_specs=VMEM,
-        compiler_params=pltpu.CompilerParams(vmem_limit_bytes=BIG),
-        cost_estimate=pl.CostEstimate(
-            flops=0, bytes_accessed=4 * slots * rows * tile, transcendentals=0
-        ),
-        name="serve_gathered",
-    )(codes, gathered)
+        scratch_shapes=[pltpu.SemaphoreType.DMA],
+        compiler_params=pltpu.CompilerParams(vmem_limit_bytes=BIG),
+        cost_estimate=pl.CostEstimate(
+            flops=0, bytes_accessed=4 * held * rows * tile, transcendentals=0
+        ),
+        name="cut_rows",
+    )(tiles, after)
 
 
 def from_others(mine):
     n = lax.axis_size("pair")
-    return [
+    return [mine] + [
         lax.ppermute(mine, "pair", [((i + step) % n, i) for i in range(n)])
         for step in range(1, n)
     ]
@@ -241,16 +249,17 @@
     vir = lax.axis_size("vir")
     here = lax.axis_index("pair").astype(jnp.int32).reshape(1)
     near = from_others(integral_tiles[:, :ROWS_FIRST])
-    gathered = lax.all_gather(integral_tiles[:, ROWS_FIRST:], "pair", axis=0, tiled=True)
+    rest = tile - ROWS_FIRST
+    far = from_others(cut(integral_tiles, near[1], ROWS_FIRST, rest))
     requests, places = ask(need_owner.reshape(1, -1), need_slot.reshape(1, -1), vir, held)
     codes = lax.all_to_all(
         requests.reshape(vir, 1, PER_COLUMN), "vir", split_axis=0, concat_axis=0, tiled=True
     )
 
-    served = serve(here, codes, integral_tiles, near, 0, ROWS_FIRST)
-    mixed = mix(amplitudes, served)
+    served = serve(here, codes, near)
+    mixed = mix(amplitudes, codes)
     got_first = lax.all_to_all(served, "vir", split_axis=0, concat_axis=0, tiled=True)
-    served = serve_gathered(codes, gathered)
+    served = serve(here, codes, far)
     got_second = lax.all_to_all(served, "vir", split_axis=0, concat_axis=0, tiled=True)
     return residual(
         places.reshape(-1),

time: 226 us -> 213 us (0.942)
  between operations: 13.5 us -> 0.13 us
  starting transfers between devices: 35.4 us -> 43.1 us
  waiting for transfers between devices: 146 us -> 142 us
  Pallas kernels: 27.1 us -> 24.3 us
    ppermute x3 -> x6, waiting for transfers between devices: 0.01 us -> 41.5 us  [from_others(): lax.ppermute(mine, 'pair', [((i + step) % n, i) for i in range(n)])]
    all_to_all x2, waiting for transfers between devices: 119 us -> 90.9 us  [body(): lax.all_to_all(served, 'vir', split_axis=0, concat_axis=0, tiled=True)]
    all_gather x1 -> x0, waiting for transfers between devices: 17.3 us -> none  [body(): lax.all_gather(integral_tiles[:, ROWS_FIRST:], 'pair', axis=0, tiled=True)]
    ppermute x3 -> x6, starting transfers between devices: 5.72 us -> 10.2 us  [from_others(): lax.ppermute(mine, 'pair', [((i + step) % n, i) for i in range(n)])]
    all_to_all x2, starting transfers between devices: 16.5 us -> 19.7 us  [body(): lax.all_to_all(served, 'vir', split_axis=0, concat_axis=0, tiled=True)]
    slice x1 -> x0, local copies, waits for them, and re-layouts: 2.36 us -> none  [body(): integral_tiles[:, ROWS_FIRST:]]
    pallas_call x2 -> x3, Pallas kernels: 8.51 us -> 8.04 us  [the longest x2 7.94 us: serve(): pl.pallas_call(functools.partial(serve_kernel, n_pair), out_shape=jax.Sha...]
  transfers between devices with their start and end apart: 7 -> 9, of which waited for: 4 -> 6; matrix products, arithmetic and copies ran while one was open for 1% -> 0% of each run, Pallas kernels for 7% -> 5%
where the time goes in v4:
time: 213 us; the launch traced here: 212 us
  waiting for transfers between devices  142 us (67%)
  starting transfers between devices  43.1 us (20%)
  Pallas kernels  24.3 us (11%)
  local copies, waits for them, and re-layouts  3.17 us (1%)
    all_to_all x2, waiting for transfers between devices, body(): lax.all_to_all(served, 'vir', split_axis=0, concat_axis=0, tiled=True)  90.9 us
    ppermute x6, waiting for transfers between devices, from_others(): lax.ppermute(mine, 'pair', [((i + step) % n, i) for i in range(n)])  41.5 us
    all_to_all x2, starting transfers between devices, body(): lax.all_to_all(served, 'vir', split_axis=0, concat_axis=0, tiled=True)  19.7 us
    all_to_all x1, starting transfers between devices, body(): lax.all_to_all(requests.reshape(vir, 1, PER_COLUMN), 'vir', split_axis=0,...  13.2 us
    pallas_call x1, Pallas kernels, residual(): pl.pallas_call(functools.partial(residual_kernel, rows_first, tile), grid...  11.3 us
    ppermute x6, starting transfers between devices, from_others(): lax.ppermute(mine, 'pair', [((i + step) % n, i) for i in range(n)])  10.2 us
    all_to_all x1, waiting for transfers between devices, body(): lax.all_to_all(requests.reshape(vir, 1, PER_COLUMN), 'vir', split_axis=0,...  9.21 us
    pallas_call x2, Pallas kernels, serve(): pl.pallas_call(functools.partial(serve_kernel, n_pair), out_shape=jax.Sha...  7.94 us
  transfers between devices with their start and end apart: 9, of which 6 were waited for; matrix products, arithmetic and copies ran while one was open for 0% of the time, Pallas kernels for 5%

profile of v4, /device:TPU:1, one launch (start us, length us, event | category | flops | bytes accessed | tf_op | source)
XLA Modules:
  0.0 212.3 jit_solution(14201743312559435843)
XLA Ops:
  0.0 1.1 slice.3.refs_0_
  1.1 2.1 collective-permute-start.2
  3.2 2.5 %collective-permute-start.1 = (bf16[48,48,128]{2,1,0:T(8,128)(2,1)S(1)}, bf16[48,48,128]{2,1,0:T(8,128)(2,1)S(1)}, u32[]{:S(2)}, u32[]{:S(2)}) collective-permute-start(bf16[48,48,128]{2,1,0:T(8,128)(2,1)S(1)} %slice.3.refs_0_), channel_id=1, source_target_pairs={{128,0},{192,64},{0,128},{64,192},{129,1},{193,65},{1,129},{65,193... | collective-permute-start | bytes 1769480 | tf_op jit(solution)/shard_map/ppermute | solution.py:127
  5.7 1.2 collective-permute-start
  6.8 1.6 make_requests.1
  8.4 13.2 %all-to-all-start = ((s32[64,1,3]{2,1,0:T(1,128)}), s32[64,1,3]{2,1,0:T(1,128)S(1)}, u32[]{:S(2)}, u32[]{:S(2)}) async-start(s32[64,1,3]{2,1,0:T(1,128)} %bitcast.8), calls=%async_computation | async-start | bytes 65536 | tf_op jit(solution)/shard_map/all_to_all | solution.py:255
  21.6 9.2 %all-to-all-done.after_ref.code_ref = s32[64,1,3]{2,1,0:T(1,128)S(1)} async-done(((s32[64,1,3]{2,1,0:T(1,128)}), s32[64,1,3]{2,1,0:T(1,128)S(1)}, u32[]{:S(2)}, u32[]{:S(2)}) %all-to-all-start) | async-done | bytes 800 | tf_op jit(solution)/shard_map/all_to_all | solution.py:255
  30.8 0.3 collective-permute-done.1.refs_2_
  31.1 3.3 %serve_tiles.2 = bf16[192,48,128]{2,1,0:T(8,128)(2,1)} custom-call(s32[1]{0:T(128)} %bitcast.5.here_ref, s32[64,1,3]{2,1,0:T(1,128)S(1)} %all-to-all-done.after_ref.code_ref, bf16[48,48,128]{2,1,0:T(8,128)(2,1)S(1)} %slice.3.refs_0_, bf16[48,48,128]{2,1,0:T(8,128)(2,1)S(1)} %collective-permute-done.refs_1_.after_ref, ...), custom_call_target="tpu_custom_call" | custom-call | bytes 4718592 | tf_op jit(solution)/shard_map/serve_tiles/pallas_call | solution.py:83
  34.4 13.5 %all-to-all-start.1 = ((bf16[192,48,128]{2,1,0:T(8,128)(2,1)}), bf16[192,48,128]{2,1,0:T(8,128)(2,1)}, u32[]{:S(2)}, u32[]{:S(2)}) async-start(bf16[192,48,128]{2,1,0:T(8,128)(2,1)} %serve_tiles.2), calls=%async_computation.1 | async-start | bytes 4718592 | tf_op jit(solution)/shard_map/all_to_all | solution.py:261
  47.9 0.1 cut_rows.1.refs_0_
  48.0 1.1 collective-permute-start.5
  49.2 2.1 collective-permute-start.4
  51.3 1.3 collective-permute-start.3
  52.6 19.7 %collective-permute-done.5.refs_3_ = bf16[48,80,128]{2,1,0:T(8,128)(2,1)S(1)} collective-permute-done((bf16[48,80,128]{2,1,0:T(8,128)(2,1)S(1)}, bf16[48,80,128]{2,1,0:T(8,128)(2,1)S(1)}, u32[]{:S(2)}, u32[]{:S(2)}) %collective-permute-start.5) | collective-permute-done | bytes 983072 | tf_op jit(solution)/shard_map/ppermute | solution.py:127
  72.2 21.6 %collective-permute-done.4.refs_2_ = bf16[48,80,128]{2,1,0:T(8,128)(2,1)S(1)} collective-permute-done((bf16[48,80,128]{2,1,0:T(8,128)(2,1)S(1)}, bf16[48,80,128]{2,1,0:T(8,128)(2,1)S(1)}, u32[]{:S(2)}, u32[]{:S(2)}) %collective-permute-start.4) | collective-permute-done | bytes 983072 | tf_op jit(solution)/shard_map/ppermute | solution.py:127
  93.8 4.6 %serve_tiles.3 = bf16[192,80,128]{2,1,0:T(8,128)(2,1)} custom-call(s32[1]{0:T(128)} %bitcast.5.here_ref, s32[64,1,3]{2,1,0:T(1,128)S(1)} %all-to-all-done.after_ref.code_ref, bf16[48,80,128]{2,1,0:T(8,128)(2,1)S(1)} %cut_rows.1.refs_0_, bf16[48,80,128]{2,1,0:T(8,128)(2,1)S(1)} %collective-permute-done.3.refs_1_, ...), custom_call_target="tpu_custom_call" | custom-call | bytes 7864320 | tf_op jit(solution)/shard_map/serve_tiles/pallas_call | solution.py:83
  98.4 6.1 %all-to-all-done.1.first_ref = bf16[192,48,128]{2,1,0:T(8,128)(2,1)} async-done(((bf16[192,48,128]{2,1,0:T(8,128)(2,1)}), bf16[192,48,128]{2,1,0:T(8,128)(2,1)}, u32[]{:S(2)}, u32[]{:S(2)}) %all-to-all-start.1) | async-done | bytes 2359328 | tf_op jit(solution)/shard_map/all_to_all | solution.py:261
  104.5 6.2 %all-to-all-start.2 = ((bf16[192,80,128]{2,1,0:T(8,128)(2,1)}), bf16[192,80,128]{2,1,0:T(8,128)(2,1)}, u32[]{:S(2)}, u32[]{:S(2)}) async-start(bf16[192,80,128]{2,1,0:T(8,128)(2,1)} %serve_tiles.3), calls=%async_computation.2 | async-start | bytes 7864320 | tf_op jit(solution)/shard_map/all_to_all | solution.py:263
  110.7 0.1 copy.10
  110.9 3.4 %mix_amplitudes.1.mixed_ref = bf16[3,768,768]{2,1,0:T(8,128)(2,1)S(1)} custom-call(bf16[3,768,768]{2,1,0:T(8,128)(2,1)} %amp_ref.1, s32[64,1,3]{2,1,0:T(1,128)S(1)} %all-to-all-done.after_ref.code_ref), custom_call_target="tpu_custom_call" | custom-call | flops 1769472 | bytes 7077888 | tf_op jit(solution)/shard_map/mix_amplitudes/pallas_call | solution.py:142
  114.4 1.8 copy-done
  116.2 84.8 %all-to-all-done.2.second_ref = bf16[192,80,128]{2,1,0:T(8,128)(2,1)} async-done(((bf16[192,80,128]{2,1,0:T(8,128)(2,1)}), bf16[192,80,128]{2,1,0:T(8,128)(2,1)}, u32[]{:S(2)}, u32[]{:S(2)}) %all-to-all-start.2) | async-done | bytes 3932192 | tf_op jit(solution)/shard_map/all_to_all | solution.py:263
  201.0 11.3 %residual.1 = f32[3,768,768]{2,1,0:T(8,128)} custom-call(s32[108]{0:T(128)S(1)} %bitcast.7, s32[6]{0:T(128)S(1)} %reshape.27.occ_ref, s32[18]{0:T(128)S(1)} %reshape.28.domain_ref, f32[400]{0:T(512)S(1)} %copy-done.3, f32[25,128]{1,0:T(8,128)S(1)} %bitcast.6, bf16[3,768,768]{2,1,0:T(8,128)(2,1)} %copy-done, bf16[192,48,128]{2,1,0:T(8,128)(2,1)} %all-to-all-done.1.first_ref, ...), custom_call_target="tpu_custom_call" | custom-call | flops 5435817984 | bytes 14155776 | tf_op jit(solution)/shard_map/residual/pallas_call | solution.py:220
  (18 shorter events, 0.2 us)
Async XLA Ops:
  1.1 29.7 %collective-permute-start.2 = (bf16[48,48,128]{2,1,0:T(8,128)(2,1)S(1)}, bf16[48,48,128]{2,1,0:T(8,128)(2,1)S(1)}, u32[]{:S(2)}, u32[]{:S(2)}) collective-permute-start(bf16[48,48,128]{2,1,0:T(8,128)(2,1)S(1)} %slice.3.refs_0_), channel_id=1, source_target_pairs={{192,0},{0,64},{64,128},{128,192},{193,1},{1,65},{65,129},{129,193... | collective-permute-start | bytes 1769480 | tf_op jit(solution)/shard_map/ppermute | solution.py:127
  3.2 27.8 %collective-permute-start.1 = (bf16[48,48,128]{2,1,0:T(8,128)(2,1)S(1)}, bf16[48,48,128]{2,1,0:T(8,128)(2,1)S(1)}, u32[]{:S(2)}, u32[]{:S(2)}) collective-permute-start(bf16[48,48,128]{2,1,0:T(8,128)(2,1)S(1)} %slice.3.refs_0_), channel_id=1, source_target_pairs={{128,0},{192,64},{0,128},{64,192},{129,1},{193,65},{1,129},{65,193... | collective-permute-start | bytes 1769480 | tf_op jit(solution)/shard_map/ppermute | solution.py:127
  5.7 25.4 %collective-permute-start = (bf16[48,48,128]{2,1,0:T(8,128)(2,1)S(1)}, bf16[48,48,128]{2,1,0:T(8,128)(2,1)S(1)}, u32[]{:S(2)}, u32[]{:S(2)}) collective-permute-start(bf16[48,48,128]{2,1,0:T(8,128)(2,1)S(1)} %slice.3.refs_0_), channel_id=1, source_target_pairs={{64,0},{128,64},{192,128},{0,192},{65,1},{129,65},{193,129},{1,193... | collective-permute-start | bytes 1769480 | tf_op jit(solution)/shard_map/ppermute | solution.py:127
  8.4 22.4 %all-to-all-start = ((s32[64,1,3]{2,1,0:T(1,128)}), s32[64,1,3]{2,1,0:T(1,128)S(1)}, u32[]{:S(2)}, u32[]{:S(2)}) async-start(s32[64,1,3]{2,1,0:T(1,128)} %bitcast.8), calls=%async_computation | async-start | bytes 65536 | tf_op jit(solution)/shard_map/all_to_all | solution.py:255
  34.4 13.5 %copy-start.1 = (bf16[48,128,128]{2,1,0:T(8,128)(2,1)S(1)}, bf16[48,128,128]{2,1,0:T(8,128)(2,1)}, u32[]{:S(2)}) copy-start(bf16[48,128,128]{2,1,0:T(8,128)(2,1)} %tiles_ref.1) | copy-start | bytes 4718596
  34.4 70.1 %all-to-all-start.1 = ((bf16[192,48,128]{2,1,0:T(8,128)(2,1)}), bf16[192,48,128]{2,1,0:T(8,128)(2,1)}, u32[]{:S(2)}, u32[]{:S(2)}) async-start(bf16[192,48,128]{2,1,0:T(8,128)(2,1)} %serve_tiles.2), calls=%async_computation.1 | async-start | bytes 4718592 | tf_op jit(solution)/shard_map/all_to_all | solution.py:261
  48.0 24.2 %collective-permute-start.5 = (bf16[48,80,128]{2,1,0:T(8,128)(2,1)S(1)}, bf16[48,80,128]{2,1,0:T(8,128)(2,1)S(1)}, u32[]{:S(2)}, u32[]{:S(2)}) collective-permute-start(bf16[48,80,128]{2,1,0:T(8,128)(2,1)S(1)} %cut_rows.1.refs_0_), channel_id=1, source_target_pairs={{192,0},{0,64},{64,128},{128,192},{193,1},{1,65},{65,129},{129,193... | collective-permute-start | bytes 2949128 | tf_op jit(solution)/shard_map/ppermute | solution.py:127
  49.2 44.6 %collective-permute-start.4 = (bf16[48,80,128]{2,1,0:T(8,128)(2,1)S(1)}, bf16[48,80,128]{2,1,0:T(8,128)(2,1)S(1)}, u32[]{:S(2)}, u32[]{:S(2)}) collective-permute-start(bf16[48,80,128]{2,1,0:T(8,128)(2,1)S(1)} %cut_rows.1.refs_0_), channel_id=1, source_target_pairs={{128,0},{192,64},{0,128},{64,192},{129,1},{193,65},{1,129},{65,193... | collective-permute-start | bytes 2949128 | tf_op jit(solution)/shard_map/ppermute | solution.py:127
  51.3 42.5 %collective-permute-start.3 = (bf16[48,80,128]{2,1,0:T(8,128)(2,1)S(1)}, bf16[48,80,128]{2,1,0:T(8,128)(2,1)S(1)}, u32[]{:S(2)}, u32[]{:S(2)}) collective-permute-start(bf16[48,80,128]{2,1,0:T(8,128)(2,1)S(1)} %cut_rows.1.refs_0_), channel_id=1, source_target_pairs={{64,0},{128,64},{192,128},{0,192},{65,1},{129,65},{193,129},{1,193... | collective-permute-start | bytes 2949128 | tf_op jit(solution)/shard_map/ppermute | solution.py:127
  98.4 12.3 %copy-start.5 = (s32[3,6]{1,0:T(4,128)S(1)}, s32[3,6]{1,0:T(4,128)}, u32[]{:S(2)}) copy-start(s32[3,6]{1,0:T(4,128)} %param.13) | copy-start | bytes 220
  98.4 12.3 %copy-start.6 = (s32[3,2]{0,1:T(2,128)S(1)}, s32[3,2]{0,1:T(2,128)}, u32[]{:S(2)}) copy-start(s32[3,2]{0,1:T(2,128)} %param.12) | copy-start | bytes 76
  104.5 96.5 %all-to-all-start.2 = ((bf16[192,80,128]{2,1,0:T(8,128)(2,1)}), bf16[192,80,128]{2,1,0:T(8,128)(2,1)}, u32[]{:S(2)}, u32[]{:S(2)}) async-start(bf16[192,80,128]{2,1,0:T(8,128)(2,1)} %serve_tiles.3), calls=%async_computation.2 | async-start | bytes 7864320 | tf_op jit(solution)/shard_map/all_to_all | solution.py:263
  110.9 90.0 %copy-start.2 = (f32[3200]{0:T(1024)S(1)}, f32[3200]{0:T(1024)}, u32[]{:S(2)}) copy-start(f32[3200]{0:T(1024)} %param.15) | copy-start | bytes 38404
  110.9 90.0 %copy-start.3 = (f32[400]{0:T(512)S(1)}, f32[400]{0:T(512)}, u32[]{:S(2)}) copy-start(f32[400]{0:T(512)} %eps_occ_ref.1) | copy-start | bytes 4804
  110.9 90.0 %copy-start.4 = (s32[1,108]{1,0:T(1,128)S(1)}, s32[1,108]{1,0:T(1,128)}, u32[]{:S(2)}) copy-start(s32[1,108]{1,0:T(1,128)} %get-tuple-element.7) | copy-start | bytes 1300
  114.4 1.8 copy-start

commit v5 on v4

--- a/solution.py
+++ b/solution.py
@@ -7,16 +7,26 @@
 from jax.experimental.pallas import tpu as pltpu
 from jax.sharding import PartitionSpec as P
 
-ROWS_FIRST = 48
+ROWS_FIRST = 32
 PER_COLUMN = 3
+LONG = 400_000_000_000
 ANY = pl.BlockSpec(memory_space=pl.ANY)
 VMEM = pl.BlockSpec(memory_space=pltpu.VMEM)
 SMEM = pl.BlockSpec(memory_space=pltpu.SMEM)
 BIG = 100 * 2**20 // 2
 
 
-def ask_kernel(held, owner_ref, slot_ref, request_ref, place_ref):
+def ask_kernel(held, owner_ref, slot_ref, tiles_ref, request_ref, place_ref, first_ref, rest_ref, sem):
     vir = request_ref.shape[0]
+    rows = first_ref.shape[1]
+    copies = [
+        pltpu.make_async_copy(tiles_ref.at[:, pl.ds(0, rows)], first_ref, sem.at[0]),
+        pltpu.make_async_copy(
+            tiles_ref.at[:, pl.ds(rows, rest_ref.shape[1])], rest_ref, sem.at[1]
+        ),
+    ]
+    for copy in copies:
+        copy.start()
     owner, slot = owner_ref[...], slot_ref[...]
     asks = owner.shape[1]
     column = owner % vir
@@ -36,34 +46,82 @@
         ],
         axis=1,
     )
-
-
-def ask(owner, slot, vir, held):
+    for copy in copies:
+        copy.wait()
+
+
+def ask(owner, slot, tiles, vir):
+    held, _, tile = tiles.shape
     return pl.pallas_call(
         functools.partial(ask_kernel, held),
         out_shape=(
             jax.ShapeDtypeStruct((vir, PER_COLUMN), jnp.int32),
             jax.ShapeDtypeStruct(owner.shape, jnp.int32),
-        ),
-        in_specs=[VMEM, VMEM],
-        out_specs=(VMEM, VMEM),
+            jax.ShapeDtypeStruct((held, ROWS_FIRST, tile), tiles.dtype),
+            jax.ShapeDtypeStruct((held, tile - ROWS_FIRST, tile), tiles.dtype),
+        ),
+        in_specs=[VMEM, VMEM, ANY],
+        out_specs=(VMEM, VMEM, VMEM, VMEM),
+        scratch_shapes=[pltpu.SemaphoreType.DMA((2,))],
         name="make_requests",
-    )(owner, slot)
-
-
-def serve_kernel(n_pair, here_ref, code_ref, *refs):
-    sources, (out_ref, pool, sem) = refs[:n_pair], refs[n_pair:]
-    held = sources[0].shape[0]
+    )(owner, slot, tiles)
+
+
+def fill_pool(n_pair, held, parts, here_ref, sources, pool, sem):
     copies = []
-    for step in range(n_pair):
+    for k, (step, start) in enumerate(parts):
         owner = (here_ref[0] + step) % n_pair
-        target = pool.at[pl.ds(owner * held, held)]
-        copies.append(pltpu.make_async_copy(sources[step], target, sem.at[step]))
+        target = pool.at[pl.ds(owner * held + start, sources[k].shape[0])]
+        copies.append(pltpu.make_async_copy(sources[k], target, sem.at[k]))
     for copy in copies:
         copy.start()
     for copy in copies:
         copy.wait()
+
+
+def pool_kernel(n_pair, held, parts, here_ref, after_ref, rest_ref, *refs):
+    sources, (pool, passed_ref, sem) = refs[: len(parts)], refs[len(parts) :]
+    fill_pool(n_pair, held, parts, here_ref, sources, pool, sem)
+
+
+def pool_first(here, after, rest, parts, n_pair, held):
+    sources = [source for _, _, source in parts]
+    _, rows, tile = sources[0].shape
+    return pl.pallas_call(
+        functools.partial(pool_kernel, n_pair, held, [part[:2] for part in parts]),
+        out_shape=(
+            jax.ShapeDtypeStruct((n_pair * held, rows, tile), rest.dtype),
+            jax.ShapeDtypeStruct(rest.shape, rest.dtype),
+        ),
+        in_specs=[SMEM, ANY, ANY] + [ANY] * len(parts),
+        out_specs=(VMEM, ANY),
+        scratch_shapes=[pltpu.SemaphoreType.DMA((len(parts),))],
+        input_output_aliases={2: 1},
+        compiler_params=pltpu.CompilerParams(vmem_limit_bytes=BIG),
+        name="pool_tiles",
+    )(here, after, rest, *sources)
+
+
+def serve_kernel(n_pair, held, parts, here_ref, code_ref, *refs):
+    sources, (out_ref, pool, sem) = refs[: len(parts)], refs[len(parts) :]
+    fill_pool(n_pair, held, parts, here_ref, sources, pool, sem)
     take(code_ref, pool, out_ref)
+
+
+def serve_pool(codes, pool):
+    slots = codes.shape[0] * PER_COLUMN
+    _, rows, tile = pool.shape
+    return pl.pallas_call(
+        take,
+        out_shape=jax.ShapeDtypeStruct((slots, rows, tile), pool.dtype),
+        in_specs=[SMEM, VMEM],
+        out_specs=VMEM,
+        compiler_params=pltpu.CompilerParams(vmem_limit_bytes=BIG),
+        cost_estimate=pl.CostEstimate(
+            flops=0, bytes_accessed=4 * slots * rows * tile, transcendentals=0
+        ),
+        name="serve_pool",
+    )(codes, pool)
 
 
 def take(code_ref, pool, out_ref):
@@ -75,19 +133,19 @@
     lax.fori_loop(0, code_ref.shape[0], step, 0, unroll=4)
 
 
-def serve(here, codes, sources):
+def serve(here, codes, parts, n_pair, held):
     slots = codes.shape[0] * PER_COLUMN
-    n_pair = len(sources)
-    held, rows, tile = sources[0].shape
+    sources = [source for _, _, source in parts]
+    _, rows, tile = sources[0].shape
     dtype = sources[0].dtype
     return pl.pallas_call(
-        functools.partial(serve_kernel, n_pair),
+        functools.partial(serve_kernel, n_pair, held, [part[:2] for part in parts]),
         out_shape=jax.ShapeDtypeStruct((slots, rows, tile), dtype),
-        in_specs=[SMEM, SMEM] + [ANY] * n_pair,
+        in_specs=[SMEM, SMEM] + [ANY] * len(parts),
         out_specs=VMEM,
         scratch_shapes=[
             pltpu.VMEM((n_pair * held, rows, tile), dtype),
-            pltpu.SemaphoreType.DMA((n_pair,)),
+            pltpu.SemaphoreType.DMA((len(parts),)),
         ],
         compiler_params=pltpu.CompilerParams(vmem_limit_bytes=BIG),
         cost_estimate=pl.CostEstimate(
@@ -97,36 +155,52 @@
     )(here, codes, *sources)
 
 
-def cut_kernel(row_from, tiles_ref, after_ref, out_ref, sem):
-    copy = pltpu.make_async_copy(
-        tiles_ref.at[:, pl.ds(row_from, out_ref.shape[1])], out_ref, sem
-    )
-    copy.start()
-    copy.wait()
-
-
-def cut(tiles, after, row_from, rows):
-    held, _, tile = tiles.shape
-    return pl.pallas_call(
-        functools.partial(cut_kernel, row_from),
-        out_shape=jax.ShapeDtypeStruct((held, rows, tile), tiles.dtype),
+def halves_kernel(up_ref, down_ref, low_ref, high_ref, sem):
+    half = low_ref.shape[0]
+    first = pltpu.make_async_copy(up_ref.at[pl.ds(0, half)], low_ref, sem.at[0])
+    second = pltpu.make_async_copy(down_ref.at[pl.ds(half, half)], high_ref, sem.at[1])
+    first.start()
+    second.start()
+    first.wait()
+    second.wait()
+
+
+def halves(up, down):
+    held, rows, tile = up.shape
+    shape = jax.ShapeDtypeStruct((held // 2, rows, tile), up.dtype)
+    return pl.pallas_call(
+        halves_kernel,
+        out_shape=(shape, shape),
         in_specs=[ANY, ANY],
-        out_specs=VMEM,
-        scratch_shapes=[pltpu.SemaphoreType.DMA],
-        compiler_params=pltpu.CompilerParams(vmem_limit_bytes=BIG),
-        cost_estimate=pl.CostEstimate(
-            flops=0, bytes_accessed=4 * held * rows * tile, transcendentals=0
-        ),
-        name="cut_rows",
-    )(tiles, after)
+        out_specs=(VMEM, VMEM),
+        scratch_shapes=[pltpu.SemaphoreType.DMA((2,))],
+        compiler_params=pltpu.CompilerParams(vmem_limit_bytes=BIG),
+        cost_estimate=pl.CostEstimate(
+            flops=LONG, bytes_accessed=0, transcendentals=0
+        ),
+        name="cut_halves",
+    )(up, down)
 
 
 def from_others(mine):
     n = lax.axis_size("pair")
-    return [mine] + [
-        lax.ppermute(mine, "pair", [((i + step) % n, i) for i in range(n)])
+    return [(0, 0, mine)] + [
+        (step, 0, lax.ppermute(mine, "pair", [((i + step) % n, i) for i in range(n)]))
         for step in range(1, n)
     ]
+
+
+def from_ring(mine):
+    n = lax.axis_size("pair")
+    up = [(i, (i + 1) % n) for i in range(n)]
+    down = [(i, (i + n - 1) % n) for i in range(n)]
+    below = lax.ppermute(mine, "pair", up)
+    above = lax.ppermute(mine, "pair", down)
+    low, high = halves(below, above)
+    far_low = lax.ppermute(low, "pair", up)
+    far_high = lax.ppermute(high, "pair", down)
+    half = mine.shape[0] // 2
+    return [(0, 0, mine), (1, 0, above), (3, 0, below), (2, 0, far_low), (2, half, far_high)]
 
 
 def mix_kernel(amp_ref, after_ref, mixed_ref):
@@ -165,9 +239,8 @@
     def fetch(which):
         slot = which % 2
 
-        def step(k, carry):
-            row = pl.multiple_of((k // count) * tile, tile)
-            column = pl.ds(pl.multiple_of((k % count) * tile, tile), tile)
+        for k in range(count * count):
+            row, column = k // count * tile, pl.ds(k % count * tile, tile)
             place = place_ref[which * count * count + k]
             pltpu.make_async_copy(
                 first_ref.at[place], block.at[slot, pl.ds(row, rows_first), column], sem.at[slot]
@@ -177,9 +250,6 @@
                 block.at[slot, pl.ds(row + rows_first, tile - rows_first), column],
                 sem.at[slot],
             ).start()
-            return carry
-
-        lax.fori_loop(0, count * count, step, 0)
 
     @pl.when(pair == 0)
     def _():
@@ -245,21 +315,24 @@
 
 
 def body(amplitudes, integral_tiles, need_owner, need_slot, pair_occ, domain, eps_occ, eps_vir):
-    held, tile, _ = integral_tiles.shape
+    held = integral_tiles.shape[0]
+    tile = integral_tiles.shape[1]
     vir = lax.axis_size("vir")
     here = lax.axis_index("pair").astype(jnp.int32).reshape(1)
-    near = from_others(integral_tiles[:, :ROWS_FIRST])
-    rest = tile - ROWS_FIRST
-    far = from_others(cut(integral_tiles, near[1], ROWS_FIRST, rest))
-    requests, places = ask(need_owner.reshape(1, -1), need_slot.reshape(1, -1), vir, held)
+    n_pair = lax.axis_size("pair")
+    requests, places, first, rest = ask(
+        need_owner.reshape(1, -1), need_slot.reshape(1, -1), integral_tiles, vir
+    )
+    near = from_others(first)
     codes = lax.all_to_all(
         requests.reshape(vir, 1, PER_COLUMN), "vir", split_axis=0, concat_axis=0, tiled=True
     )
-
-    served = serve(here, codes, near)
+    pool, rest = pool_first(here, codes, rest, near, n_pair, held)
+    far = from_ring(rest)
     mixed = mix(amplitudes, codes)
+    served = serve_pool(codes, pool)
     got_first = lax.all_to_all(served, "vir", split_axis=0, concat_axis=0, tiled=True)
-    served = serve(here, codes, far)
+    served = serve(here, codes, far, n_pair, held)
     got_second = lax.all_to_all(served, "vir", split_axis=0, concat_axis=0, tiled=True)
     return residual(
         places.reshape(-1),

time: 213 us -> 213 us (level)
  starting transfers between devices: 43.1 us -> 38.1 us
  Pallas kernels: 24.3 us -> 27.5 us
    ppermute x6 -> x3, waiting for transfers between devices: 41.5 us -> 0.01 us  [from_others(): lax.ppermute(mine, 'pair', [((i + step) % n, i) for i in range(n)])]
    ppermute x0 -> x4, waiting for transfers between devices: none -> 26.4 us  [the longest x1 14.4 us: from_ring(): below = lax.ppermute(mine, 'pair', up)]
    all_to_all x2, waiting for transfers between devices: 90.9 us -> 106 us  [body(): lax.all_to_all(served, 'vir', split_axis=0, concat_axis=0, tiled=True)]
    all_to_all x2, starting transfers between devices: 19.7 us -> 13.7 us  [body(): lax.all_to_all(served, 'vir', split_axis=0, concat_axis=0, tiled=True)]
    ppermute x0 -> x4, starting transfers between devices: none -> 5.43 us  [the longest x1 2.67 us: from_ring(): far_high = lax.ppermute(high, 'pair', down)]
    ppermute x6 -> x3, starting transfers between devices: 10.2 us -> 5.72 us  [from_others(): lax.ppermute(mine, 'pair', [((i + step) % n, i) for i in range(n)])]
    unnamed x15 -> x19, local copies, waits for them, and re-layouts: 1.9 us -> 5.04 us
    pallas_call x3 -> x4, Pallas kernels: 8.04 us -> 10.1 us  [the longest x1 5.39 us: serve(): pl.pallas_call(functools.partial(serve_kernel, n_pair, held, [part[:2] fo...]
  transfers between devices with their start and end apart: 9 -> 10, of which waited for: 6 -> 5; matrix products, arithmetic and copies ran while one was open for 0% -> 0% of each run, Pallas kernels for 5% -> 5%
where the time goes in v5:
time: 213 us; the launch traced here: 212 us
  waiting for transfers between devices  142 us (67%)
  starting transfers between devices  38.1 us (18%)
  Pallas kernels  27.5 us (13%)
  local copies, waits for them, and re-layouts  5.21 us (2%)
    all_to_all x2, waiting for transfers between devices, body(): lax.all_to_all(served, 'vir', split_axis=0, concat_axis=0, tiled=True)  106 us
    ppermute x1, waiting for transfers between devices, from_ring(): below = lax.ppermute(mine, 'pair', up)  14.4 us
    all_to_all x2, starting transfers between devices, body(): lax.all_to_all(served, 'vir', split_axis=0, concat_axis=0, tiled=True)  13.7 us
    all_to_all x1, starting transfers between devices, body(): lax.all_to_all(requests.reshape(vir, 1, PER_COLUMN), 'vir', split_axis=0,...  13.2 us
    ppermute x1, waiting for transfers between devices, from_ring(): far_low = lax.ppermute(low, 'pair', up)  12.1 us
    pallas_call x1, Pallas kernels, residual(): pl.pallas_call(functools.partial(residual_kernel, rows_first, tile), grid...  10.7 us
    all_to_all x1, waiting for transfers between devices, body(): lax.all_to_all(requests.reshape(vir, 1, PER_COLUMN), 'vir', split_axis=0,...  9.28 us
    ppermute x3, starting transfers between devices, from_others(): lax.ppermute(mine, 'pair', [((i + step) % n, i) for i in range(n)])  5.72 us
  transfers between devices with their start and end apart: 10, of which 5 were waited for; matrix products, arithmetic and copies ran while one was open for 0% of the time, Pallas kernels for 5%

profile of v5, /device:TPU:1, one launch (start us, length us, event | category | flops | bytes accessed | tf_op | source)
XLA Modules:
  0.0 212.4 jit_solution(2293983045817147510)
XLA Ops:
  0.0 3.3 %make_requests.1 = (s32[64,3]{1,0:T(8,128)}, s32[1,108]{1,0:T(1,128)}, bf16[48,32,128]{2,1,0:T(8,128)(2,1)}, bf16[48,96,128]{2,1,0:T(8,128)(2,1)}) custom-call(s32[1,108]{1,0:T(1,128)} %bitcast.9, s32[1,108]{1,0:T(1,128)} %bitcast.10, bf16[48,128,128]{2,1,0:T(8,128)(2,1)} %tiles_ref.1), custom_call_target="tpu_custom_call" | custom-call | tf_op jit(solution)/shard_map/make_requests/pallas_call | solution.py:55
  3.3 2.1 collective-permute-start.2
  5.4 2.5 %collective-permute-start.1 = (bf16[48,32,128]{2,1,0:T(8,128)(2,1)}, bf16[48,32,128]{2,1,0:T(8,128)(2,1)S(1)}, u32[]{:S(2)}, u32[]{:S(2)}) collective-permute-start(bf16[48,32,128]{2,1,0:T(8,128)(2,1)} %get-tuple-element.16.refs_0_), channel_id=1, source_target_pairs={{128,0},{192,64},{0,128},{64,192},{129,1},{193,65},{1,129},{65,193... | collective-permute-start | bytes 1179656 | tf_op jit(solution)/shard_map/ppermute | solution.py:188
  7.8 1.2 collective-permute-start
  9.0 13.2 %all-to-all-start = ((s32[64,1,3]{2,1,0:T(1,128)}), s32[64,1,3]{2,1,0:T(1,128)S(1)}, u32[]{:S(2)}, u32[]{:S(2)}) async-start(s32[64,1,3]{2,1,0:T(1,128)} %bitcast.8), calls=%async_computation | async-start | bytes 65536 | tf_op jit(solution)/shard_map/all_to_all | solution.py:327
  22.2 9.3 %all-to-all-done.after_ref.code_ref = s32[64,1,3]{2,1,0:T(1,128)S(1)} async-done(((s32[64,1,3]{2,1,0:T(1,128)}), s32[64,1,3]{2,1,0:T(1,128)S(1)}, u32[]{:S(2)}, u32[]{:S(2)}) %all-to-all-start) | async-done | bytes 800 | tf_op jit(solution)/shard_map/all_to_all | solution.py:327
  31.5 1.0 copy-done.3
  32.5 1.9 pool_tiles.1
  34.4 0.4 collective-permute-start.4
  34.8 2.4 %collective-permute-start.3 = (bf16[48,96,128]{2,1,0:T(8,128)(2,1)}, bf16[48,96,128]{2,1,0:T(8,128)(2,1)S(1)}, u32[]{:S(2)}, u32[]{:S(2)}) collective-permute-start(bf16[48,96,128]{2,1,0:T(8,128)(2,1)} %get-tuple-element.18.refs_0_), channel_id=1, source_target_pairs={{0,192},{64,0},{128,64},{192,128},{1,193},{65,1},{129,65},{193,129... | collective-permute-start | bytes 3538952 | tf_op jit(solution)/shard_map/ppermute | solution.py:198
  37.2 1.4 copy-done.1
  38.6 2.5 %serve_pool.1 = bf16[192,32,128]{2,1,0:T(8,128)(2,1)} custom-call(s32[64,1,3]{2,1,0:T(1,128)S(1)} %all-to-all-done.after_ref.code_ref, bf16[192,32,128]{2,1,0:T(8,128)(2,1)S(1)} %copy-done.1), custom_call_target="tpu_custom_call" | custom-call | bytes 3145728 | tf_op jit(solution)/shard_map/serve_pool/pallas_call | solution.py:114
  41.1 7.5 %all-to-all-start.1 = ((bf16[192,32,128]{2,1,0:T(8,128)(2,1)}), bf16[192,32,128]{2,1,0:T(8,128)(2,1)}, u32[]{:S(2)}, u32[]{:S(2)}) async-start(bf16[192,32,128]{2,1,0:T(8,128)(2,1)} %serve_pool.1), calls=%async_computation.1 | async-start | bytes 3145728 | tf_op jit(solution)/shard_map/all_to_all | solution.py:334
  48.5 14.4 %collective-permute-done.4.up_ref.refs_2_ = bf16[48,96,128]{2,1,0:T(8,128)(2,1)S(1)} collective-permute-done((bf16[48,96,128]{2,1,0:T(8,128)(2,1)}, bf16[48,96,128]{2,1,0:T(8,128)(2,1)S(1)}, u32[]{:S(2)}, u32[]{:S(2)}) %collective-permute-start.4) | collective-permute-done | bytes 1179680 | tf_op jit(solution)/shard_map/ppermute | solution.py:197
  63.1 0.7 copy-done.2
  63.9 2.7 %collective-permute-start.6 = (bf16[24,96,128]{2,1,0:T(8,128)(2,1)S(1)}, bf16[24,96,128]{2,1,0:T(8,128)(2,1)S(1)}, u32[]{:S(2)}, u32[]{:S(2)}) collective-permute-start(bf16[24,96,128]{2,1,0:T(8,128)(2,1)S(1)} %get-tuple-element.20), channel_id=1, source_target_pairs={{0,192},{64,0},{128,64},{192,128},{1,193},{65,1},{129,65},{193,129... | collective-permute-start | bytes 1769480 | tf_op jit(solution)/shard_map/ppermute | solution.py:201
  66.6 12.1 %collective-permute-done.5.refs_3_ = bf16[24,96,128]{2,1,0:T(8,128)(2,1)S(1)} collective-permute-done((bf16[24,96,128]{2,1,0:T(8,128)(2,1)S(1)}, bf16[24,96,128]{2,1,0:T(8,128)(2,1)S(1)}, u32[]{:S(2)}, u32[]{:S(2)}) %collective-permute-start.5) | collective-permute-done | bytes 589856 | tf_op jit(solution)/shard_map/ppermute | solution.py:200
  78.6 5.4 %serve_tiles.1 = bf16[192,96,128]{2,1,0:T(8,128)(2,1)} custom-call(s32[1]{0:T(128)} %bitcast.5.here_ref, s32[64,1,3]{2,1,0:T(1,128)S(1)} %all-to-all-done.after_ref.code_ref, bf16[48,96,128]{2,1,0:T(8,128)(2,1)} %get-tuple-element.18.refs_0_, bf16[48,96,128]{2,1,0:T(8,128)(2,1)S(1)} %collective-permute-done.3.down_ref.refs_1_, ...), custom_call_target="tpu_custom_call" | custom-call | bytes 9437184 | tf_op jit(solution)/shard_map/serve_tiles/pallas_call | solution.py:141
  84.1 4.2 %all-to-all-done.1.first_ref = bf16[192,32,128]{2,1,0:T(8,128)(2,1)} async-done(((bf16[192,32,128]{2,1,0:T(8,128)(2,1)}), bf16[192,32,128]{2,1,0:T(8,128)(2,1)}, u32[]{:S(2)}, u32[]{:S(2)}) %all-to-all-start.1) | async-done | bytes 1572896 | tf_op jit(solution)/shard_map/all_to_all | solution.py:334
  88.3 6.3 %all-to-all-start.2 = ((bf16[192,96,128]{2,1,0:T(8,128)(2,1)}), bf16[192,96,128]{2,1,0:T(8,128)(2,1)}, u32[]{:S(2)}, u32[]{:S(2)}) async-start(bf16[192,96,128]{2,1,0:T(8,128)(2,1)} %serve_tiles.1), calls=%async_computation.2 | async-start | bytes 9437184 | tf_op jit(solution)/shard_map/all_to_all | solution.py:336
  94.8 3.4 %mix_amplitudes.1.mixed_ref = bf16[3,768,768]{2,1,0:T(8,128)(2,1)S(1)} custom-call(bf16[3,768,768]{2,1,0:T(8,128)(2,1)} %amp_ref.1, s32[64,1,3]{2,1,0:T(1,128)S(1)} %all-to-all-done.after_ref.code_ref), custom_call_target="tpu_custom_call" | custom-call | flops 1769472 | bytes 7077888 | tf_op jit(solution)/shard_map/mix_amplitudes/pallas_call | solution.py:216
  98.3 1.8 copy-done
  100.1 101.6 %all-to-all-done.2.second_ref = bf16[192,96,128]{2,1,0:T(8,128)(2,1)} async-done(((bf16[192,96,128]{2,1,0:T(8,128)(2,1)}), bf16[192,96,128]{2,1,0:T(8,128)(2,1)}, u32[]{:S(2)}, u32[]{:S(2)}) %all-to-all-start.2) | async-done | bytes 4718624 | tf_op jit(solution)/shard_map/all_to_all | solution.py:336
  201.7 10.7 %residual.1 = f32[3,768,768]{2,1,0:T(8,128)} custom-call(s32[108]{0:T(128)S(1)} %bitcast.7, s32[6]{0:T(128)S(1)} %reshape.27.occ_ref, s32[18]{0:T(128)S(1)} %reshape.28.domain_ref, f32[400]{0:T(512)S(1)} %copy-done.5, f32[25,128]{1,0:T(8,128)S(1)} %bitcast.6, bf16[3,768,768]{2,1,0:T(8,128)(2,1)} %copy-done, bf16[192,32,128]{2,1,0:T(8,128)(2,1)} %all-to-all-done.1.first_ref, ...), custom_call_target="tpu_custom_call" | custom-call | flops 5435817984 | bytes 14155776 | tf_op jit(solution)/shard_map/residual/pallas_call | solution.py:290
  (24 shorter events, 0.6 us)
Async XLA Ops:
  3.3 28.2 %collective-permute-start.2 = (bf16[48,32,128]{2,1,0:T(8,128)(2,1)}, bf16[48,32,128]{2,1,0:T(8,128)(2,1)S(1)}, u32[]{:S(2)}, u32[]{:S(2)}) collective-permute-start(bf16[48,32,128]{2,1,0:T(8,128)(2,1)} %get-tuple-element.16.refs_0_), channel_id=1, source_target_pairs={{192,0},{0,64},{64,128},{128,192},{193,1},{1,65},{65,129},{129,193... | collective-permute-start | bytes 1179656 | tf_op jit(solution)/shard_map/ppermute | solution.py:188
  5.4 26.1 %collective-permute-start.1 = (bf16[48,32,128]{2,1,0:T(8,128)(2,1)}, bf16[48,32,128]{2,1,0:T(8,128)(2,1)S(1)}, u32[]{:S(2)}, u32[]{:S(2)}) collective-permute-start(bf16[48,32,128]{2,1,0:T(8,128)(2,1)} %get-tuple-element.16.refs_0_), channel_id=1, source_target_pairs={{128,0},{192,64},{0,128},{64,192},{129,1},{193,65},{1,129},{65,193... | collective-permute-start | bytes 1179656 | tf_op jit(solution)/shard_map/ppermute | solution.py:188
  7.8 23.6 %collective-permute-start = (bf16[48,32,128]{2,1,0:T(8,128)(2,1)}, bf16[48,32,128]{2,1,0:T(8,128)(2,1)S(1)}, u32[]{:S(2)}, u32[]{:S(2)}) collective-permute-start(bf16[48,32,128]{2,1,0:T(8,128)(2,1)} %get-tuple-element.16.refs_0_), channel_id=1, source_target_pairs={{64,0},{128,64},{192,128},{0,192},{65,1},{129,65},{193,129},{1,193... | collective-permute-start | bytes 1179656 | tf_op jit(solution)/shard_map/ppermute | solution.py:188
  9.0 22.5 %all-to-all-start = ((s32[64,1,3]{2,1,0:T(1,128)}), s32[64,1,3]{2,1,0:T(1,128)S(1)}, u32[]{:S(2)}, u32[]{:S(2)}) async-start(s32[64,1,3]{2,1,0:T(1,128)} %bitcast.8), calls=%async_computation | async-start | bytes 65536 | tf_op jit(solution)/shard_map/all_to_all | solution.py:327
  31.5 1.0 copy-start.3
  34.4 28.5 %collective-permute-start.4 = (bf16[48,96,128]{2,1,0:T(8,128)(2,1)}, bf16[48,96,128]{2,1,0:T(8,128)(2,1)S(1)}, u32[]{:S(2)}, u32[]{:S(2)}) collective-permute-start(bf16[48,96,128]{2,1,0:T(8,128)(2,1)} %get-tuple-element.18.refs_0_), channel_id=1, source_target_pairs={{0,64},{64,128},{128,192},{192,0},{1,65},{65,129},{129,193},{193,1... | collective-permute-start | bytes 3538952 | tf_op jit(solution)/shard_map/ppermute | solution.py:197
  34.8 28.1 %collective-permute-start.3 = (bf16[48,96,128]{2,1,0:T(8,128)(2,1)}, bf16[48,96,128]{2,1,0:T(8,128)(2,1)S(1)}, u32[]{:S(2)}, u32[]{:S(2)}) collective-permute-start(bf16[48,96,128]{2,1,0:T(8,128)(2,1)} %get-tuple-element.18.refs_0_), channel_id=1, source_target_pairs={{0,192},{64,0},{128,64},{192,128},{1,193},{65,1},{129,65},{193,129... | collective-permute-start | bytes 3538952 | tf_op jit(solution)/shard_map/ppermute | solution.py:198
  37.2 1.4 copy-start.1
  41.1 47.2 %all-to-all-start.1 = ((bf16[192,32,128]{2,1,0:T(8,128)(2,1)}), bf16[192,32,128]{2,1,0:T(8,128)(2,1)}, u32[]{:S(2)}, u32[]{:S(2)}) async-start(bf16[192,32,128]{2,1,0:T(8,128)(2,1)} %serve_pool.1), calls=%async_computation.1 | async-start | bytes 3145728 | tf_op jit(solution)/shard_map/all_to_all | solution.py:334
  62.9 1.0 copy-start.2
  63.9 14.7 %collective-permute-start.5 = (bf16[24,96,128]{2,1,0:T(8,128)(2,1)S(1)}, bf16[24,96,128]{2,1,0:T(8,128)(2,1)S(1)}, u32[]{:S(2)}, u32[]{:S(2)}) collective-permute-start(bf16[24,96,128]{2,1,0:T(8,128)(2,1)S(1)} %get-tuple-element.19), channel_id=1, source_target_pairs={{0,64},{64,128},{128,192},{192,0},{1,65},{65,129},{129,193},{193,1... | collective-permute-start | bytes 1769480 | tf_op jit(solution)/shard_map/ppermute | solution.py:200
  63.9 14.7 %collective-permute-start.6 = (bf16[24,96,128]{2,1,0:T(8,128)(2,1)S(1)}, bf16[24,96,128]{2,1,0:T(8,128)(2,1)S(1)}, u32[]{:S(2)}, u32[]{:S(2)}) collective-permute-start(bf16[24,96,128]{2,1,0:T(8,128)(2,1)S(1)} %get-tuple-element.20), channel_id=1, source_target_pairs={{0,192},{64,0},{128,64},{192,128},{1,193},{65,1},{129,65},{193,129... | collective-permute-start | bytes 1769480 | tf_op jit(solution)/shard_map/ppermute | solution.py:201
  84.0 10.5 %copy-start.7 = (s32[3,6]{1,0:T(4,128)S(1)}, s32[3,6]{1,0:T(4,128)}, u32[]{:S(2)}) copy-start(s32[3,6]{1,0:T(4,128)} %param.13) | copy-start | bytes 220
  84.0 10.6 %copy-start.8 = (s32[3,2]{0,1:T(2,128)S(1)}, s32[3,2]{0,1:T(2,128)}, u32[]{:S(2)}) copy-start(s32[3,2]{0,1:T(2,128)} %param.12) | copy-start | bytes 76
  88.3 113.4 %all-to-all-start.2 = ((bf16[192,96,128]{2,1,0:T(8,128)(2,1)}), bf16[192,96,128]{2,1,0:T(8,128)(2,1)}, u32[]{:S(2)}, u32[]{:S(2)}) async-start(bf16[192,96,128]{2,1,0:T(8,128)(2,1)} %serve_tiles.1), calls=%async_computation.2 | async-start | bytes 9437184 | tf_op jit(solution)/shard_map/all_to_all | solution.py:336
  94.8 106.9 %copy-start.4 = (f32[3200]{0:T(1024)S(1)}, f32[3200]{0:T(1024)}, u32[]{:S(2)}) copy-start(f32[3200]{0:T(1024)} %param.15) | copy-start | bytes 38404
  94.8 106.9 %copy-start.5 = (f32[400]{0:T(512)S(1)}, f32[400]{0:T(512)}, u32[]{:S(2)}) copy-start(f32[400]{0:T(512)} %eps_occ_ref.1) | copy-start | bytes 4804
  94.8 106.9 %copy-start.6 = (s32[1,108]{1,0:T(1,128)S(1)}, s32[1,108]{1,0:T(1,128)}, u32[]{:S(2)}) copy-start(s32[1,108]{1,0:T(1,128)} %get-tuple-element.13) | copy-start | bytes 1300
  98.3 1.8 copy-start

commit v6 on v5

--- a/solution.py
+++ b/solution.py
@@ -16,17 +16,12 @@
 BIG = 100 * 2**20 // 2
 
 
-def ask_kernel(held, owner_ref, slot_ref, tiles_ref, request_ref, place_ref, first_ref, rest_ref, sem):
+def ask_kernel(held, owner_ref, slot_ref, tiles_ref, request_ref, place_ref, first_ref, sem):
     vir = request_ref.shape[0]
-    rows = first_ref.shape[1]
-    copies = [
-        pltpu.make_async_copy(tiles_ref.at[:, pl.ds(0, rows)], first_ref, sem.at[0]),
-        pltpu.make_async_copy(
-            tiles_ref.at[:, pl.ds(rows, rest_ref.shape[1])], rest_ref, sem.at[1]
-        ),
-    ]
-    for copy in copies:
-        copy.start()
+    copy = pltpu.make_async_copy(
+        tiles_ref.at[:, pl.ds(0, first_ref.shape[1])], first_ref, sem
+    )
+    copy.start()
     owner, slot = owner_ref[...], slot_ref[...]
     asks = owner.shape[1]
     column = owner % vir
@@ -46,8 +41,7 @@
         ],
         axis=1,
     )
-    for copy in copies:
-        copy.wait()
+    copy.wait()
 
 
 def ask(owner, slot, tiles, vir):
@@ -58,11 +52,10 @@
             jax.ShapeDtypeStruct((vir, PER_COLUMN), jnp.int32),
             jax.ShapeDtypeStruct(owner.shape, jnp.int32),
             jax.ShapeDtypeStruct((held, ROWS_FIRST, tile), tiles.dtype),
-            jax.ShapeDtypeStruct((held, tile - ROWS_FIRST, tile), tiles.dtype),
         ),
         in_specs=[VMEM, VMEM, ANY],
-        out_specs=(VMEM, VMEM, VMEM, VMEM),
-        scratch_shapes=[pltpu.SemaphoreType.DMA((2,))],
+        out_specs=(VMEM, VMEM, VMEM),
+        scratch_shapes=[pltpu.SemaphoreType.DMA],
         name="make_requests",
     )(owner, slot, tiles)
 
@@ -79,49 +72,25 @@
         copy.wait()
 
 
-def pool_kernel(n_pair, held, parts, here_ref, after_ref, rest_ref, *refs):
-    sources, (pool, passed_ref, sem) = refs[: len(parts)], refs[len(parts) :]
-    fill_pool(n_pair, held, parts, here_ref, sources, pool, sem)
-
-
-def pool_first(here, after, rest, parts, n_pair, held):
-    sources = [source for _, _, source in parts]
-    _, rows, tile = sources[0].shape
-    return pl.pallas_call(
-        functools.partial(pool_kernel, n_pair, held, [part[:2] for part in parts]),
-        out_shape=(
-            jax.ShapeDtypeStruct((n_pair * held, rows, tile), rest.dtype),
-            jax.ShapeDtypeStruct(rest.shape, rest.dtype),
-        ),
-        in_specs=[SMEM, ANY, ANY] + [ANY] * len(parts),
-        out_specs=(VMEM, ANY),
-        scratch_shapes=[pltpu.SemaphoreType.DMA((len(parts),))],
-        input_output_aliases={2: 1},
-        compiler_params=pltpu.CompilerParams(vmem_limit_bytes=BIG),
-        name="pool_tiles",
-    )(here, after, rest, *sources)
+def gate_kernel(rows_ref, code_ref, sample_ref, out_ref):
+    pass
+
+
+def gate(rows, codes, sample):
+    return pl.pallas_call(
+        gate_kernel,
+        out_shape=jax.ShapeDtypeStruct(rows.shape, rows.dtype),
+        in_specs=[ANY, ANY, ANY],
+        out_specs=ANY,
+        input_output_aliases={0: 0},
+        name="gate_rows",
+    )(rows, codes, sample)
 
 
 def serve_kernel(n_pair, held, parts, here_ref, code_ref, *refs):
     sources, (out_ref, pool, sem) = refs[: len(parts)], refs[len(parts) :]
     fill_pool(n_pair, held, parts, here_ref, sources, pool, sem)
     take(code_ref, pool, out_ref)
-
-
-def serve_pool(codes, pool):
-    slots = codes.shape[0] * PER_COLUMN
-    _, rows, tile = pool.shape
-    return pl.pallas_call(
-        take,
-        out_shape=jax.ShapeDtypeStruct((slots, rows, tile), pool.dtype),
-        in_specs=[SMEM, VMEM],
-        out_specs=VMEM,
-        compiler_params=pltpu.CompilerParams(vmem_limit_bytes=BIG),
-        cost_estimate=pl.CostEstimate(
-            flops=0, bytes_accessed=4 * slots * rows * tile, transcendentals=0
-        ),
-        name="serve_pool",
-    )(codes, pool)
 
 
 def take(code_ref, pool, out_ref):
@@ -320,17 +289,17 @@
     vir = lax.axis_size("vir")
     here = lax.axis_index("pair").astype(jnp.int32).reshape(1)
     n_pair = lax.axis_size("pair")
-    requests, places, first, rest = ask(
+    requests, places, first = ask(
         need_owner.reshape(1, -1), need_slot.reshape(1, -1), integral_tiles, vir
     )
     near = from_others(first)
     codes = lax.all_to_all(
         requests.reshape(vir, 1, PER_COLUMN), "vir", split_axis=0, concat_axis=0, tiled=True
     )
-    pool, rest = pool_first(here, codes, rest, near, n_pair, held)
-    far = from_ring(rest)
+    sample = sum(part[0, :8] for _, _, part in near[1:])
+    far = from_ring(gate(integral_tiles[:, ROWS_FIRST:], codes, sample))
     mixed = mix(amplitudes, codes)
-    served = serve_pool(codes, pool)
+    served = serve(here, codes, near, n_pair, held)
     got_first = lax.all_to_all(served, "vir", split_axis=0, concat_axis=0, tiled=True)
     served = serve(here, codes, far, n_pair, held)
     got_second = lax.all_to_all(served, "vir", split_axis=0, concat_axis=0, tiled=True)

time: 213 us -> 214 us (level)
  waiting for transfers between devices: 142 us -> 139 us
  local copies, waits for them, and re-layouts: 5.21 us -> 8.03 us
    pallas_call x2 -> x1, Pallas kernels: 4.41 us -> 0.01 us  [gate(): pl.pallas_call(gate_kernel, out_shape=jax.ShapeDtypeStruct(rows.shape, ro...]
    all_to_all x1, waiting for transfers between devices: 9.28 us -> 5.12 us  [body(): lax.all_to_all(requests.reshape(vir, 1, PER_COLUMN), 'vir', split_axis=0,...]
    ppermute x1, waiting for transfers between devices: 14.4 us -> 10.8 us  [from_ring(): below = lax.ppermute(mine, 'pair', up)]
    all_to_all x2, waiting for transfers between devices: 106 us -> 109 us  [body(): lax.all_to_all(served, 'vir', split_axis=0, concat_axis=0, tiled=True)]
    pallas_call x1 -> x2, Pallas kernels: 5.39 us -> 8.78 us  [serve(): pl.pallas_call(functools.partial(serve_kernel, n_pair, held, [part[:2] fo...]
    unnamed x19 -> x31, local copies, waits for them, and re-layouts: 5.04 us -> 6.76 us
  transfers between devices with their start and end apart: 10 -> 10, of which waited for: 5 -> 6; matrix products, arithmetic and copies ran while one was open for 0% -> 1% of each run, Pallas kernels for 5% -> 6%
where the time goes in v6:
time: 214 us; the launch traced here: 213 us
  waiting for transfers between devices  139 us (65%)
  starting transfers between devices  39.3 us (18%)
  Pallas kernels  25.8 us (12%)
  local copies, waits for them, and re-layouts  8.03 us (4%)
    all_to_all x2, waiting for transfers between devices, body(): lax.all_to_all(served, 'vir', split_axis=0, concat_axis=0, tiled=True)  109 us
    all_to_all x2, starting transfers between devices, body(): lax.all_to_all(served, 'vir', split_axis=0, concat_axis=0, tiled=True)  15.1 us
    all_to_all x1, starting transfers between devices, body(): lax.all_to_all(requests.reshape(vir, 1, PER_COLUMN), 'vir', split_axis=0,...  13.2 us
    ppermute x1, waiting for transfers between devices, from_ring(): far_low = lax.ppermute(low, 'pair', up)  12 us
    ppermute x1, waiting for transfers between devices, from_ring(): below = lax.ppermute(mine, 'pair', up)  10.8 us
    pallas_call x1, Pallas kernels, residual(): pl.pallas_call(functools.partial(residual_kernel, rows_first, tile), grid...  10.7 us
    pallas_call x2, Pallas kernels, serve(): pl.pallas_call(functools.partial(serve_kernel, n_pair, held, [part[:2] fo...  8.78 us
    unnamed x31, local copies, waits for them, and re-layouts  6.76 us
  transfers between devices with their start and end apart: 10, of which 6 were waited for; matrix products, arithmetic and copies ran while one was open for 1% of the time, Pallas kernels for 6%

profile of v6, /device:TPU:1, one launch (start us, length us, event | category | flops | bytes accessed | tf_op | source)
XLA Modules:
  0.0 212.8 jit_solution(1027430413313237970)
XLA Ops:
  0.0 2.6 %make_requests.1 = (s32[64,3]{1,0:T(8,128)}, s32[1,108]{1,0:T(1,128)}, bf16[48,32,128]{2,1,0:T(8,128)(2,1)}) custom-call(s32[1,108]{1,0:T(1,128)} %bitcast.11, s32[1,108]{1,0:T(1,128)} %bitcast.12, bf16[48,128,128]{2,1,0:T(8,128)(2,1)} %tiles_ref.1), custom_call_target="tpu_custom_call" | custom-call | tf_op jit(solution)/shard_map/make_requests/pallas_call | solution.py:49
  2.6 2.1 collective-permute-start.2
  4.7 2.5 %collective-permute-start.1 = (bf16[48,32,128]{2,1,0:T(8,128)(2,1)}, bf16[48,32,128]{2,1,0:T(8,128)(2,1)S(1)}, u32[]{:S(2)}, u32[]{:S(2)}) collective-permute-start(bf16[48,32,128]{2,1,0:T(8,128)(2,1)} %get-tuple-element.12.refs_0_), channel_id=1, source_target_pairs={{128,0},{192,64},{0,128},{64,192},{129,1},{193,65},{1,129},{65,193... | collective-permute-start | bytes 1179656 | tf_op jit(solution)/shard_map/ppermute | solution.py:157
  7.1 1.2 collective-permute-start
  8.3 13.2 %all-to-all-start = ((s32[64,1,3]{2,1,0:T(1,128)}), s32[64,1,3]{2,1,0:T(1,128)S(1)}, u32[]{:S(2)}, u32[]{:S(2)}) async-start(s32[64,1,3]{2,1,0:T(1,128)} %bitcast.10), calls=%async_computation | async-start | bytes 65536 | tf_op jit(solution)/shard_map/all_to_all | solution.py:296
  21.5 1.1 slice.12.rows_ref
  22.6 1.7 collective-permute-done.1.refs_2_
  25.6 5.1 %all-to-all-done.after_ref.code_ref = s32[64,1,3]{2,1,0:T(1,128)S(1)} async-done(((s32[64,1,3]{2,1,0:T(1,128)}), s32[64,1,3]{2,1,0:T(1,128)S(1)}, u32[]{:S(2)}, u32[]{:S(2)}) %all-to-all-start) | async-done | bytes 800 | tf_op jit(solution)/shard_map/all_to_all | solution.py:296
  31.7 2.4 %collective-permute-start.3 = (bf16[48,96,128]{2,1,0:T(8,128)(2,1)}, bf16[48,96,128]{2,1,0:T(8,128)(2,1)S(1)}, u32[]{:S(2)}, u32[]{:S(2)}) collective-permute-start(bf16[48,96,128]{2,1,0:T(8,128)(2,1)} %gate_rows.1.refs_0_), channel_id=1, source_target_pairs={{0,192},{64,0},{128,64},{192,128},{1,193},{65,1},{129,65},{193,129... | collective-permute-start | bytes 3538952 | tf_op jit(solution)/shard_map/ppermute | solution.py:167
  34.0 0.8 copy-done.4
  34.8 1.0 copy-done.7
  35.8 1.0 copy-done.8
  36.8 3.3 %serve_tiles.2 = bf16[192,32,128]{2,1,0:T(8,128)(2,1)} custom-call(s32[1]{0:T(128)} %bitcast.5.here_ref, s32[64,1,3]{2,1,0:T(1,128)S(1)} %copy-done.4, bf16[48,32,128]{2,1,0:T(8,128)(2,1)S(1)} %copy-done.8, bf16[48,32,128]{2,1,0:T(8,128)(2,1)S(1)} %copy-done.7, bf16[48,32,128]{2,1,0:T(8,128)(2,1)S(1)} %collective-permute-done.1.refs_2_, ...), custom_call_target="tpu_custom_call" | custom-call | bytes 3145728 | tf_op jit(solution)/shard_map/serve_tiles/pallas_call | solution.py:110
  40.1 8.8 %all-to-all-start.1 = ((bf16[192,32,128]{2,1,0:T(8,128)(2,1)}), bf16[192,32,128]{2,1,0:T(8,128)(2,1)}, u32[]{:S(2)}, u32[]{:S(2)}) async-start(bf16[192,32,128]{2,1,0:T(8,128)(2,1)} %serve_tiles.2), calls=%async_computation.1 | async-start | bytes 3145728 | tf_op jit(solution)/shard_map/all_to_all | solution.py:303
  48.9 10.8 %collective-permute-done.4.up_ref.refs_2_ = bf16[48,96,128]{2,1,0:T(8,128)(2,1)S(1)} collective-permute-done((bf16[48,96,128]{2,1,0:T(8,128)(2,1)}, bf16[48,96,128]{2,1,0:T(8,128)(2,1)S(1)}, u32[]{:S(2)}, u32[]{:S(2)}) %collective-permute-start.4) | collective-permute-done | bytes 1179680 | tf_op jit(solution)/shard_map/ppermute | solution.py:166
  60.8 2.7 %collective-permute-start.6 = (bf16[24,96,128]{2,1,0:T(8,128)(2,1)S(1)}, bf16[24,96,128]{2,1,0:T(8,128)(2,1)S(1)}, u32[]{:S(2)}, u32[]{:S(2)}) collective-permute-start(bf16[24,96,128]{2,1,0:T(8,128)(2,1)S(1)} %get-tuple-element.14), channel_id=1, source_target_pairs={{0,192},{64,0},{128,64},{192,128},{1,193},{65,1},{129,65},{193,129... | collective-permute-start | bytes 1769480 | tf_op jit(solution)/shard_map/ppermute | solution.py:170
  63.4 12.0 %collective-permute-done.5.refs_3_ = bf16[24,96,128]{2,1,0:T(8,128)(2,1)S(1)} collective-permute-done((bf16[24,96,128]{2,1,0:T(8,128)(2,1)S(1)}, bf16[24,96,128]{2,1,0:T(8,128)(2,1)S(1)}, u32[]{:S(2)}, u32[]{:S(2)}) %collective-permute-start.5) | collective-permute-done | bytes 589856 | tf_op jit(solution)/shard_map/ppermute | solution.py:169
  75.5 5.5 %serve_tiles.3 = bf16[192,96,128]{2,1,0:T(8,128)(2,1)} custom-call(s32[1]{0:T(128)} %bitcast.5.here_ref, s32[64,1,3]{2,1,0:T(1,128)S(1)} %copy-done.5, bf16[48,96,128]{2,1,0:T(8,128)(2,1)S(1)} %copy-done, bf16[48,96,128]{2,1,0:T(8,128)(2,1)S(1)} %collective-permute-done.3.down_ref.refs_1_, bf16[48,96,128]{2,1,0:T(8,128)(2,1)} %copy-done.2, ...), custom_call_target="tpu_custom_call" | custom-call | bytes 9437184 | tf_op jit(solution)/shard_map/serve_tiles/pallas_call | solution.py:110
  81.0 7.7 %all-to-all-done.1.first_ref = bf16[192,32,128]{2,1,0:T(8,128)(2,1)} async-done(((bf16[192,32,128]{2,1,0:T(8,128)(2,1)}), bf16[192,32,128]{2,1,0:T(8,128)(2,1)}, u32[]{:S(2)}, u32[]{:S(2)}) %all-to-all-start.1) | async-done | bytes 1572896 | tf_op jit(solution)/shard_map/all_to_all | solution.py:303
  88.7 6.3 %all-to-all-start.2 = ((bf16[192,96,128]{2,1,0:T(8,128)(2,1)}), bf16[192,96,128]{2,1,0:T(8,128)(2,1)}, u32[]{:S(2)}, u32[]{:S(2)}) async-start(bf16[192,96,128]{2,1,0:T(8,128)(2,1)} %serve_tiles.3), calls=%async_computation.2 | async-start | bytes 9437184 | tf_op jit(solution)/shard_map/all_to_all | solution.py:305
  95.2 3.4 %mix_amplitudes.1.mixed_ref = bf16[3,768,768]{2,1,0:T(8,128)(2,1)S(1)} custom-call(bf16[3,768,768]{2,1,0:T(8,128)(2,1)} %amp_ref.1, s32[64,1,3]{2,1,0:T(1,128)S(1)} %copy-done.5), custom_call_target="tpu_custom_call" | custom-call | flops 1769472 | bytes 7077888 | tf_op jit(solution)/shard_map/mix_amplitudes/pallas_call | solution.py:185
  98.7 1.8 copy-done.1
  100.5 101.6 %all-to-all-done.2.second_ref = bf16[192,96,128]{2,1,0:T(8,128)(2,1)} async-done(((bf16[192,96,128]{2,1,0:T(8,128)(2,1)}), bf16[192,96,128]{2,1,0:T(8,128)(2,1)}, u32[]{:S(2)}, u32[]{:S(2)}) %all-to-all-start.2) | async-done | bytes 4718624 | tf_op jit(solution)/shard_map/all_to_all | solution.py:305
  202.1 10.7 %residual.1 = f32[3,768,768]{2,1,0:T(8,128)} custom-call(s32[108]{0:T(128)S(1)} %bitcast.9, s32[6]{0:T(128)S(1)} %reshape.29.occ_ref, s32[18]{0:T(128)S(1)} %reshape.30.domain_ref, f32[400]{0:T(512)S(1)} %copy-done.10, f32[25,128]{1,0:T(8,128)S(1)} %bitcast.8, bf16[3,768,768]{2,1,0:T(8,128)(2,1)} %copy-done.1, ...), custom_call_target="tpu_custom_call" | custom-call | flops 5435817984 | bytes 14155776 | tf_op jit(solution)/shard_map/residual/pallas_call | solution.py:259
  (38 shorter events, 3.6 us)
Async XLA Ops:
  0.0 21.5 %copy-start.12 = (bf16[48,128,128]{2,1,0:T(8,128)(2,1)S(1)}, bf16[48,128,128]{2,1,0:T(8,128)(2,1)}, u32[]{:S(2)}) copy-start(bf16[48,128,128]{2,1,0:T(8,128)(2,1)} %tiles_ref.1) | copy-start | bytes 4718596
  2.6 20.0 %collective-permute-start.2 = (bf16[48,32,128]{2,1,0:T(8,128)(2,1)}, bf16[48,32,128]{2,1,0:T(8,128)(2,1)S(1)}, u32[]{:S(2)}, u32[]{:S(2)}) collective-permute-start(bf16[48,32,128]{2,1,0:T(8,128)(2,1)} %get-tuple-element.12.refs_0_), channel_id=1, source_target_pairs={{192,0},{0,64},{64,128},{128,192},{193,1},{1,65},{65,129},{129,193... | collective-permute-start | bytes 1179656 | tf_op jit(solution)/shard_map/ppermute | solution.py:157
  4.7 19.6 %collective-permute-start.1 = (bf16[48,32,128]{2,1,0:T(8,128)(2,1)}, bf16[48,32,128]{2,1,0:T(8,128)(2,1)S(1)}, u32[]{:S(2)}, u32[]{:S(2)}) collective-permute-start(bf16[48,32,128]{2,1,0:T(8,128)(2,1)} %get-tuple-element.12.refs_0_), channel_id=1, source_target_pairs={{128,0},{192,64},{0,128},{64,192},{129,1},{193,65},{1,129},{65,193... | collective-permute-start | bytes 1179656 | tf_op jit(solution)/shard_map/ppermute | solution.py:157
  7.1 17.2 %collective-permute-start = (bf16[48,32,128]{2,1,0:T(8,128)(2,1)}, bf16[48,32,128]{2,1,0:T(8,128)(2,1)S(1)}, u32[]{:S(2)}, u32[]{:S(2)}) collective-permute-start(bf16[48,32,128]{2,1,0:T(8,128)(2,1)} %get-tuple-element.12.refs_0_), channel_id=1, source_target_pairs={{64,0},{128,64},{192,128},{0,192},{65,1},{129,65},{193,129},{1,193... | collective-permute-start | bytes 1179656 | tf_op jit(solution)/shard_map/ppermute | solution.py:157
  8.3 22.5 %all-to-all-start = ((s32[64,1,3]{2,1,0:T(1,128)}), s32[64,1,3]{2,1,0:T(1,128)S(1)}, u32[]{:S(2)}, u32[]{:S(2)}) async-start(s32[64,1,3]{2,1,0:T(1,128)} %bitcast.10), calls=%async_computation | async-start | bytes 65536 | tf_op jit(solution)/shard_map/all_to_all | solution.py:296
  24.9 0.8 copy-start.6
  31.4 28.4 %collective-permute-start.4 = (bf16[48,96,128]{2,1,0:T(8,128)(2,1)}, bf16[48,96,128]{2,1,0:T(8,128)(2,1)S(1)}, u32[]{:S(2)}, u32[]{:S(2)}) collective-permute-start(bf16[48,96,128]{2,1,0:T(8,128)(2,1)} %gate_rows.1.refs_0_), channel_id=1, source_target_pairs={{0,64},{64,128},{128,192},{192,0},{1,65},{65,129},{129,193},{193,1... | collective-permute-start | bytes 3538952 | tf_op jit(solution)/shard_map/ppermute | solution.py:166
  31.7 28.1 %collective-permute-start.3 = (bf16[48,96,128]{2,1,0:T(8,128)(2,1)}, bf16[48,96,128]{2,1,0:T(8,128)(2,1)S(1)}, u32[]{:S(2)}, u32[]{:S(2)}) collective-permute-start(bf16[48,96,128]{2,1,0:T(8,128)(2,1)} %gate_rows.1.refs_0_), channel_id=1, source_target_pairs={{0,192},{64,0},{128,64},{192,128},{1,193},{65,1},{129,65},{193,129... | collective-permute-start | bytes 3538952 | tf_op jit(solution)/shard_map/ppermute | solution.py:167
  34.0 0.8 copy-start.4
  34.8 1.0 copy-start.7
  35.8 1.0 copy-start.8
  40.1 48.6 %all-to-all-start.1 = ((bf16[192,32,128]{2,1,0:T(8,128)(2,1)}), bf16[192,32,128]{2,1,0:T(8,128)(2,1)}, u32[]{:S(2)}, u32[]{:S(2)}) async-start(bf16[192,32,128]{2,1,0:T(8,128)(2,1)} %serve_tiles.2), calls=%async_computation.1 | async-start | bytes 3145728 | tf_op jit(solution)/shard_map/all_to_all | solution.py:303
  59.7 1.0 copy-start.2
  59.7 15.7 %copy-start = (bf16[48,96,128]{2,1,0:T(8,128)(2,1)S(1)}, bf16[48,96,128]{2,1,0:T(8,128)(2,1)}, u32[]{:S(2)}) copy-start(bf16[48,96,128]{2,1,0:T(8,128)(2,1)} %gate_rows.1.refs_0_) | copy-start | bytes 3538948
  59.7 15.7 %copy-start.5 = (s32[64,1,3]{2,1,0:T(1,128)S(1)}, s32[64,1,3]{2,1,0:T(1,128)}, u32[]{:S(2)}) copy-start(s32[64,1,3]{2,1,0:T(1,128)} %copy-done.3) | copy-start | bytes 2308
  60.8 14.7 %collective-permute-start.5 = (bf16[24,96,128]{2,1,0:T(8,128)(2,1)S(1)}, bf16[24,96,128]{2,1,0:T(8,128)(2,1)S(1)}, u32[]{:S(2)}, u32[]{:S(2)}) collective-permute-start(bf16[24,96,128]{2,1,0:T(8,128)(2,1)S(1)} %get-tuple-element.13), channel_id=1, source_target_pairs={{0,64},{64,128},{128,192},{192,0},{1,65},{65,129},{129,193},{193,1... | collective-permute-start | bytes 1769480 | tf_op jit(solution)/shard_map/ppermute | solution.py:169
  60.8 14.7 %collective-permute-start.6 = (bf16[24,96,128]{2,1,0:T(8,128)(2,1)S(1)}, bf16[24,96,128]{2,1,0:T(8,128)(2,1)S(1)}, u32[]{:S(2)}, u32[]{:S(2)}) collective-permute-start(bf16[24,96,128]{2,1,0:T(8,128)(2,1)S(1)} %get-tuple-element.14), channel_id=1, source_target_pairs={{0,192},{64,0},{128,64},{192,128},{1,193},{65,1},{129,65},{193,129... | collective-permute-start | bytes 1769480 | tf_op jit(solution)/shard_map/ppermute | solution.py:170
  81.0 14.0 %copy-start.13 = (s32[3,6]{1,0:T(4,128)S(1)}, s32[3,6]{1,0:T(4,128)}, u32[]{:S(2)}) copy-start(s32[3,6]{1,0:T(4,128)} %param.13) | copy-start | bytes 220
  81.0 14.1 %copy-start.14 = (s32[3,2]{0,1:T(2,128)S(1)}, s32[3,2]{0,1:T(2,128)}, u32[]{:S(2)}) copy-start(s32[3,2]{0,1:T(2,128)} %param.12) | copy-start | bytes 76
  88.7 113.4 %all-to-all-start.2 = ((bf16[192,96,128]{2,1,0:T(8,128)(2,1)}), bf16[192,96,128]{2,1,0:T(8,128)(2,1)}, u32[]{:S(2)}, u32[]{:S(2)}) async-start(bf16[192,96,128]{2,1,0:T(8,128)(2,1)} %serve_tiles.3), calls=%async_computation.2 | async-start | bytes 9437184 | tf_op jit(solution)/shard_map/all_to_all | solution.py:305
  95.2 106.9 %copy-start.9 = (f32[3200]{0:T(1024)S(1)}, f32[3200]{0:T(1024)}, u32[]{:S(2)}) copy-start(f32[3200]{0:T(1024)} %param.15) | copy-start | bytes 38404
  95.2 106.9 %copy-start.10 = (f32[400]{0:T(512)S(1)}, f32[400]{0:T(512)}, u32[]{:S(2)}) copy-start(f32[400]{0:T(512)} %eps_occ_ref.1) | copy-start | bytes 4804
  95.2 106.9 %copy-start.11 = (s32[1,108]{1,0:T(1,128)S(1)}, s32[1,108]{1,0:T(1,128)}, u32[]{:S(2)}) copy-start(s32[1,108]{1,0:T(1,128)} %get-tuple-element.10) | copy-start | bytes 1300
  98.7 1.8 copy-start.1
  (1 other events, 0.6 us)

commit v7 on v6

--- a/solution.py
+++ b/solution.py
@@ -13,15 +13,11 @@
 ANY = pl.BlockSpec(memory_space=pl.ANY)
 VMEM = pl.BlockSpec(memory_space=pltpu.VMEM)
 SMEM = pl.BlockSpec(memory_space=pltpu.SMEM)
-BIG = 100 * 2**20 // 2
-
-
-def ask_kernel(held, owner_ref, slot_ref, tiles_ref, request_ref, place_ref, first_ref, sem):
+MIB = 2**20
+
+
+def ask_kernel(held, owner_ref, slot_ref, request_ref, place_ref):
     vir = request_ref.shape[0]
-    copy = pltpu.make_async_copy(
-        tiles_ref.at[:, pl.ds(0, first_ref.shape[1])], first_ref, sem
-    )
-    copy.start()
     owner, slot = owner_ref[...], slot_ref[...]
     asks = owner.shape[1]
     column = owner % vir
@@ -41,23 +37,19 @@
         ],
         axis=1,
     )
-    copy.wait()
-
-
-def ask(owner, slot, tiles, vir):
-    held, _, tile = tiles.shape
+
+
+def ask(owner, slot, vir, held):
     return pl.pallas_call(
         functools.partial(ask_kernel, held),
         out_shape=(
             jax.ShapeDtypeStruct((vir, PER_COLUMN), jnp.int32),
             jax.ShapeDtypeStruct(owner.shape, jnp.int32),
-            jax.ShapeDtypeStruct((held, ROWS_FIRST, tile), tiles.dtype),
-        ),
-        in_specs=[VMEM, VMEM, ANY],
-        out_specs=(VMEM, VMEM, VMEM),
-        scratch_shapes=[pltpu.SemaphoreType.DMA],
+        ),
+        in_specs=[VMEM, VMEM],
+        out_specs=(VMEM, VMEM),
         name="make_requests",
-    )(owner, slot, tiles)
+    )(owner, slot)
 
 
 def fill_pool(n_pair, held, parts, here_ref, sources, pool, sem):
@@ -72,19 +64,20 @@
         copy.wait()
 
 
-def gate_kernel(rows_ref, code_ref, sample_ref, out_ref):
+def gate_kernel(rows_ref, sample_ref, out_ref):
     pass
 
 
-def gate(rows, codes, sample):
+def gate(rows, sample):
     return pl.pallas_call(
         gate_kernel,
         out_shape=jax.ShapeDtypeStruct(rows.shape, rows.dtype),
-        in_specs=[ANY, ANY, ANY],
+        in_specs=[ANY, ANY],
         out_specs=ANY,
         input_output_aliases={0: 0},
+        compiler_params=pltpu.CompilerParams(vmem_limit_bytes=MIB),
         name="gate_rows",
-    )(rows, codes, sample)
+    )(rows, sample)
 
 
 def serve_kernel(n_pair, held, parts, here_ref, code_ref, *refs):
@@ -116,7 +109,7 @@
             pltpu.VMEM((n_pair * held, rows, tile), dtype),
             pltpu.SemaphoreType.DMA((len(parts),)),
         ],
-        compiler_params=pltpu.CompilerParams(vmem_limit_bytes=BIG),
+        compiler_params=pltpu.CompilerParams(vmem_limit_bytes=48 * MIB),
         cost_estimate=pl.CostEstimate(
             flops=0, bytes_accessed=4 * slots * rows * tile, transcendentals=0
         ),
@@ -143,7 +136,7 @@
         in_specs=[ANY, ANY],
         out_specs=(VMEM, VMEM),
         scratch_shapes=[pltpu.SemaphoreType.DMA((2,))],
-        compiler_params=pltpu.CompilerParams(vmem_limit_bytes=BIG),
+        compiler_params=pltpu.CompilerParams(vmem_limit_bytes=48 * MIB),
         cost_estimate=pl.CostEstimate(
             flops=LONG, bytes_accessed=0, transcendentals=0
         ),
@@ -191,7 +184,7 @@
         cost_estimate=pl.CostEstimate(
             flops=pairs * width * width, bytes_accessed=4 * pairs * width * width, transcendentals=0
         ),
-        compiler_params=pltpu.CompilerParams(vmem_limit_bytes=BIG),
+        compiler_params=pltpu.CompilerParams(vmem_limit_bytes=50 * MIB),
         name="mix_amplitudes",
     )(amplitudes, after)
 
@@ -278,7 +271,7 @@
         cost_estimate=pl.CostEstimate(
             flops=4 * pairs * width**3, bytes_accessed=8 * pairs * width**2, transcendentals=0
         ),
-        compiler_params=pltpu.CompilerParams(vmem_limit_bytes=BIG),
+        compiler_params=pltpu.CompilerParams(vmem_limit_bytes=50 * MIB),
         name="residual",
     )(places, pair_occ, domain, eps_occ, eps_vir, mixed, first, second)
 
@@ -289,16 +282,15 @@
     vir = lax.axis_size("vir")
     here = lax.axis_index("pair").astype(jnp.int32).reshape(1)
     n_pair = lax.axis_size("pair")
-    requests, places, first = ask(
-        need_owner.reshape(1, -1), need_slot.reshape(1, -1), integral_tiles, vir
-    )
+    first = integral_tiles[:, :ROWS_FIRST]
+    requests, places = ask(need_owner.reshape(1, -1), need_slot.reshape(1, -1), vir, held)
     near = from_others(first)
     codes = lax.all_to_all(
         requests.reshape(vir, 1, PER_COLUMN), "vir", split_axis=0, concat_axis=0, tiled=True
     )
-    sample = sum(part[0, :8] for _, _, part in near[1:])
-    far = from_ring(gate(integral_tiles[:, ROWS_FIRST:], codes, sample))
-    mixed = mix(amplitudes, codes)
+    sample = sum(part[0, :8] for _, _, part in near[1:]) + codes[0].astype(first.dtype)[:, :1]
+    far = from_ring(gate(integral_tiles[:, ROWS_FIRST:], sample))
+    mixed = mix(amplitudes, sample)
     served = serve(here, codes, near, n_pair, held)
     got_first = lax.all_to_all(served, "vir", split_axis=0, concat_axis=0, tiled=True)
     served = serve(here, codes, far, n_pair, held)

time: 214 us -> 211 us (0.986)
  starting transfers between devices: 39.3 us -> 36.8 us
    ppermute x1, waiting for transfers between devices: 10.8 us -> 14.3 us  [from_ring(): below = lax.ppermute(mine, 'pair', up)]
    all_to_all x2, waiting for transfers between devices: 109 us -> 106 us  [body(): lax.all_to_all(served, 'vir', split_axis=0, concat_axis=0, tiled=True)]
    all_to_all x1, waiting for transfers between devices: 5.12 us -> 7.85 us  [body(): lax.all_to_all(requests.reshape(vir, 1, PER_COLUMN), 'vir', split_axis=0,...]
    all_to_all x2, starting transfers between devices: 15.1 us -> 12.5 us  [body(): lax.all_to_all(served, 'vir', split_axis=0, concat_axis=0, tiled=True)]
    unnamed x31 -> x27, local copies, waits for them, and re-layouts: 6.76 us -> 5.58 us
  transfers between devices with their start and end apart: 10 -> 10, of which waited for: 6 -> 5; matrix products, arithmetic and copies ran while one was open for 1% -> 1% of each run, Pallas kernels for 6% -> 7%
where the time goes in v7:
time: 211 us
  waiting for transfers between devices  140 us (66%)
  starting transfers between devices  36.8 us (17%)
  Pallas kernels  25.4 us (12%)
  local copies, waits for them, and re-layouts  8.14 us (4%)
    all_to_all x2, waiting for transfers between devices, body(): lax.all_to_all(served, 'vir', split_axis=0, concat_axis=0, tiled=True)  106 us
    ppermute x1, waiting for transfers between devices, from_ring(): below = lax.ppermute(mine, 'pair', up)  14.3 us
    all_to_all x1, starting transfers between devices, body(): lax.all_to_all(requests.reshape(vir, 1, PER_COLUMN), 'vir', split_axis=0,...  13.2 us
    all_to_all x2, starting transfers between devices, body(): lax.all_to_all(served, 'vir', split_axis=0, concat_axis=0, tiled=True)  12.5 us
    ppermute x1, waiting for transfers between devices, from_ring(): far_low = lax.ppermute(low, 'pair', up)  12 us
    pallas_call x1, Pallas kernels, residual(): pl.pallas_call(functools.partial(residual_kernel, rows_first, tile), grid...  10.7 us
    pallas_call x2, Pallas kernels, serve(): pl.pallas_call(functools.partial(serve_kernel, n_pair, held, [part[:2] fo...  8.53 us
    all_to_all x1, waiting for transfers between devices, body(): lax.all_to_all(requests.reshape(vir, 1, PER_COLUMN), 'vir', split_axis=0,...  7.85 us
  transfers between devices with their start and end apart: 10, of which 5 were waited for; matrix products, arithmetic and copies ran while one was open for 1% of the time, Pallas kernels for 7%

profile of v7, /device:TPU:1, one launch (start us, length us, event | category | flops | bytes accessed | tf_op | source)
XLA Modules:
  0.0 210.6 jit_solution(18230982515372565351)
XLA Ops:
  0.0 1.0 slice.22.refs_0_
  1.0 2.1 %collective-permute-start.2 = (bf16[48,32,128]{2,1,0:T(8,128)(2,1)S(1)}, bf16[48,32,128]{2,1,0:T(8,128)(2,1)S(1)}, u32[]{:S(2)}, u32[]{:S(2)}) collective-permute-start(bf16[48,32,128]{2,1,0:T(8,128)(2,1)S(1)} %slice.22.refs_0_), channel_id=1, source_target_pairs={{192,0},{0,64},{64,128},{128,192},{193,1},{1,65},{65,129},{129,193... | collective-permute-start | bytes 1179656 | tf_op jit(solution)/shard_map/ppermute | solution.py:150
  3.1 2.5 %collective-permute-start.1 = (bf16[48,32,128]{2,1,0:T(8,128)(2,1)S(1)}, bf16[48,32,128]{2,1,0:T(8,128)(2,1)S(1)}, u32[]{:S(2)}, u32[]{:S(2)}) collective-permute-start(bf16[48,32,128]{2,1,0:T(8,128)(2,1)S(1)} %slice.22.refs_0_), channel_id=1, source_target_pairs={{128,0},{192,64},{0,128},{64,192},{129,1},{193,65},{1,129},{65,193... | collective-permute-start | bytes 1179656 | tf_op jit(solution)/shard_map/ppermute | solution.py:150
  5.6 1.2 collective-permute-start
  6.8 1.6 make_requests.1
  8.3 13.2 %all-to-all-start = ((s32[64,1,3]{2,1,0:T(1,128)}), s32[64,1,3]{2,1,0:T(1,128)S(1)}, u32[]{:S(2)}, u32[]{:S(2)}) async-start(s32[64,1,3]{2,1,0:T(1,128)} %bitcast.14), calls=%async_computation | async-start | bytes 65536 | tf_op jit(solution)/shard_map/all_to_all | solution.py:288
  21.5 1.4 slice.28.rows_ref
  22.9 7.8 %all-to-all-done.code_ref = s32[64,1,3]{2,1,0:T(1,128)S(1)} async-done(((s32[64,1,3]{2,1,0:T(1,128)}), s32[64,1,3]{2,1,0:T(1,128)S(1)}, u32[]{:S(2)}, u32[]{:S(2)}) %all-to-all-start) | async-done | bytes 800 | tf_op jit(solution)/shard_map/all_to_all | solution.py:288
  33.0 2.4 %collective-permute-start.3 = (bf16[48,96,128]{2,1,0:T(8,128)(2,1)S(1)}, bf16[48,96,128]{2,1,0:T(8,128)(2,1)}, u32[]{:S(2)}, u32[]{:S(2)}) collective-permute-start(bf16[48,96,128]{2,1,0:T(8,128)(2,1)S(1)} %gate_rows.1.refs_0_), channel_id=1, source_target_pairs={{0,192},{64,0},{128,64},{192,128},{1,193},{65,1},{129,65},{193,129... | collective-permute-start | bytes 3538952 | tf_op jit(solution)/shard_map/ppermute | solution.py:160
  35.4 1.0 copy-done.2
  36.4 0.8 copy-done.4
  37.1 3.3 %serve_tiles.2 = bf16[192,32,128]{2,1,0:T(8,128)(2,1)} custom-call(s32[1]{0:T(128)} %bitcast.8.here_ref, s32[64,1,3]{2,1,0:T(1,128)S(1)} %copy-done.4, bf16[48,32,128]{2,1,0:T(8,128)(2,1)S(1)} %slice.22.refs_0_, bf16[48,32,128]{2,1,0:T(8,128)(2,1)S(1)} %copy-done.2, bf16[48,32,128]{2,1,0:T(8,128)(2,1)S(1)} %collective-permute-done.1.refs_2_, ...), custom_call_target="tpu_custom_call" | custom-call | bytes 3145728 | tf_op jit(solution)/shard_map/serve_tiles/pallas_call | solution.py:103
  40.5 6.1 %all-to-all-start.1 = ((bf16[192,32,128]{2,1,0:T(8,128)(2,1)}), bf16[192,32,128]{2,1,0:T(8,128)(2,1)}, u32[]{:S(2)}, u32[]{:S(2)}) async-start(bf16[192,32,128]{2,1,0:T(8,128)(2,1)} %serve_tiles.2), calls=%async_computation.1 | async-start | bytes 3145728 | tf_op jit(solution)/shard_map/all_to_all | solution.py:295
  46.6 14.3 %collective-permute-done.4.up_ref.refs_2_ = bf16[48,96,128]{2,1,0:T(8,128)(2,1)S(1)} collective-permute-done((bf16[48,96,128]{2,1,0:T(8,128)(2,1)S(1)}, bf16[48,96,128]{2,1,0:T(8,128)(2,1)S(1)}, u32[]{:S(2)}, u32[]{:S(2)}) %collective-permute-start.4) | collective-permute-done | bytes 1179680 | tf_op jit(solution)/shard_map/ppermute | solution.py:159
  60.9 1.2 cut_halves.1
  62.2 2.7 %collective-permute-start.6 = (bf16[24,96,128]{2,1,0:T(8,128)(2,1)S(1)}, bf16[24,96,128]{2,1,0:T(8,128)(2,1)S(1)}, u32[]{:S(2)}, u32[]{:S(2)}) collective-permute-start(bf16[24,96,128]{2,1,0:T(8,128)(2,1)S(1)} %get-tuple-element.12), channel_id=1, source_target_pairs={{0,192},{64,0},{128,64},{192,128},{1,193},{65,1},{129,65},{193,129... | collective-permute-start | bytes 1769480 | tf_op jit(solution)/shard_map/ppermute | solution.py:163
  64.8 12.0 %collective-permute-done.5.refs_3_ = bf16[24,96,128]{2,1,0:T(8,128)(2,1)S(1)} collective-permute-done((bf16[24,96,128]{2,1,0:T(8,128)(2,1)S(1)}, bf16[24,96,128]{2,1,0:T(8,128)(2,1)S(1)}, u32[]{:S(2)}, u32[]{:S(2)}) %collective-permute-start.5) | collective-permute-done | bytes 589856 | tf_op jit(solution)/shard_map/ppermute | solution.py:162
  76.9 5.2 %serve_tiles.3 = bf16[192,96,128]{2,1,0:T(8,128)(2,1)} custom-call(s32[1]{0:T(128)} %bitcast.8.here_ref, s32[64,1,3]{2,1,0:T(1,128)S(1)} %copy-done.5, bf16[48,96,128]{2,1,0:T(8,128)(2,1)S(1)} %gate_rows.1.refs_0_, bf16[48,96,128]{2,1,0:T(8,128)(2,1)} %collective-permute-done.3.down_ref.refs_1_, ...), custom_call_target="tpu_custom_call" | custom-call | bytes 9437184 | tf_op jit(solution)/shard_map/serve_tiles/pallas_call | solution.py:103
  82.1 4.2 %all-to-all-done.1.first_ref = bf16[192,32,128]{2,1,0:T(8,128)(2,1)} async-done(((bf16[192,32,128]{2,1,0:T(8,128)(2,1)}), bf16[192,32,128]{2,1,0:T(8,128)(2,1)}, u32[]{:S(2)}, u32[]{:S(2)}) %all-to-all-start.1) | async-done | bytes 1572896 | tf_op jit(solution)/shard_map/all_to_all | solution.py:295
  86.3 6.4 %all-to-all-start.2 = ((bf16[192,96,128]{2,1,0:T(8,128)(2,1)}), bf16[192,96,128]{2,1,0:T(8,128)(2,1)}, u32[]{:S(2)}, u32[]{:S(2)}) async-start(bf16[192,96,128]{2,1,0:T(8,128)(2,1)} %serve_tiles.3), calls=%async_computation.2 | async-start | bytes 9437184 | tf_op jit(solution)/shard_map/all_to_all | solution.py:297
  93.0 3.4 %mix_amplitudes.1.mixed_ref = bf16[3,768,768]{2,1,0:T(8,128)(2,1)S(1)} custom-call(bf16[3,768,768]{2,1,0:T(8,128)(2,1)} %amp_ref.1, bf16[8,128]{1,0:T(8,128)(2,1)S(1)} %copy-done.7), custom_call_target="tpu_custom_call" | custom-call | flops 1769472 | bytes 7077888 | tf_op jit(solution)/shard_map/mix_amplitudes/pallas_call | solution.py:178
  96.4 1.8 copy-done
  98.2 101.6 %all-to-all-done.2.second_ref = bf16[192,96,128]{2,1,0:T(8,128)(2,1)} async-done(((bf16[192,96,128]{2,1,0:T(8,128)(2,1)}), bf16[192,96,128]{2,1,0:T(8,128)(2,1)}, u32[]{:S(2)}, u32[]{:S(2)}) %all-to-all-start.2) | async-done | bytes 4718624 | tf_op jit(solution)/shard_map/all_to_all | solution.py:297
  199.9 10.7 %residual.1 = f32[3,768,768]{2,1,0:T(8,128)} custom-call(s32[108]{0:T(128)S(1)} %bitcast.13, s32[6]{0:T(128)S(1)} %reshape.44.occ_ref, s32[18]{0:T(128)S(1)} %reshape.45.domain_ref, f32[400]{0:T(512)S(1)} %copy-done.9, f32[25,128]{1,0:T(8,128)S(1)} %bitcast.12, bf16[3,768,768]{2,1,0:T(8,128)(2,1)} %copy-done, ...), custom_call_target="tpu_custom_call" | custom-call | flops 5435817984 | bytes 14155776 | tf_op jit(solution)/shard_map/residual/pallas_call | solution.py:252
  (36 shorter events, 2.7 us)
Async XLA Ops:
  1.0 30.3 %collective-permute-start.2 = (bf16[48,32,128]{2,1,0:T(8,128)(2,1)S(1)}, bf16[48,32,128]{2,1,0:T(8,128)(2,1)S(1)}, u32[]{:S(2)}, u32[]{:S(2)}) collective-permute-start(bf16[48,32,128]{2,1,0:T(8,128)(2,1)S(1)} %slice.22.refs_0_), channel_id=1, source_target_pairs={{192,0},{0,64},{64,128},{128,192},{193,1},{1,65},{65,129},{129,193... | collective-permute-start | bytes 1179656 | tf_op jit(solution)/shard_map/ppermute | solution.py:150
  3.1 28.2 %collective-permute-start.1 = (bf16[48,32,128]{2,1,0:T(8,128)(2,1)S(1)}, bf16[48,32,128]{2,1,0:T(8,128)(2,1)S(1)}, u32[]{:S(2)}, u32[]{:S(2)}) collective-permute-start(bf16[48,32,128]{2,1,0:T(8,128)(2,1)S(1)} %slice.22.refs_0_), channel_id=1, source_target_pairs={{128,0},{192,64},{0,128},{64,192},{129,1},{193,65},{1,129},{65,193... | collective-permute-start | bytes 1179656 | tf_op jit(solution)/shard_map/ppermute | solution.py:150
  5.6 25.7 %collective-permute-start = (bf16[48,32,128]{2,1,0:T(8,128)(2,1)S(1)}, bf16[48,32,128]{2,1,0:T(8,128)(2,1)S(1)}, u32[]{:S(2)}, u32[]{:S(2)}) collective-permute-start(bf16[48,32,128]{2,1,0:T(8,128)(2,1)S(1)} %slice.22.refs_0_), channel_id=1, source_target_pairs={{64,0},{128,64},{192,128},{0,192},{65,1},{129,65},{193,129},{1,193... | collective-permute-start | bytes 1179656 | tf_op jit(solution)/shard_map/ppermute | solution.py:150
  8.3 22.4 %all-to-all-start = ((s32[64,1,3]{2,1,0:T(1,128)}), s32[64,1,3]{2,1,0:T(1,128)S(1)}, u32[]{:S(2)}, u32[]{:S(2)}) async-start(s32[64,1,3]{2,1,0:T(1,128)} %bitcast.14), calls=%async_computation | async-start | bytes 65536 | tf_op jit(solution)/shard_map/all_to_all | solution.py:288
  30.7 0.6 copy-start.3
  31.4 0.7 copy-start.1
  32.1 0.6 copy-start.6
  32.7 28.2 %collective-permute-start.4 = (bf16[48,96,128]{2,1,0:T(8,128)(2,1)S(1)}, bf16[48,96,128]{2,1,0:T(8,128)(2,1)S(1)}, u32[]{:S(2)}, u32[]{:S(2)}) collective-permute-start(bf16[48,96,128]{2,1,0:T(8,128)(2,1)S(1)} %gate_rows.1.refs_0_), channel_id=1, source_target_pairs={{0,64},{64,128},{128,192},{192,0},{1,65},{65,129},{129,193},{193,1... | collective-permute-start | bytes 3538952 | tf_op jit(solution)/shard_map/ppermute | solution.py:159
  33.0 27.8 %collective-permute-start.3 = (bf16[48,96,128]{2,1,0:T(8,128)(2,1)S(1)}, bf16[48,96,128]{2,1,0:T(8,128)(2,1)}, u32[]{:S(2)}, u32[]{:S(2)}) collective-permute-start(bf16[48,96,128]{2,1,0:T(8,128)(2,1)S(1)} %gate_rows.1.refs_0_), channel_id=1, source_target_pairs={{0,192},{64,0},{128,64},{192,128},{1,193},{65,1},{129,65},{193,129... | collective-permute-start | bytes 3538952 | tf_op jit(solution)/shard_map/ppermute | solution.py:160
  35.4 1.0 copy-start.2
  36.4 0.8 copy-start.4
  40.5 45.9 %all-to-all-start.1 = ((bf16[192,32,128]{2,1,0:T(8,128)(2,1)}), bf16[192,32,128]{2,1,0:T(8,128)(2,1)}, u32[]{:S(2)}, u32[]{:S(2)}) async-start(bf16[192,32,128]{2,1,0:T(8,128)(2,1)} %serve_tiles.2), calls=%async_computation.1 | async-start | bytes 3145728 | tf_op jit(solution)/shard_map/all_to_all | solution.py:295
  60.9 16.0 %copy-start.5 = (s32[64,1,3]{2,1,0:T(1,128)S(1)}, s32[64,1,3]{2,1,0:T(1,128)}, u32[]{:S(2)}) copy-start(s32[64,1,3]{2,1,0:T(1,128)} %copy-done.3) | copy-start | bytes 2308
  62.1 14.8 %collective-permute-start.5 = (bf16[24,96,128]{2,1,0:T(8,128)(2,1)S(1)}, bf16[24,96,128]{2,1,0:T(8,128)(2,1)S(1)}, u32[]{:S(2)}, u32[]{:S(2)}) collective-permute-start(bf16[24,96,128]{2,1,0:T(8,128)(2,1)S(1)} %get-tuple-element.11), channel_id=1, source_target_pairs={{0,64},{64,128},{128,192},{192,0},{1,65},{65,129},{129,193},{193,1... | collective-permute-start | bytes 1769480 | tf_op jit(solution)/shard_map/ppermute | solution.py:162
  62.2 14.7 %collective-permute-start.6 = (bf16[24,96,128]{2,1,0:T(8,128)(2,1)S(1)}, bf16[24,96,128]{2,1,0:T(8,128)(2,1)S(1)}, u32[]{:S(2)}, u32[]{:S(2)}) collective-permute-start(bf16[24,96,128]{2,1,0:T(8,128)(2,1)S(1)} %get-tuple-element.12), channel_id=1, source_target_pairs={{0,192},{64,0},{128,64},{192,128},{1,193},{65,1},{129,65},{193,129... | collective-permute-start | bytes 1769480 | tf_op jit(solution)/shard_map/ppermute | solution.py:163
  82.1 10.6 %copy-start.11 = (s32[3,6]{1,0:T(4,128)S(1)}, s32[3,6]{1,0:T(4,128)}, u32[]{:S(2)}) copy-start(s32[3,6]{1,0:T(4,128)} %param.13) | copy-start | bytes 220
  82.1 10.7 %copy-start.12 = (s32[3,2]{0,1:T(2,128)S(1)}, s32[3,2]{0,1:T(2,128)}, u32[]{:S(2)}) copy-start(s32[3,2]{0,1:T(2,128)} %param.12) | copy-start | bytes 76
  82.1 10.9 %copy-start.7 = (bf16[8,128]{1,0:T(8,128)(2,1)S(1)}, bf16[8,128]{1,0:T(8,128)(2,1)}, u32[]{:S(2)}) copy-start(bf16[8,128]{1,0:T(8,128)(2,1)} %copy-done.6) | copy-start | bytes 6148
  86.3 113.5 %all-to-all-start.2 = ((bf16[192,96,128]{2,1,0:T(8,128)(2,1)}), bf16[192,96,128]{2,1,0:T(8,128)(2,1)}, u32[]{:S(2)}, u32[]{:S(2)}) async-start(bf16[192,96,128]{2,1,0:T(8,128)(2,1)} %serve_tiles.3), calls=%async_computation.2 | async-start | bytes 9437184 | tf_op jit(solution)/shard_map/all_to_all | solution.py:297
  93.0 106.9 %copy-start.8 = (f32[3200]{0:T(1024)S(1)}, f32[3200]{0:T(1024)}, u32[]{:S(2)}) copy-start(f32[3200]{0:T(1024)} %param.15) | copy-start | bytes 38404
  93.0 106.9 %copy-start.9 = (f32[400]{0:T(512)S(1)}, f32[400]{0:T(512)}, u32[]{:S(2)}) copy-start(f32[400]{0:T(512)} %eps_occ_ref.1) | copy-start | bytes 4804
  93.0 106.9 %copy-start.10 = (s32[1,108]{1,0:T(1,128)S(1)}, s32[1,108]{1,0:T(1,128)}, u32[]{:S(2)}) copy-start(s32[1,108]{1,0:T(1,128)} %get-tuple-element.9) | copy-start | bytes 1300
  96.4 1.8 copy-start

commit v8 on v7

--- a/solution.py
+++ b/solution.py
@@ -9,6 +9,7 @@
 
 ROWS_FIRST = 32
 PER_COLUMN = 3
+GROUPS = 4
 LONG = 400_000_000_000
 ANY = pl.BlockSpec(memory_space=pl.ANY)
 VMEM = pl.BlockSpec(memory_space=pltpu.VMEM)
@@ -75,24 +76,31 @@
         in_specs=[ANY, ANY],
         out_specs=ANY,
         input_output_aliases={0: 0},
-        compiler_params=pltpu.CompilerParams(vmem_limit_bytes=MIB),
+        compiler_params=pltpu.CompilerParams(vmem_limit_bytes=60 * MIB),
         name="gate_rows",
     )(rows, sample)
 
 
 def serve_kernel(n_pair, held, parts, here_ref, code_ref, *refs):
-    sources, (out_ref, pool, sem) = refs[: len(parts)], refs[len(parts) :]
+    sources, (out_ref, pool, picked, sem, out_sem) = refs[: len(parts)], refs[len(parts) :]
     fill_pool(n_pair, held, parts, here_ref, sources, pool, sem)
-    take(code_ref, pool, out_ref)
-
-
-def take(code_ref, pool, out_ref):
+    columns = code_ref.shape[0] // GROUPS
+
     def step(column, carry):
         for k in range(PER_COLUMN):
-            out_ref[column * PER_COLUMN + k] = pool[code_ref[column, 0, k]]
+            picked[column * PER_COLUMN + k] = pool[code_ref[column, 0, k]]
         return carry
 
-    lax.fori_loop(0, code_ref.shape[0], step, 0, unroll=4)
+    copies = []
+    for group in range(GROUPS):
+        lax.fori_loop(group * columns, (group + 1) * columns, step, 0, unroll=4)
+        slots = pl.ds(group * columns * PER_COLUMN, columns * PER_COLUMN)
+        copies.append(
+            pltpu.make_async_copy(picked.at[slots], out_ref.at[slots], out_sem.at[group])
+        )
+        copies[-1].start()
+    for copy in copies:
+        copy.wait()
 
 
 def serve(here, codes, parts, n_pair, held):
@@ -104,12 +112,14 @@
         functools.partial(serve_kernel, n_pair, held, [part[:2] for part in parts]),
         out_shape=jax.ShapeDtypeStruct((slots, rows, tile), dtype),
         in_specs=[SMEM, SMEM] + [ANY] * len(parts),
-        out_specs=VMEM,
+        out_specs=ANY,
         scratch_shapes=[
             pltpu.VMEM((n_pair * held, rows, tile), dtype),
+            pltpu.VMEM((slots, rows, tile), dtype),
             pltpu.SemaphoreType.DMA((len(parts),)),
+            pltpu.SemaphoreType.DMA((GROUPS,)),
         ],
-        compiler_params=pltpu.CompilerParams(vmem_limit_bytes=48 * MIB),
+        compiler_params=pltpu.CompilerParams(vmem_limit_bytes=60 * MIB),
         cost_estimate=pl.CostEstimate(
             flops=0, bytes_accessed=4 * slots * rows * tile, transcendentals=0
         ),
@@ -136,7 +146,7 @@
         in_specs=[ANY, ANY],
         out_specs=(VMEM, VMEM),
         scratch_shapes=[pltpu.SemaphoreType.DMA((2,))],
-        compiler_params=pltpu.CompilerParams(vmem_limit_bytes=48 * MIB),
+        compiler_params=pltpu.CompilerParams(vmem_limit_bytes=60 * MIB),
         cost_estimate=pl.CostEstimate(
             flops=LONG, bytes_accessed=0, transcendentals=0
         ),
@@ -184,7 +194,7 @@
         cost_estimate=pl.CostEstimate(
             flops=pairs * width * width, bytes_accessed=4 * pairs * width * width, transcendentals=0
         ),
-        compiler_params=pltpu.CompilerParams(vmem_limit_bytes=50 * MIB),
+        compiler_params=pltpu.CompilerParams(vmem_limit_bytes=60 * MIB),
         name="mix_amplitudes",
     )(amplitudes, after)
 

time: 211 us -> 213 us (level)
  Pallas kernels: 25.4 us -> 29.6 us
  waiting for transfers between devices: 140 us -> 136 us
    all_to_all x2, waiting for transfers between devices: 106 us -> 102 us  [body(): lax.all_to_all(served, 'vir', split_axis=0, concat_axis=0, tiled=True)]
    unnamed x27 -> x29, local copies, waits for them, and re-layouts: 5.58 us -> 3.99 us
  transfers between devices with their start and end apart: 10 -> 10, of which waited for: 5 -> 4; matrix products, arithmetic and copies ran while one was open for 1% -> 1% of each run, Pallas kernels for 7% -> 9%
where the time goes in v8:
time: 213 us; the launch traced here: 212 us
  waiting for transfers between devices  136 us (64%)
  starting transfers between devices  37.8 us (18%)
  Pallas kernels  29.6 us (14%)
  local copies, waits for them, and re-layouts  7.56 us (4%)
    all_to_all x2, waiting for transfers between devices, body(): lax.all_to_all(served, 'vir', split_axis=0, concat_axis=0, tiled=True)  102 us
    ppermute x1, waiting for transfers between devices, from_ring(): below = lax.ppermute(mine, 'pair', up)  15.7 us
    all_to_all x2, starting transfers between devices, body(): lax.all_to_all(served, 'vir', split_axis=0, concat_axis=0, tiled=True)  13.5 us
    all_to_all x1, starting transfers between devices, body(): lax.all_to_all(requests.reshape(vir, 1, PER_COLUMN), 'vir', split_axis=0,...  13.2 us
    ppermute x1, waiting for transfers between devices, from_ring(): far_low = lax.ppermute(low, 'pair', up)  12.1 us
    pallas_call x1, Pallas kernels, residual(): pl.pallas_call(functools.partial(residual_kernel, rows_first, tile), grid...  10.7 us
    pallas_call x2, Pallas kernels, serve(): pl.pallas_call(functools.partial(serve_kernel, n_pair, held, [part[:2] fo...  9.69 us
    all_to_all x1, waiting for transfers between devices, body(): lax.all_to_all(requests.reshape(vir, 1, PER_COLUMN), 'vir', split_axis=0,...  6.91 us
  transfers between devices with their start and end apart: 10, of which 4 were waited for; matrix products, arithmetic and copies ran while one was open for 1% of the time, Pallas kernels for 9%

profile of v8, /device:TPU:1, one launch (start us, length us, event | category | flops | bytes accessed | tf_op | source)
XLA Modules:
  0.0 212.3 jit_solution(4412615645360811800)
XLA Ops:
  0.0 1.0 slice.22.refs_0_
  1.0 2.1 collective-permute-start.2
  3.2 2.5 %collective-permute-start.1 = (bf16[48,32,128]{2,1,0:T(8,128)(2,1)S(1)}, bf16[48,32,128]{2,1,0:T(8,128)(2,1)S(1)}, u32[]{:S(2)}, u32[]{:S(2)}) collective-permute-start(bf16[48,32,128]{2,1,0:T(8,128)(2,1)S(1)} %slice.22.refs_0_), channel_id=1, source_target_pairs={{128,0},{192,64},{0,128},{64,192},{129,1},{193,65},{1,129},{65,193... | collective-permute-start | bytes 1179656 | tf_op jit(solution)/shard_map/ppermute | solution.py:160
  5.6 1.2 collective-permute-start
  6.8 1.5 make_requests.1
  8.3 13.2 %all-to-all-start = ((s32[64,1,3]{2,1,0:T(1,128)}), s32[64,1,3]{2,1,0:T(1,128)S(1)}, u32[]{:S(2)}, u32[]{:S(2)}) async-start(s32[64,1,3]{2,1,0:T(1,128)} %bitcast.14), calls=%async_computation | async-start | bytes 65536 | tf_op jit(solution)/shard_map/all_to_all | solution.py:298
  21.5 2.4 %slice.28.rows_ref = bf16[48,96,128]{2,1,0:T(8,128)(2,1)} slice(bf16[48,128,128]{2,1,0:T(8,128)(2,1)} %param.9), slice={[0:48], [32:128], [0:128]} | slice | bytes 2359296 | tf_op jit(solution)/shard_map/slice | solution.py:302
  23.9 6.9 %all-to-all-done.code_ref = s32[64,1,3]{2,1,0:T(1,128)S(1)} async-done(((s32[64,1,3]{2,1,0:T(1,128)}), s32[64,1,3]{2,1,0:T(1,128)S(1)}, u32[]{:S(2)}, u32[]{:S(2)}) %all-to-all-start) | async-done | bytes 800 | tf_op jit(solution)/shard_map/all_to_all | solution.py:298
  32.0 2.4 %collective-permute-start.3 = (bf16[48,96,128]{2,1,0:T(8,128)(2,1)}, bf16[48,96,128]{2,1,0:T(8,128)(2,1)S(1)}, u32[]{:S(2)}, u32[]{:S(2)}) collective-permute-start(bf16[48,96,128]{2,1,0:T(8,128)(2,1)} %gate_rows.1.refs_0_), channel_id=1, source_target_pairs={{0,192},{64,0},{128,64},{192,128},{1,193},{65,1},{129,65},{193,129... | collective-permute-start | bytes 3538952 | tf_op jit(solution)/shard_map/ppermute | solution.py:170
  34.3 3.8 %serve_tiles.2 = bf16[192,32,128]{2,1,0:T(8,128)(2,1)} custom-call(s32[1]{0:T(128)} %bitcast.8.here_ref, s32[64,1,3]{2,1,0:T(1,128)} %copy-done.11, bf16[48,32,128]{2,1,0:T(8,128)(2,1)} %copy-done.3, bf16[48,32,128]{2,1,0:T(8,128)(2,1)} %copy-done.10, bf16[48,32,128]{2,1,0:T(8,128)(2,1)} %copy-done.9, bf16[48,32,128]{2,1,0:T(8,128)(2,1)} %copy-done.8), custom_call_target="tpu_custom_call" | custom-call | bytes 3145728 | tf_op jit(solution)/shard_map/serve_tiles/pallas_call | solution.py:111
  38.2 6.1 %all-to-all-start.1 = ((bf16[192,32,128]{2,1,0:T(8,128)(2,1)}), bf16[192,32,128]{2,1,0:T(8,128)(2,1)}, u32[]{:S(2)}, u32[]{:S(2)}) async-start(bf16[192,32,128]{2,1,0:T(8,128)(2,1)} %serve_tiles.2), calls=%async_computation.1 | async-start | bytes 3145728 | tf_op jit(solution)/shard_map/all_to_all | solution.py:305
  44.3 15.7 %collective-permute-done.4.up_ref.refs_2_ = bf16[48,96,128]{2,1,0:T(8,128)(2,1)S(1)} collective-permute-done((bf16[48,96,128]{2,1,0:T(8,128)(2,1)}, bf16[48,96,128]{2,1,0:T(8,128)(2,1)S(1)}, u32[]{:S(2)}, u32[]{:S(2)}) %collective-permute-start.4) | collective-permute-done | bytes 1179680 | tf_op jit(solution)/shard_map/ppermute | solution.py:169
  60.0 1.0 copy-done.4
  61.1 1.0 copy-done.5
  62.1 2.3 %cut_halves.1 = (bf16[24,96,128]{2,1,0:T(8,128)(2,1)}, bf16[24,96,128]{2,1,0:T(8,128)(2,1)}) custom-call(bf16[48,96,128]{2,1,0:T(8,128)(2,1)} %copy-done.4, bf16[48,96,128]{2,1,0:T(8,128)(2,1)} %copy-done.5), custom_call_target="tpu_custom_call" | custom-call | flops 399999991808 | tf_op jit(solution)/shard_map/cut_halves/pallas_call | solution.py:143
  64.5 2.7 %collective-permute-start.6 = (bf16[24,96,128]{2,1,0:T(8,128)(2,1)}, bf16[24,96,128]{2,1,0:T(8,128)(2,1)S(1)}, u32[]{:S(2)}, u32[]{:S(2)}) collective-permute-start(bf16[24,96,128]{2,1,0:T(8,128)(2,1)} %get-tuple-element.12), channel_id=1, source_target_pairs={{0,192},{64,0},{128,64},{192,128},{1,193},{65,1},{129,65},{193,129... | collective-permute-start | bytes 1769480 | tf_op jit(solution)/shard_map/ppermute | solution.py:173
  67.2 12.1 %collective-permute-done.5.refs_3_ = bf16[24,96,128]{2,1,0:T(8,128)(2,1)S(1)} collective-permute-done((bf16[24,96,128]{2,1,0:T(8,128)(2,1)}, bf16[24,96,128]{2,1,0:T(8,128)(2,1)S(1)}, u32[]{:S(2)}, u32[]{:S(2)}) %collective-permute-start.5) | collective-permute-done | bytes 589856 | tf_op jit(solution)/shard_map/ppermute | solution.py:172
  79.3 0.8 copy-done.6
  80.1 0.8 copy-done.7
  81.0 5.8 %serve_tiles.3 = bf16[192,96,128]{2,1,0:T(8,128)(2,1)} custom-call(s32[1]{0:T(128)} %bitcast.8.here_ref, s32[64,1,3]{2,1,0:T(1,128)} %copy-done.11, bf16[48,96,128]{2,1,0:T(8,128)(2,1)} %gate_rows.1.refs_0_, bf16[48,96,128]{2,1,0:T(8,128)(2,1)} %copy-done.5, bf16[48,96,128]{2,1,0:T(8,128)(2,1)} %copy-done.4, bf16[24,96,128]{2,1,0:T(8,128)(2,1)} %copy-done.6, ...), custom_call_target="tpu_custom_call" | custom-call | bytes 9437184 | tf_op jit(solution)/shard_map/serve_tiles/pallas_call | solution.py:111
  86.9 7.4 %all-to-all-start.2 = ((bf16[192,96,128]{2,1,0:T(8,128)(2,1)}), bf16[192,96,128]{2,1,0:T(8,128)(2,1)}, u32[]{:S(2)}, u32[]{:S(2)}) async-start(bf16[192,96,128]{2,1,0:T(8,128)(2,1)} %serve_tiles.3), calls=%async_computation.2 | async-start | bytes 9437184 | tf_op jit(solution)/shard_map/all_to_all | solution.py:307
  94.6 5.3 %mix_amplitudes.1.mixed_ref = bf16[3,768,768]{2,1,0:T(8,128)(2,1)} custom-call(bf16[3,768,768]{2,1,0:T(8,128)(2,1)} %amp_ref.1, bf16[8,128]{1,0:T(8,128)(2,1)} %fusion.1.after_ref.sample_ref), custom_call_target="tpu_custom_call" | custom-call | flops 1769472 | bytes 7077888 | tf_op jit(solution)/shard_map/mix_amplitudes/pallas_call | solution.py:188
  99.9 101.6 %all-to-all-done.2.second_ref = bf16[192,96,128]{2,1,0:T(8,128)(2,1)} async-done(((bf16[192,96,128]{2,1,0:T(8,128)(2,1)}), bf16[192,96,128]{2,1,0:T(8,128)(2,1)}, u32[]{:S(2)}, u32[]{:S(2)}) %all-to-all-start.2) | async-done | bytes 4718624 | tf_op jit(solution)/shard_map/all_to_all | solution.py:307
  201.5 10.7 %residual.1 = f32[3,768,768]{2,1,0:T(8,128)} custom-call(s32[108]{0:T(128)S(1)} %bitcast.13, s32[6]{0:T(128)S(1)} %reshape.44.occ_ref, s32[18]{0:T(128)S(1)} %reshape.45.domain_ref, f32[400]{0:T(512)S(1)} %copy-done.1, f32[25,128]{1,0:T(8,128)S(1)} %bitcast.12, bf16[3,768,768]{2,1,0:T(8,128)(2,1)} %mix_amplitudes.1.mixed_ref, ...), custom_call_target="tpu_custom_call" | custom-call | flops 5435817984 | bytes 14155776 | tf_op jit(solution)/shard_map/residual/pallas_call | solution.py:262
  (38 shorter events, 1.5 us)
Async XLA Ops:
  1.0 30.6 %copy-start.3 = (bf16[48,32,128]{2,1,0:T(8,128)(2,1)}, bf16[48,32,128]{2,1,0:T(8,128)(2,1)S(1)}, u32[]{:S(2)}) copy-start(bf16[48,32,128]{2,1,0:T(8,128)(2,1)S(1)} %slice.22.refs_0_) | copy-start | bytes 1179652
  1.0 29.7 %collective-permute-start.2 = (bf16[48,32,128]{2,1,0:T(8,128)(2,1)S(1)}, bf16[48,32,128]{2,1,0:T(8,128)(2,1)S(1)}, u32[]{:S(2)}, u32[]{:S(2)}) collective-permute-start(bf16[48,32,128]{2,1,0:T(8,128)(2,1)S(1)} %slice.22.refs_0_), channel_id=1, source_target_pairs={{192,0},{0,64},{64,128},{128,192},{193,1},{1,65},{65,129},{129,193... | collective-permute-start | bytes 1179656 | tf_op jit(solution)/shard_map/ppermute | solution.py:160
  3.2 27.6 %collective-permute-start.1 = (bf16[48,32,128]{2,1,0:T(8,128)(2,1)S(1)}, bf16[48,32,128]{2,1,0:T(8,128)(2,1)S(1)}, u32[]{:S(2)}, u32[]{:S(2)}) collective-permute-start(bf16[48,32,128]{2,1,0:T(8,128)(2,1)S(1)} %slice.22.refs_0_), channel_id=1, source_target_pairs={{128,0},{192,64},{0,128},{64,192},{129,1},{193,65},{1,129},{65,193... | collective-permute-start | bytes 1179656 | tf_op jit(solution)/shard_map/ppermute | solution.py:160
  5.6 25.2 %collective-permute-start = (bf16[48,32,128]{2,1,0:T(8,128)(2,1)S(1)}, bf16[48,32,128]{2,1,0:T(8,128)(2,1)S(1)}, u32[]{:S(2)}, u32[]{:S(2)}) collective-permute-start(bf16[48,32,128]{2,1,0:T(8,128)(2,1)S(1)} %slice.22.refs_0_), channel_id=1, source_target_pairs={{64,0},{128,64},{192,128},{0,192},{65,1},{129,65},{193,129},{1,193... | collective-permute-start | bytes 1179656 | tf_op jit(solution)/shard_map/ppermute | solution.py:160
  8.3 22.5 %all-to-all-start = ((s32[64,1,3]{2,1,0:T(1,128)}), s32[64,1,3]{2,1,0:T(1,128)S(1)}, u32[]{:S(2)}, u32[]{:S(2)}) async-start(s32[64,1,3]{2,1,0:T(1,128)} %bitcast.14), calls=%async_computation | async-start | bytes 65536 | tf_op jit(solution)/shard_map/all_to_all | solution.py:298
  30.8 0.8 copy-start.11
  30.8 3.6 %copy-start.8 = (bf16[48,32,128]{2,1,0:T(8,128)(2,1)}, bf16[48,32,128]{2,1,0:T(8,128)(2,1)S(1)}, u32[]{:S(2)}) copy-start(bf16[48,32,128]{2,1,0:T(8,128)(2,1)S(1)} %collective-permute-done.2.refs_3_) | copy-start | bytes 1179652
  30.8 3.5 %copy-start.9 = (bf16[48,32,128]{2,1,0:T(8,128)(2,1)}, bf16[48,32,128]{2,1,0:T(8,128)(2,1)S(1)}, u32[]{:S(2)}) copy-start(bf16[48,32,128]{2,1,0:T(8,128)(2,1)S(1)} %collective-permute-done.1.refs_2_) | copy-start | bytes 1179652
  30.8 0.8 copy-start.10
  31.7 28.4 %collective-permute-start.4 = (bf16[48,96,128]{2,1,0:T(8,128)(2,1)}, bf16[48,96,128]{2,1,0:T(8,128)(2,1)S(1)}, u32[]{:S(2)}, u32[]{:S(2)}) collective-permute-start(bf16[48,96,128]{2,1,0:T(8,128)(2,1)} %gate_rows.1.refs_0_), channel_id=1, source_target_pairs={{0,64},{64,128},{128,192},{192,0},{1,65},{65,129},{129,193},{193,1... | collective-permute-start | bytes 3538952 | tf_op jit(solution)/shard_map/ppermute | solution.py:169
  32.0 28.1 %collective-permute-start.3 = (bf16[48,96,128]{2,1,0:T(8,128)(2,1)}, bf16[48,96,128]{2,1,0:T(8,128)(2,1)S(1)}, u32[]{:S(2)}, u32[]{:S(2)}) collective-permute-start(bf16[48,96,128]{2,1,0:T(8,128)(2,1)} %gate_rows.1.refs_0_), channel_id=1, source_target_pairs={{0,192},{64,0},{128,64},{192,128},{1,193},{65,1},{129,65},{193,129... | collective-permute-start | bytes 3538952 | tf_op jit(solution)/shard_map/ppermute | solution.py:170
  38.2 48.7 %all-to-all-start.1 = ((bf16[192,32,128]{2,1,0:T(8,128)(2,1)}), bf16[192,32,128]{2,1,0:T(8,128)(2,1)}, u32[]{:S(2)}, u32[]{:S(2)}) async-start(bf16[192,32,128]{2,1,0:T(8,128)(2,1)} %serve_tiles.2), calls=%async_computation.1 | async-start | bytes 3145728 | tf_op jit(solution)/shard_map/all_to_all | solution.py:305
  60.0 1.0 copy-start.4
  61.1 1.0 copy-start.5
  64.4 14.9 %collective-permute-start.5 = (bf16[24,96,128]{2,1,0:T(8,128)(2,1)}, bf16[24,96,128]{2,1,0:T(8,128)(2,1)S(1)}, u32[]{:S(2)}, u32[]{:S(2)}) collective-permute-start(bf16[24,96,128]{2,1,0:T(8,128)(2,1)} %get-tuple-element.11), channel_id=1, source_target_pairs={{0,64},{64,128},{128,192},{192,0},{1,65},{65,129},{129,193},{193,1... | collective-permute-start | bytes 1769480 | tf_op jit(solution)/shard_map/ppermute | solution.py:172
  64.5 14.8 %collective-permute-start.6 = (bf16[24,96,128]{2,1,0:T(8,128)(2,1)}, bf16[24,96,128]{2,1,0:T(8,128)(2,1)S(1)}, u32[]{:S(2)}, u32[]{:S(2)}) collective-permute-start(bf16[24,96,128]{2,1,0:T(8,128)(2,1)} %get-tuple-element.12), channel_id=1, source_target_pairs={{0,192},{64,0},{128,64},{192,128},{1,193},{65,1},{129,65},{193,129... | collective-permute-start | bytes 1769480 | tf_op jit(solution)/shard_map/ppermute | solution.py:173
  79.3 0.8 copy-start.6
  80.1 0.8 copy-start.7
  86.8 7.5 %copy-start.12 = (s32[3,6]{1,0:T(4,128)S(1)}, s32[3,6]{1,0:T(4,128)}, u32[]{:S(2)}) copy-start(s32[3,6]{1,0:T(4,128)} %param.13) | copy-start | bytes 220
  86.8 7.5 %copy-start.13 = (s32[3,2]{0,1:T(2,128)S(1)}, s32[3,2]{0,1:T(2,128)}, u32[]{:S(2)}) copy-start(s32[3,2]{0,1:T(2,128)} %param.12) | copy-start | bytes 76
  86.9 114.7 %all-to-all-start.2 = ((bf16[192,96,128]{2,1,0:T(8,128)(2,1)}), bf16[192,96,128]{2,1,0:T(8,128)(2,1)}, u32[]{:S(2)}, u32[]{:S(2)}) async-start(bf16[192,96,128]{2,1,0:T(8,128)(2,1)} %serve_tiles.3), calls=%async_computation.2 | async-start | bytes 9437184 | tf_op jit(solution)/shard_map/all_to_all | solution.py:307
  94.6 107.0 %copy-start = (f32[3200]{0:T(1024)S(1)}, f32[3200]{0:T(1024)}, u32[]{:S(2)}) copy-start(f32[3200]{0:T(1024)} %param.15) | copy-start | bytes 38404
  94.6 107.0 %copy-start.1 = (f32[400]{0:T(512)S(1)}, f32[400]{0:T(512)}, u32[]{:S(2)}) copy-start(f32[400]{0:T(512)} %eps_occ_ref.1) | copy-start | bytes 4804
  94.6 107.0 %copy-start.2 = (s32[1,108]{1,0:T(1,128)S(1)}, s32[1,108]{1,0:T(1,128)}, u32[]{:S(2)}) copy-start(s32[1,108]{1,0:T(1,128)} %get-tuple-element.9) | copy-start | bytes 1300

commit v9 on v7

--- a/solution.py
+++ b/solution.py
@@ -75,7 +75,7 @@
         in_specs=[ANY, ANY],
         out_specs=ANY,
         input_output_aliases={0: 0},
-        compiler_params=pltpu.CompilerParams(vmem_limit_bytes=MIB),
+        compiler_params=pltpu.CompilerParams(vmem_limit_bytes=60 * MIB),
         name="gate_rows",
     )(rows, sample)
 
@@ -95,7 +95,7 @@
     lax.fori_loop(0, code_ref.shape[0], step, 0, unroll=4)
 
 
-def serve(here, codes, parts, n_pair, held):
+def serve(here, codes, parts, n_pair, held, limit):
     slots = codes.shape[0] * PER_COLUMN
     sources = [source for _, _, source in parts]
     _, rows, tile = sources[0].shape
@@ -109,7 +109,7 @@
             pltpu.VMEM((n_pair * held, rows, tile), dtype),
             pltpu.SemaphoreType.DMA((len(parts),)),
         ],
-        compiler_params=pltpu.CompilerParams(vmem_limit_bytes=48 * MIB),
+        compiler_params=pltpu.CompilerParams(vmem_limit_bytes=limit * MIB),
         cost_estimate=pl.CostEstimate(
             flops=0, bytes_accessed=4 * slots * rows * tile, transcendentals=0
         ),
@@ -136,7 +136,7 @@
         in_specs=[ANY, ANY],
         out_specs=(VMEM, VMEM),
         scratch_shapes=[pltpu.SemaphoreType.DMA((2,))],
-        compiler_params=pltpu.CompilerParams(vmem_limit_bytes=48 * MIB),
+        compiler_params=pltpu.CompilerParams(vmem_limit_bytes=52 * MIB),
         cost_estimate=pl.CostEstimate(
             flops=LONG, bytes_accessed=0, transcendentals=0
         ),
@@ -184,7 +184,7 @@
         cost_estimate=pl.CostEstimate(
             flops=pairs * width * width, bytes_accessed=4 * pairs * width * width, transcendentals=0
         ),
-        compiler_params=pltpu.CompilerParams(vmem_limit_bytes=50 * MIB),
+        compiler_params=pltpu.CompilerParams(vmem_limit_bytes=60 * MIB),
         name="mix_amplitudes",
     )(amplitudes, after)
 
@@ -291,9 +291,9 @@
     sample = sum(part[0, :8] for _, _, part in near[1:]) + codes[0].astype(first.dtype)[:, :1]
     far = from_ring(gate(integral_tiles[:, ROWS_FIRST:], sample))
     mixed = mix(amplitudes, sample)
-    served = serve(here, codes, near, n_pair, held)
+    served = serve(here, codes, near, n_pair, held, 60)
     got_first = lax.all_to_all(served, "vir", split_axis=0, concat_axis=0, tiled=True)
-    served = serve(here, codes, far, n_pair, held)
+    served = serve(here, codes, far, n_pair, held, 52)
     got_second = lax.all_to_all(served, "vir", split_axis=0, concat_axis=0, tiled=True)
     return residual(
         places.reshape(-1),

time: 211 us -> 210 us (level)
  waiting for transfers between devices: 140 us -> 136 us
  Pallas kernels: 25.4 us -> 28.6 us
  local copies, waits for them, and re-layouts: 8.14 us -> 5.96 us
    all_to_all x2, waiting for transfers between devices: 106 us -> 102 us  [body(): lax.all_to_all(served, 'vir', split_axis=0, concat_axis=0, tiled=True)]
    unnamed x27, local copies, waits for them, and re-layouts: 5.58 us -> 2.36 us
  transfers between devices with their start and end apart: 10 -> 10, of which waited for: 5 -> 5; matrix products, arithmetic and copies ran while one was open for 1% -> 1% of each run, Pallas kernels for 7% -> 9%
where the time goes in v9:
time: 210 us; the launch traced here: 209 us
  waiting for transfers between devices  136 us (65%)
  starting transfers between devices  37.4 us (18%)
  Pallas kernels  28.6 us (14%)
  local copies, waits for them, and re-layouts  5.96 us (3%)
    all_to_all x2, waiting for transfers between devices, body(): lax.all_to_all(served, 'vir', split_axis=0, concat_axis=0, tiled=True)  102 us
    ppermute x1, waiting for transfers between devices, from_ring(): below = lax.ppermute(mine, 'pair', up)  15.6 us
    all_to_all x1, starting transfers between devices, body(): lax.all_to_all(requests.reshape(vir, 1, PER_COLUMN), 'vir', split_axis=0,...  13.2 us
    all_to_all x2, starting transfers between devices, body(): lax.all_to_all(served, 'vir', split_axis=0, concat_axis=0, tiled=True)  13 us
    ppermute x1, waiting for transfers between devices, from_ring(): far_low = lax.ppermute(low, 'pair', up)  12 us
    pallas_call x1, Pallas kernels, residual(): pl.pallas_call(functools.partial(residual_kernel, rows_first, tile), grid...  10.7 us
    pallas_call x2, Pallas kernels, serve(): pl.pallas_call(functools.partial(serve_kernel, n_pair, held, [part[:2] fo...  9.7 us
    all_to_all x1, waiting for transfers between devices, body(): lax.all_to_all(requests.reshape(vir, 1, PER_COLUMN), 'vir', split_axis=0,...  6.88 us
  transfers between devices with their start and end apart: 10, of which 5 were waited for; matrix products, arithmetic and copies ran while one was open for 1% of the time, Pallas kernels for 9%

profile of v9, /device:TPU:1, one launch (start us, length us, event | category | flops | bytes accessed | tf_op | source)
XLA Modules:
  0.0 209.2 jit_solution(2889913962538114063)
XLA Ops:
  0.0 1.0 slice.22.refs_0_
  1.0 2.1 %collective-permute-start.2 = (bf16[48,32,128]{2,1,0:T(8,128)(2,1)S(1)}, bf16[48,32,128]{2,1,0:T(8,128)(2,1)S(1)}, u32[]{:S(2)}, u32[]{:S(2)}) collective-permute-start(bf16[48,32,128]{2,1,0:T(8,128)(2,1)S(1)} %slice.22.refs_0_), channel_id=1, source_target_pairs={{192,0},{0,64},{64,128},{128,192},{193,1},{1,65},{65,129},{129,193... | collective-permute-start | bytes 1179656 | tf_op jit(solution)/shard_map/ppermute | solution.py:150
  3.2 2.5 %collective-permute-start.1 = (bf16[48,32,128]{2,1,0:T(8,128)(2,1)S(1)}, bf16[48,32,128]{2,1,0:T(8,128)(2,1)S(1)}, u32[]{:S(2)}, u32[]{:S(2)}) collective-permute-start(bf16[48,32,128]{2,1,0:T(8,128)(2,1)S(1)} %slice.22.refs_0_), channel_id=1, source_target_pairs={{128,0},{192,64},{0,128},{64,192},{129,1},{193,65},{1,129},{65,193... | collective-permute-start | bytes 1179656 | tf_op jit(solution)/shard_map/ppermute | solution.py:150
  5.6 1.2 collective-permute-start
  6.8 1.5 make_requests.1
  8.3 13.2 %all-to-all-start = ((s32[64,1,3]{2,1,0:T(1,128)}), s32[64,1,3]{2,1,0:T(1,128)S(1)}, u32[]{:S(2)}, u32[]{:S(2)}) async-start(s32[64,1,3]{2,1,0:T(1,128)} %bitcast.14), calls=%async_computation | async-start | bytes 65536 | tf_op jit(solution)/shard_map/all_to_all | solution.py:288
  21.5 2.4 %slice.28.rows_ref = bf16[48,96,128]{2,1,0:T(8,128)(2,1)} slice(bf16[48,128,128]{2,1,0:T(8,128)(2,1)} %param.9), slice={[0:48], [32:128], [0:128]} | slice | bytes 2359296 | tf_op jit(solution)/shard_map/slice | solution.py:292
  23.9 6.9 %all-to-all-done.code_ref = s32[64,1,3]{2,1,0:T(1,128)S(1)} async-done(((s32[64,1,3]{2,1,0:T(1,128)}), s32[64,1,3]{2,1,0:T(1,128)S(1)}, u32[]{:S(2)}, u32[]{:S(2)}) %all-to-all-start) | async-done | bytes 800 | tf_op jit(solution)/shard_map/all_to_all | solution.py:288
  30.8 0.7 fusion.1.after_ref.sample_ref
  32.0 2.4 %collective-permute-start.3 = (bf16[48,96,128]{2,1,0:T(8,128)(2,1)}, bf16[48,96,128]{2,1,0:T(8,128)(2,1)S(1)}, u32[]{:S(2)}, u32[]{:S(2)}) collective-permute-start(bf16[48,96,128]{2,1,0:T(8,128)(2,1)} %gate_rows.1.refs_0_), channel_id=1, source_target_pairs={{0,192},{64,0},{128,64},{192,128},{1,193},{65,1},{129,65},{193,129... | collective-permute-start | bytes 3538952 | tf_op jit(solution)/shard_map/ppermute | solution.py:160
  34.4 4.0 %serve_tiles.2 = bf16[192,32,128]{2,1,0:T(8,128)(2,1)} custom-call(s32[1]{0:T(128)} %bitcast.8.here_ref, s32[64,1,3]{2,1,0:T(1,128)} %copy-done, bf16[48,32,128]{2,1,0:T(8,128)(2,1)} %copy-done.5, bf16[48,32,128]{2,1,0:T(8,128)(2,1)} %copy-done.10, bf16[48,32,128]{2,1,0:T(8,128)(2,1)} %copy-done.9, bf16[48,32,128]{2,1,0:T(8,128)(2,1)} %copy-done.8), custom_call_target="tpu_custom_call" | custom-call | bytes 3145728 | tf_op jit(solution)/shard_map/serve_tiles/pallas_call | solution.py:103
  38.4 6.1 %all-to-all-start.1 = ((bf16[192,32,128]{2,1,0:T(8,128)(2,1)}), bf16[192,32,128]{2,1,0:T(8,128)(2,1)}, u32[]{:S(2)}, u32[]{:S(2)}) async-start(bf16[192,32,128]{2,1,0:T(8,128)(2,1)} %serve_tiles.2), calls=%async_computation.1 | async-start | bytes 3145728 | tf_op jit(solution)/shard_map/all_to_all | solution.py:295
  44.5 15.6 %collective-permute-done.4.up_ref.refs_2_ = bf16[48,96,128]{2,1,0:T(8,128)(2,1)S(1)} collective-permute-done((bf16[48,96,128]{2,1,0:T(8,128)(2,1)}, bf16[48,96,128]{2,1,0:T(8,128)(2,1)S(1)}, u32[]{:S(2)}, u32[]{:S(2)}) %collective-permute-start.4) | collective-permute-done | bytes 1179680 | tf_op jit(solution)/shard_map/ppermute | solution.py:159
  60.1 1.0 copy-done.6
  61.1 1.0 copy-done.7
  62.1 1.3 cut_halves.1
  63.5 2.7 %collective-permute-start.6 = (bf16[24,96,128]{2,1,0:T(8,128)(2,1)S(1)}, bf16[24,96,128]{2,1,0:T(8,128)(2,1)S(1)}, u32[]{:S(2)}, u32[]{:S(2)}) collective-permute-start(bf16[24,96,128]{2,1,0:T(8,128)(2,1)S(1)} %get-tuple-element.12), channel_id=1, source_target_pairs={{0,192},{64,0},{128,64},{192,128},{1,193},{65,1},{129,65},{193,129... | collective-permute-start | bytes 1769480 | tf_op jit(solution)/shard_map/ppermute | solution.py:163
  66.2 12.0 %collective-permute-done.5.refs_3_ = bf16[24,96,128]{2,1,0:T(8,128)(2,1)S(1)} collective-permute-done((bf16[24,96,128]{2,1,0:T(8,128)(2,1)S(1)}, bf16[24,96,128]{2,1,0:T(8,128)(2,1)S(1)}, u32[]{:S(2)}, u32[]{:S(2)}) %collective-permute-start.5) | collective-permute-done | bytes 589856 | tf_op jit(solution)/shard_map/ppermute | solution.py:162
  78.2 5.7 %serve_tiles.3 = bf16[192,96,128]{2,1,0:T(8,128)(2,1)} custom-call(s32[1]{0:T(128)} %bitcast.8.here_ref, s32[64,1,3]{2,1,0:T(1,128)S(1)} %copy-done.1, bf16[48,96,128]{2,1,0:T(8,128)(2,1)} %gate_rows.1.refs_0_, bf16[48,96,128]{2,1,0:T(8,128)(2,1)} %copy-done.7, bf16[48,96,128]{2,1,0:T(8,128)(2,1)} %copy-done.6, ...), custom_call_target="tpu_custom_call" | custom-call | bytes 9437184 | tf_op jit(solution)/shard_map/serve_tiles/pallas_call | solution.py:103
  83.9 0.4 all-to-all-done.1.first_ref
  84.3 6.9 %all-to-all-start.2 = ((bf16[192,96,128]{2,1,0:T(8,128)(2,1)}), bf16[192,96,128]{2,1,0:T(8,128)(2,1)}, u32[]{:S(2)}, u32[]{:S(2)}) async-start(bf16[192,96,128]{2,1,0:T(8,128)(2,1)} %serve_tiles.3), calls=%async_computation.2 | async-start | bytes 9437184 | tf_op jit(solution)/shard_map/all_to_all | solution.py:297
  91.5 5.3 %mix_amplitudes.1.mixed_ref = bf16[3,768,768]{2,1,0:T(8,128)(2,1)} custom-call(bf16[3,768,768]{2,1,0:T(8,128)(2,1)} %amp_ref.1, bf16[8,128]{1,0:T(8,128)(2,1)} %fusion.1.after_ref.sample_ref), custom_call_target="tpu_custom_call" | custom-call | flops 1769472 | bytes 7077888 | tf_op jit(solution)/shard_map/mix_amplitudes/pallas_call | solution.py:178
  96.9 101.6 %all-to-all-done.2.second_ref = bf16[192,96,128]{2,1,0:T(8,128)(2,1)} async-done(((bf16[192,96,128]{2,1,0:T(8,128)(2,1)}), bf16[192,96,128]{2,1,0:T(8,128)(2,1)}, u32[]{:S(2)}, u32[]{:S(2)}) %all-to-all-start.2) | async-done | bytes 4718624 | tf_op jit(solution)/shard_map/all_to_all | solution.py:297
  198.5 10.7 %residual.1 = f32[3,768,768]{2,1,0:T(8,128)} custom-call(s32[108]{0:T(128)S(1)} %bitcast.13, s32[6]{0:T(128)S(1)} %reshape.44.occ_ref, s32[18]{0:T(128)S(1)} %reshape.45.domain_ref, f32[400]{0:T(512)S(1)} %copy-done.3, f32[25,128]{1,0:T(8,128)S(1)} %bitcast.12, bf16[3,768,768]{2,1,0:T(8,128)(2,1)} %mix_amplitudes.1.mixed_ref, ...), custom_call_target="tpu_custom_call" | custom-call | flops 5435817984 | bytes 14155776 | tf_op jit(solution)/shard_map/residual/pallas_call | solution.py:252
  (36 shorter events, 0.9 us)
Async XLA Ops:
  1.0 30.7 %copy-start.5 = (bf16[48,32,128]{2,1,0:T(8,128)(2,1)}, bf16[48,32,128]{2,1,0:T(8,128)(2,1)S(1)}, u32[]{:S(2)}) copy-start(bf16[48,32,128]{2,1,0:T(8,128)(2,1)S(1)} %slice.22.refs_0_) | copy-start | bytes 1179652
  1.0 29.7 %collective-permute-start.2 = (bf16[48,32,128]{2,1,0:T(8,128)(2,1)S(1)}, bf16[48,32,128]{2,1,0:T(8,128)(2,1)S(1)}, u32[]{:S(2)}, u32[]{:S(2)}) collective-permute-start(bf16[48,32,128]{2,1,0:T(8,128)(2,1)S(1)} %slice.22.refs_0_), channel_id=1, source_target_pairs={{192,0},{0,64},{64,128},{128,192},{193,1},{1,65},{65,129},{129,193... | collective-permute-start | bytes 1179656 | tf_op jit(solution)/shard_map/ppermute | solution.py:150
  3.2 27.6 %collective-permute-start.1 = (bf16[48,32,128]{2,1,0:T(8,128)(2,1)S(1)}, bf16[48,32,128]{2,1,0:T(8,128)(2,1)S(1)}, u32[]{:S(2)}, u32[]{:S(2)}) collective-permute-start(bf16[48,32,128]{2,1,0:T(8,128)(2,1)S(1)} %slice.22.refs_0_), channel_id=1, source_target_pairs={{128,0},{192,64},{0,128},{64,192},{129,1},{193,65},{1,129},{65,193... | collective-permute-start | bytes 1179656 | tf_op jit(solution)/shard_map/ppermute | solution.py:150
  5.6 25.2 %collective-permute-start = (bf16[48,32,128]{2,1,0:T(8,128)(2,1)S(1)}, bf16[48,32,128]{2,1,0:T(8,128)(2,1)S(1)}, u32[]{:S(2)}, u32[]{:S(2)}) collective-permute-start(bf16[48,32,128]{2,1,0:T(8,128)(2,1)S(1)} %slice.22.refs_0_), channel_id=1, source_target_pairs={{64,0},{128,64},{192,128},{0,192},{65,1},{129,65},{193,129},{1,193... | collective-permute-start | bytes 1179656 | tf_op jit(solution)/shard_map/ppermute | solution.py:150
  8.3 22.5 %all-to-all-start = ((s32[64,1,3]{2,1,0:T(1,128)}), s32[64,1,3]{2,1,0:T(1,128)S(1)}, u32[]{:S(2)}, u32[]{:S(2)}) async-start(s32[64,1,3]{2,1,0:T(1,128)} %bitcast.14), calls=%async_computation | async-start | bytes 65536 | tf_op jit(solution)/shard_map/all_to_all | solution.py:288
  30.8 3.6 %copy-start = (s32[64,1,3]{2,1,0:T(1,128)}, s32[64,1,3]{2,1,0:T(1,128)S(1)}, u32[]{:S(2)}) copy-start(s32[64,1,3]{2,1,0:T(1,128)S(1)} %all-to-all-done.code_ref) | copy-start | bytes 2308
  30.8 3.6 %copy-start.8 = (bf16[48,32,128]{2,1,0:T(8,128)(2,1)}, bf16[48,32,128]{2,1,0:T(8,128)(2,1)S(1)}, u32[]{:S(2)}) copy-start(bf16[48,32,128]{2,1,0:T(8,128)(2,1)S(1)} %collective-permute-done.2.refs_3_) | copy-start | bytes 1179652
  30.8 0.8 copy-start.9
  30.8 0.9 copy-start.10
  31.7 28.4 %collective-permute-start.4 = (bf16[48,96,128]{2,1,0:T(8,128)(2,1)}, bf16[48,96,128]{2,1,0:T(8,128)(2,1)S(1)}, u32[]{:S(2)}, u32[]{:S(2)}) collective-permute-start(bf16[48,96,128]{2,1,0:T(8,128)(2,1)} %gate_rows.1.refs_0_), channel_id=1, source_target_pairs={{0,64},{64,128},{128,192},{192,0},{1,65},{65,129},{129,193},{193,1... | collective-permute-start | bytes 3538952 | tf_op jit(solution)/shard_map/ppermute | solution.py:159
  32.0 28.1 %collective-permute-start.3 = (bf16[48,96,128]{2,1,0:T(8,128)(2,1)}, bf16[48,96,128]{2,1,0:T(8,128)(2,1)S(1)}, u32[]{:S(2)}, u32[]{:S(2)}) collective-permute-start(bf16[48,96,128]{2,1,0:T(8,128)(2,1)} %gate_rows.1.refs_0_), channel_id=1, source_target_pairs={{0,192},{64,0},{128,64},{192,128},{1,193},{65,1},{129,65},{193,129... | collective-permute-start | bytes 3538952 | tf_op jit(solution)/shard_map/ppermute | solution.py:160
  38.4 45.9 %all-to-all-start.1 = ((bf16[192,32,128]{2,1,0:T(8,128)(2,1)}), bf16[192,32,128]{2,1,0:T(8,128)(2,1)}, u32[]{:S(2)}, u32[]{:S(2)}) async-start(bf16[192,32,128]{2,1,0:T(8,128)(2,1)} %serve_tiles.2), calls=%async_computation.1 | async-start | bytes 3145728 | tf_op jit(solution)/shard_map/all_to_all | solution.py:295
  60.1 1.0 copy-start.6
  61.1 1.0 copy-start.7
  62.1 16.1 %copy-start.1 = (s32[64,1,3]{2,1,0:T(1,128)S(1)}, s32[64,1,3]{2,1,0:T(1,128)}, u32[]{:S(2)}) copy-start(s32[64,1,3]{2,1,0:T(1,128)} %copy-done) | copy-start | bytes 2308
  63.4 14.8 %collective-permute-start.5 = (bf16[24,96,128]{2,1,0:T(8,128)(2,1)S(1)}, bf16[24,96,128]{2,1,0:T(8,128)(2,1)S(1)}, u32[]{:S(2)}, u32[]{:S(2)}) collective-permute-start(bf16[24,96,128]{2,1,0:T(8,128)(2,1)S(1)} %get-tuple-element.11), channel_id=1, source_target_pairs={{0,64},{64,128},{128,192},{192,0},{1,65},{65,129},{129,193},{193,1... | collective-permute-start | bytes 1769480 | tf_op jit(solution)/shard_map/ppermute | solution.py:162
  63.5 14.7 %collective-permute-start.6 = (bf16[24,96,128]{2,1,0:T(8,128)(2,1)S(1)}, bf16[24,96,128]{2,1,0:T(8,128)(2,1)S(1)}, u32[]{:S(2)}, u32[]{:S(2)}) collective-permute-start(bf16[24,96,128]{2,1,0:T(8,128)(2,1)S(1)} %get-tuple-element.12), channel_id=1, source_target_pairs={{0,192},{64,0},{128,64},{192,128},{1,193},{65,1},{129,65},{193,129... | collective-permute-start | bytes 1769480 | tf_op jit(solution)/shard_map/ppermute | solution.py:163
  83.9 7.3 %copy-start.11 = (s32[3,6]{1,0:T(4,128)S(1)}, s32[3,6]{1,0:T(4,128)}, u32[]{:S(2)}) copy-start(s32[3,6]{1,0:T(4,128)} %param.13) | copy-start | bytes 220
  83.9 7.4 %copy-start.12 = (s32[3,2]{0,1:T(2,128)S(1)}, s32[3,2]{0,1:T(2,128)}, u32[]{:S(2)}) copy-start(s32[3,2]{0,1:T(2,128)} %param.12) | copy-start | bytes 76
  84.3 114.2 %all-to-all-start.2 = ((bf16[192,96,128]{2,1,0:T(8,128)(2,1)}), bf16[192,96,128]{2,1,0:T(8,128)(2,1)}, u32[]{:S(2)}, u32[]{:S(2)}) async-start(bf16[192,96,128]{2,1,0:T(8,128)(2,1)} %serve_tiles.3), calls=%async_computation.2 | async-start | bytes 9437184 | tf_op jit(solution)/shard_map/all_to_all | solution.py:297
  91.5 107.0 %copy-start.2 = (f32[3200]{0:T(1024)S(1)}, f32[3200]{0:T(1024)}, u32[]{:S(2)}) copy-start(f32[3200]{0:T(1024)} %param.15) | copy-start | bytes 38404
  91.5 107.0 %copy-start.3 = (f32[400]{0:T(512)S(1)}, f32[400]{0:T(512)}, u32[]{:S(2)}) copy-start(f32[400]{0:T(512)} %eps_occ_ref.1) | copy-start | bytes 4804
  91.5 107.0 %copy-start.4 = (s32[1,108]{1,0:T(1,128)S(1)}, s32[1,108]{1,0:T(1,128)}, u32[]{:S(2)}) copy-start(s32[1,108]{1,0:T(1,128)} %get-tuple-element.9) | copy-start | bytes 1300
